TPU v7x, 128 devices: a whole 4x4x4 slice. The times are simulated.
128 devices in a mesh: gx: 16 (over y, x), gy: 8 (over z, core).
Axes of the slice: x: 4, y: 4, z: 4, core: 2. Of those that a mesh axis runs over, the one named last changes fastest.
Arguments:
- tracer: float32 [12, 960, 5760], P(None, 'gy', 'gx'), may hold values from -6 to 6
- east_velocity: float32 [12, 960, 5760], P(None, 'gy', 'gx'), may hold values from -3 to 3
- north_velocity: float32 [12, 960, 5760], P(None, 'gy', 'gx'), may hold values from -3 to 3
- kmt: int32 [960, 5760], P('gy', 'gx'), may hold values from 0 to 12, as said below
- block_mask: int32 [16, 64], P('gy', 'gx'), may hold values 0 or 1
- surface_forcing: float32 [960, 5760], P('gy', 'gx'), may hold values from -6 to 6
Outputs:
- updated: float32 [12, 960, 5760], P(None, 'gy', 'gx')
- sea_level: float32 [960, 5760], P('gy', 'gx')
- residual: float32 [960, 5760], P('gy', 'gx')
Inputs may be any that keep to these rules, and one draw needn't show every extreme that they name: `kmt`: zero on the grid's first and last rows.
All inputs are finite; a program needn't handle non-finite values. No bound on the sum of `block_mask` on one device may be relied on, other than what follows from the above.
Results may differ from a plain program's by a relative error of at most 0.0003.
Values sent between devices are 32-bit elements; how exact they have to be, the bound alone decides.
No kernel may reach another device: no remote copies, remote signals or barrier semaphores. Data moves between devices by JAX's collectives and lax.ppermute only.
A program may use at most 128 MiB of HBM per device.

v0:
```python
import math

import jax
import jax.numpy as jnp
from jax import lax
from jax.sharding import PartitionSpec as P

BSX = 90
BSY = 60
ITERS = 8


DT_STEP = 0.2
KAPPA_H = 0.2
KAPPA_V = 0.3
SHIFT = 0.002


def extended(array, sides, width):
    for axis, dim in sides:
        count, length = (lax.axis_size(axis), array.shape[dim])
        up = [(i, (i + 1) % count) for i in range(count)]
        down = [(j, i) for i, j in up]
        last = lax.slice_in_dim(array, length - width, length, axis=dim)
        initial = lax.slice_in_dim(array, 0, width, axis=dim)
        before = lax.ppermute(last, axis, up)
        after = lax.ppermute(initial, axis, down)
        array = jnp.concatenate([before, array, after], axis=dim)
    return array


def tracer_update(tracer_pad, east_pad, north_pad, ocean_pad):
    middle_rows = tracer_pad[:, 1:-1, :]
    east_rows = east_pad[:, 1:-1, :]
    ocean_rows = ocean_pad[:, 1:-1, :]
    open_east = ocean_rows[:, :, :-1] * ocean_rows[:, :, 1:]
    flux_east = (
        KAPPA_H * (middle_rows[:, :, 1:] - middle_rows[:, :, :-1])
        - east_rows[:, :, :-1] * 0.5 * (middle_rows[:, :, :-1] + middle_rows[:, :, 1:])
    ) * open_east
    middle_cols = tracer_pad[:, :, 1:-1]
    north_cols = north_pad[:, :, 1:-1]
    ocean_cols = ocean_pad[:, :, 1:-1]
    open_north = ocean_cols[:, :-1, :] * ocean_cols[:, 1:, :]
    flux_north = (
        KAPPA_H * (middle_cols[:, 1:, :] - middle_cols[:, :-1, :])
        - north_cols[:, :-1, :] * 0.5 * (middle_cols[:, :-1, :] + middle_cols[:, 1:, :])
    ) * open_north
    horizontal = (
        flux_east[:, :, 1:] - flux_east[:, :, :-1] + flux_north[:, 1:, :] - flux_north[:, :-1, :]
    )
    center = tracer_pad[:, 1:-1, 1:-1]
    ocean = ocean_pad[:, 1:-1, 1:-1]
    flux_down = KAPPA_V * (center[1:] - center[:-1]) * (ocean[:-1] * ocean[1:])
    vertical = jnp.pad(flux_down, ((0, 1), (0, 0), (0, 0))) - jnp.pad(
        flux_down, ((1, 0), (0, 0), (0, 0))
    )
    return center + DT_STEP * ocean * (horizontal + vertical)


def face_weights(depth_pad, wet_pad):
    wet_rows = wet_pad[1:-1, :]
    depth_rows = depth_pad[1:-1, :]
    east_face = wet_rows[:, :-1] * wet_rows[:, 1:] * 0.5 * (depth_rows[:, :-1] + depth_rows[:, 1:])
    wet_cols = wet_pad[:, 1:-1]
    depth_cols = depth_pad[:, 1:-1]
    north_face = wet_cols[:-1, :] * wet_cols[1:, :] * 0.5 * (depth_cols[:-1, :] + depth_cols[1:, :])
    depth = depth_pad[1:-1, 1:-1]
    wet = wet_pad[1:-1, 1:-1]
    diagonal = (
        SHIFT * depth
        + east_face[:, 1:]
        + east_face[:, :-1]
        + north_face[1:, :]
        + north_face[:-1, :]
    )
    diagonal = jnp.where(wet > 0.5, diagonal, jnp.float32(1.0))
    return (east_face, north_face, diagonal)


def apply_operator(field_pad, east_face, north_face, diagonal):
    center = field_pad[1:-1, 1:-1]
    beside = east_face[:, 1:] * field_pad[1:-1, 2:] + east_face[:, :-1] * field_pad[1:-1, :-2]
    beside = (
        beside + north_face[1:, :] * field_pad[2:, 1:-1] + north_face[:-1, :] * field_pad[:-2, 1:-1]
    )
    return diagonal * center - beside


def pad_blocks(field):
    return extended(field, (("gx", 1), ("gy", 0)), 1)


def weighted_sum(value):
    return lax.psum(jnp.sum(value), ("gx", "gy"))


def solve(rhs_work, coefficients, padder):
    east_face, north_face, diagonal = coefficients
    sea_level = jnp.zeros_like(rhs_work)
    residual = rhs_work
    precond = residual / diagonal
    direction = precond
    norm_now = weighted_sum(residual * precond)
    for step in range(ITERS):
        image = apply_operator(padder(direction), east_face, north_face, diagonal)
        alpha = norm_now / lax.psum(jnp.sum(direction * image), ("gx", "gy"))
        sea_level = sea_level + alpha * direction
        residual = residual - alpha * image
        precond = residual / diagonal
        norm_next = weighted_sum(residual * precond)
        direction = precond + norm_next / norm_now * direction
        norm_now = norm_next
    return (sea_level, residual)


def shards(tracer, east_velocity, north_velocity, kmt, block_mask, surface_forcing):
    layers = tracer.shape[0]
    keep = jnp.repeat(jnp.repeat(block_mask, BSY, axis=0), BSX, axis=1)
    levels = kmt * keep
    levels_pad = extended(levels, (("gx", 1), ("gy", 0)), 1)
    ocean_pad = (jnp.arange(layers, dtype=jnp.int32)[:, None, None] < levels_pad[None]).astype(
        jnp.float32
    )
    stacked = jnp.stack([tracer, east_velocity, north_velocity])
    stacked_pad = extended(stacked, (("gx", 3), ("gy", 2)), 1)
    updated = tracer_update(stacked_pad[0], stacked_pad[1], stacked_pad[2], ocean_pad)
    thick = 1.0 + 0.5 * jnp.arange(layers).astype(jnp.float32) / layers
    depth_pad = jnp.sum(thick[:, None, None] * ocean_pad, axis=0)
    wet_pad = (levels_pad > 0).astype(jnp.float32)
    column = jnp.sum(thick[:, None, None] * ocean_pad[:, 1:-1, 1:-1] * updated, axis=0) / math.sqrt(
        layers
    )
    rhs = wet_pad[1:-1, 1:-1] * (column + surface_forcing)
    sea_level, residual = solve(rhs, face_weights(depth_pad, wet_pad), pad_blocks)
    return (updated, sea_level, residual)


def solution(mesh):
    in_specs = (
        P(None, "gy", "gx"),
        P(None, "gy", "gx"),
        P(None, "gy", "gx"),
        P("gy", "gx"),
        P("gy", "gx"),
        P("gy", "gx"),
    )
    out_specs = (P(None, "gy", "gx"), P("gy", "gx"), P("gy", "gx"))
    return jax.shard_map(shards, mesh=mesh, in_specs=in_specs, out_specs=out_specs, check_vma=False)
```

profile of v0, /device:TPU:1, one launch (start us, length us, event | category | flops | bytes accessed | tf_op | source)
XLA Modules:
  0.0 1184.1 jit_solution(10715774016316058657)
XLA Ops:
  10.7 3.8 copy.25
  18.5 4.8 collective-permute-start.1
  32.0 5.3 pad_maximum_fusion
  37.3 11.6 fusion.90
  48.9 4.7 copy.27
  53.6 5.3 copy.28
  59.7 4.9 copy.29
  64.7 5.0 copy.30
  69.7 10.2 pad_maximum_fusion.1
  93.9 4.0 collective-permute-done.9
  103.4 64.1 %all-reduce.2 = (f32[]{:T(128)}, f32[]{:T(128)}) all-reduce(f32[]{:T(128)} %get-tuple-element.13, f32[]{:T(128)} %get-tuple-element.12), channel_id=1, replica_groups=mesh['gx'=16,'gy'=8] {'gx','gy'}, use_global_device_ids=true, to_apply=%region_3.4 | all-reduce | flops 2 | bytes 16 | tf_op jit(solution)/shard_map/psum | solution.py:95
  169.4 63.5 %psum.114 = f32[]{:T(128)} all-reduce(f32[]{:T(128)} %get-tuple-element.48), channel_id=1, replica_groups=mesh['gx'=16,'gy'=8] {'gx','gy'}, use_global_device_ids=true, to_apply=%region_7.8 | all-reduce | flops 1 | bytes 8 | tf_op jit(solution)/shard_map/psum | solution.py:95
  238.3 5.1 collective-permute-done.13
  247.6 64.5 %psum.115 = f32[]{:T(128)} all-reduce(f32[]{:T(128)} %get-tuple-element.46), channel_id=1, replica_groups=mesh['gx'=16,'gy'=8] {'gx','gy'}, use_global_device_ids=true, to_apply=%region_9.10 | all-reduce | flops 1 | bytes 8 | tf_op jit(solution)/shard_map/psum | solution.py:107
  314.1 62.5 %psum.116 = f32[]{:T(128)} all-reduce(f32[]{:T(128)} %get-tuple-element.43), channel_id=1, replica_groups=mesh['gx'=16,'gy'=8] {'gx','gy'}, use_global_device_ids=true, to_apply=%region_11.12 | all-reduce | flops 1 | bytes 8 | tf_op jit(solution)/shard_map/psum | solution.py:95
  381.7 5.1 collective-permute-done.17
  392.2 63.3 %psum.117 = f32[]{:T(128)} all-reduce(f32[]{:T(128)} %get-tuple-element.41), channel_id=1, replica_groups=mesh['gx'=16,'gy'=8] {'gx','gy'}, use_global_device_ids=true, to_apply=%region_13.14 | all-reduce | flops 1 | bytes 8 | tf_op jit(solution)/shard_map/psum | solution.py:107
  457.5 62.5 %psum.118 = f32[]{:T(128)} all-reduce(f32[]{:T(128)} %get-tuple-element.38), channel_id=1, replica_groups=mesh['gx'=16,'gy'=8] {'gx','gy'}, use_global_device_ids=true, to_apply=%region_15.16 | all-reduce | flops 1 | bytes 8 | tf_op jit(solution)/shard_map/psum | solution.py:95
  525.1 5.1 collective-permute-done.21
  535.6 63.3 %psum.119 = f32[]{:T(128)} all-reduce(f32[]{:T(128)} %get-tuple-element.36), channel_id=1, replica_groups=mesh['gx'=16,'gy'=8] {'gx','gy'}, use_global_device_ids=true, to_apply=%region_17.18 | all-reduce | flops 1 | bytes 8 | tf_op jit(solution)/shard_map/psum | solution.py:107
  600.9 62.5 %psum.120 = f32[]{:T(128)} all-reduce(f32[]{:T(128)} %get-tuple-element.33), channel_id=1, replica_groups=mesh['gx'=16,'gy'=8] {'gx','gy'}, use_global_device_ids=true, to_apply=%region_19.20 | all-reduce | flops 1 | bytes 8 | tf_op jit(solution)/shard_map/psum | solution.py:95
  668.5 5.1 collective-permute-done.25
  679.0 63.5 %psum.121 = f32[]{:T(128)} all-reduce(f32[]{:T(128)} %get-tuple-element.31), channel_id=1, replica_groups=mesh['gx'=16,'gy'=8] {'gx','gy'}, use_global_device_ids=true, to_apply=%region_21.22 | all-reduce | flops 1 | bytes 8 | tf_op jit(solution)/shard_map/psum | solution.py:107
  744.6 62.5 %psum.122 = f32[]{:T(128)} all-reduce(f32[]{:T(128)} %get-tuple-element.28), channel_id=1, replica_groups=mesh['gx'=16,'gy'=8] {'gx','gy'}, use_global_device_ids=true, to_apply=%region_23.24 | all-reduce | flops 1 | bytes 8 | tf_op jit(solution)/shard_map/psum | solution.py:95
  812.1 5.1 collective-permute-done.29
  822.6 63.3 %psum.123 = f32[]{:T(128)} all-reduce(f32[]{:T(128)} %get-tuple-element.26), channel_id=1, replica_groups=mesh['gx'=16,'gy'=8] {'gx','gy'}, use_global_device_ids=true, to_apply=%region_25.26 | all-reduce | flops 1 | bytes 8 | tf_op jit(solution)/shard_map/psum | solution.py:107
  888.7 62.5 %psum.124 = f32[]{:T(128)} all-reduce(f32[]{:T(128)} %get-tuple-element.23), channel_id=1, replica_groups=mesh['gx'=16,'gy'=8] {'gx','gy'}, use_global_device_ids=true, to_apply=%region_27.28 | all-reduce | flops 1 | bytes 8 | tf_op jit(solution)/shard_map/psum | solution.py:95
  957.3 5.1 collective-permute-done.33
  968.5 63.3 %psum.125 = f32[]{:T(128)} all-reduce(f32[]{:T(128)} %get-tuple-element.21), channel_id=1, replica_groups=mesh['gx'=16,'gy'=8] {'gx','gy'}, use_global_device_ids=true, to_apply=%region_29.30 | all-reduce | flops 1 | bytes 8 | tf_op jit(solution)/shard_map/psum | solution.py:107
  1035.6 62.5 %psum.126 = f32[]{:T(128)} all-reduce(f32[]{:T(128)} %get-tuple-element.18), channel_id=1, replica_groups=mesh['gx'=16,'gy'=8] {'gx','gy'}, use_global_device_ids=true, to_apply=%region_31.32 | all-reduce | flops 1 | bytes 8 | tf_op jit(solution)/shard_map/psum | solution.py:95
  1104.1 5.1 collective-permute-done.37
  1117.4 63.1 %psum.127 = f32[]{:T(128)} all-reduce(f32[]{:T(128)} %get-tuple-element.16), channel_id=1, replica_groups=mesh['gx'=16,'gy'=8] {'gx','gy'}, use_global_device_ids=true, to_apply=%region_33.34 | all-reduce | flops 1 | bytes 8 | tf_op jit(solution)/shard_map/psum | solution.py:107
  (165 shorter events, 121.0 us)
Async XLA Ops:
  2.8 20.5 %collective-permute-start.4 = (s32[120,1]{1,0:T(8,128)S(1)}, s32[120,1]{1,0:T(8,128)S(1)}, u32[]{:S(2)}, u32[]{:S(2)}) collective-permute-start(s32[120,1]{1,0:T(8,128)S(1)} %get-tuple-element.104), channel_id=1, source_target_pairs={{0,8},{8,16},{16,24},{24,32},{32,40},{40,48},{48,56},{56,64},{64,7... | collective-permute-start | bytes 1448 | tf_op jit(solution)/shard_map/ppermute | solution.py:26
  4.8 18.4 %collective-permute-start.5 = (s32[120,1]{1,0:T(8,128)S(1)}, s32[120,1]{1,0:T(8,128)S(1)}, u32[]{:S(2)}, u32[]{:S(2)}) collective-permute-start(s32[120,1]{1,0:T(8,128)S(1)} %get-tuple-element.105), channel_id=1, source_target_pairs={{8,0},{16,8},{24,16},{32,24},{40,32},{48,40},{56,48},{64,56},{72,6... | collective-permute-start | bytes 1448 | tf_op jit(solution)/shard_map/ppermute | solution.py:27
  18.4 13.5 %collective-permute-start = (f32[3,12,120,1]{2,3,1,0:T(1,128)S(1)}, f32[3,12,120,1]{2,3,1,0:T(1,128)S(1)}, u32[]{:S(2)}, u32[]{:S(2)}) collective-permute-start(f32[3,12,120,1]{2,3,1,0:T(1,128)S(1)} %get-tuple-element.64), channel_id=1, source_target_pairs={{0,8},{8,16},{16,24},{24,32},{32,40},{40,48},{48,56},{56,64},{64,7... | collective-permute-start | bytes 51848 | tf_op jit(solution)/shard_map/ppermute | solution.py:26
  18.5 13.5 %collective-permute-start.1 = (f32[3,12,120,1]{2,3,1,0:T(1,128)S(1)}, f32[3,12,120,1]{2,3,1,0:T(1,128)S(1)}, u32[]{:S(2)}, u32[]{:S(2)}) collective-permute-start(f32[3,12,120,1]{2,3,1,0:T(1,128)S(1)} %get-tuple-element.65), channel_id=1, source_target_pairs={{8,0},{16,8},{24,16},{32,24},{40,32},{48,40},{56,48},{64,56},{72,6... | collective-permute-start | bytes 51848 | tf_op jit(solution)/shard_map/ppermute | solution.py:27
  23.3 3.8 collective-permute-start.6
  26.4 3.0 collective-permute-start.7
  53.5 6.2 collective-permute-start.2
  58.9 5.8 collective-permute-start.3
  90.8 3.1 collective-permute-start.8
  91.5 6.4 collective-permute-start.9
  98.0 4.4 collective-permute-start.10
  234.4 3.8 collective-permute-start.12
  237.0 6.4 collective-permute-start.13
  243.4 3.0 collective-permute-start.14
  378.1 3.6 collective-permute-start.16
  380.4 6.4 collective-permute-start.17
  386.8 4.4 collective-permute-start.18
  521.5 3.6 collective-permute-start.20
  523.8 6.4 collective-permute-start.21
  530.3 4.4 collective-permute-start.22
  664.9 3.6 collective-permute-start.24
  667.2 6.4 collective-permute-start.25
  673.7 4.4 collective-permute-start.26
  808.5 3.6 collective-permute-start.28
  810.8 6.4 collective-permute-start.29
  817.3 4.4 collective-permute-start.30
  953.7 3.6 collective-permute-start.32
  956.0 6.4 collective-permute-start.33
  962.5 4.4 collective-permute-start.34
  1100.5 3.6 collective-permute-start.36
  1102.8 6.4 collective-permute-start.37
  1109.8 5.1 collective-permute-start.38
  (18 other events, 391.6 us)
where the time goes:
time: 1190 us; the launch traced here: 1180 us
  blocking collectives  947 us (80%)
  waiting for transfers between devices  62 us (5%)
  starting transfers between devices  56.7 us (5%)
  other arithmetic  50.5 us (4%)
  local copies, waits for them, and re-layouts  47.1 us (4%)
  between operations  20.8 us (2%)
    psum x8, blocking collectives, weighted_sum(): return lax.psum(jnp.sum(value), ('gx', 'gy'))  503 us
    psum x7, blocking collectives, solve(): alpha = norm_now / lax.psum(jnp.sum(direction * image), ('gx', 'gy'))  444 us
    ppermute x20, starting transfers between devices, extended(): after = lax.ppermute(initial, axis, down)  43.9 us
    ppermute x20, waiting for transfers between devices, extended(): before = lax.ppermute(last, axis, up)  40.7 us
  transfers between devices with their start and end apart: 40, of which 26 were waited for; matrix products, arithmetic and copies ran while one was open for 2% of the time, Pallas kernels for 0%

commit v1 on v0

v1 whole, which is shorter than its diff:
```python
import math

import jax
import jax.numpy as jnp
from jax import lax
from jax.experimental import pallas as pl
from jax.experimental.pallas import tpu as pltpu
from jax.sharding import PartitionSpec as P

BSX = 90
BSY = 60
KL = 12
ITERS = 8

DT_STEP = 0.2
KAPPA_H = 0.2
KAPPA_V = 0.3
SHIFT = 0.002

H = 120
W = 360
LW = 384
EH = 144

GRAD = DT_STEP * KAPPA_H
ADV = DT_STEP * 0.5
VERT = DT_STEP * KAPPA_V
ROOT = 1.0 / math.sqrt(KL)

LEV0 = 8
TR0 = 17
VE0 = 29
C_T0 = 48
C_T1 = 56
C_V1 = 64

R_LEV = 8
R_TR = 24
R_VE = 40

F32 = jnp.float32
VMEM_LIMIT = 40 * 1024 * 1024


def lanes(shape):
    return lax.broadcasted_iota(jnp.int32, shape, 1)


def rows(shape):
    return lax.broadcasted_iota(jnp.int32, shape, 0)


def widen(x, width):
    return jnp.concatenate([x, jnp.zeros((x.shape[0], width - x.shape[1]), x.dtype)], axis=1)


def roll(x, shift, axis):
    shift = shift % x.shape[axis]
    return x if shift == 0 else pltpu.roll(x, shift, axis)


def thickness(level):
    return 1.0 + (0.5 / KL) * level


def tracer_kernel(
    mask_ref, kmt_ref, forcing_ref, t_hbm, u_hbm, v_hbm,
    upd_hbm, rhs_ref, lev_ref, msg_e, msg_w, row_n, row_s,
    t_s, u_s, v_s, o_s, min_e, min_n, col, sem_in, sem_out,
):
    def load(i, k):
        src, dst = ((t_hbm, t_s), (u_hbm, u_s), (v_hbm, v_s))[i]
        return pltpu.make_async_copy(src.at[k], dst.at[k], sem_in.at[i, k])

    def store(k):
        return pltpu.make_async_copy(o_s.at[k], upd_hbm.at[k], sem_out.at[k])

    for k in range(KL):
        for i in range(3):
            load(i, k).start()

    lane = lanes((8, LW))
    row = rows((8, LW))
    for r in range(0, H, 8):
        keep = jnp.zeros((8, LW), jnp.int32)
        for b in range(W // BSX):
            inside = (lane >= b * BSX) & (lane < (b + 1) * BSX)
            upper = jnp.where(row + r < BSY, mask_ref[0, b], mask_ref[1, b])
            keep = jnp.where(inside, upper, keep)
        lev = widen(kmt_ref[r : r + 8, :], LW) * keep
        lev_ref[r : r + 8, :] = lev.astype(F32)
    for r in range(0, H, 8):
        lev = lev_ref[r : r + 8, :]
        if r + 8 < H:
            north = lev_ref[r + 1 : r + 9, :]
        else:
            north = jnp.where(row == 7, 0.0, roll(lev, -1, 0))
        min_e[r : r + 8, :] = jnp.minimum(lev, roll(lev, -1, 1))
        min_n[r : r + 8, :] = jnp.minimum(lev, north)
        col[r : r + 8, :] = jnp.zeros((8, LW), F32)
    row_n[...] = jnp.zeros((32, LW), F32)
    row_s[...] = jnp.zeros((16, LW), F32)

    load(0, 0).wait()
    row360 = rows((8, W))

    def level(k, carry):
        above = jnp.minimum(k + 1, KL - 1)
        below = jnp.maximum(k - 1, 0)

        @pl.when(k < KL - 1)
        def _():
            load(0, above).wait()

        load(1, k).wait()
        load(2, k).wait()
        kf = k.astype(F32)
        thick = thickness(kf)
        before = jnp.zeros((8, W), F32)
        for r in range(0, H, 8):
            here = slice(r, r + 8)
            t = t_s[k, here, :]
            t_e = roll(widen(t, LW), -1, 1)[:, :W]
            if r + 8 < H:
                t_n = t_s[k, r + 1 : r + 9, :]
            else:
                t_n = roll(t, -1, 0)
            u = u_s[k, here, :]
            v = v_s[k, here, :]
            lev = lev_ref[here, :W]
            f_e = jnp.where(min_e[here, :W] > kf, GRAD * (t_e - t) - (ADV * u) * (t + t_e), 0.0)
            f_n = jnp.where(min_n[here, :W] > kf, GRAD * (t_n - t) - (ADV * v) * (t + t_n), 0.0)
            f_w = roll(widen(f_e, LW), 1, 1)[:, :W]
            shifted = roll(f_n, 1, 0)
            f_s = jnp.where(row360 == 0, before, shifted)
            before = shifted
            wet = lev > kf
            up = jnp.where(lev > kf + 1.0, t_s[above, here, :] - t, 0.0)
            down = jnp.where(wet, t - t_s[below, here, :], 0.0)
            updated = t + ((f_e - f_w) + (f_n - f_s) + VERT * (up - down))
            o_s[k, here, :] = updated
            col[here, :W] += jnp.where(wet, thick * updated, 0.0)
        store(k).start()
        row_s[pl.ds(k, 1), :] = widen(t_s[k, 0:1, :], LW)
        row_n[pl.ds(k, 1), :] = widen(t_s[k, H - 1 : H, :], LW)
        row_n[pl.ds(16 + k, 1), :] = widen(v_s[k, H - 1 : H, :], LW)
        return carry

    lax.fori_loop(0, KL, level, 0)

    lane = lanes((8, 128))
    for r in range(0, H, 8):
        here = slice(r, r + 8)
        lev = lev_ref[here, :]
        rhs = jnp.where(
            lev > 0.0, ROOT * col[here, :] + widen(forcing_ref[here, :], LW), 0.0
        )
        rhs_ref[here, :] = rhs
        east = jnp.where(lane < LEV0, roll(rhs[:, 256:], 32, 1), roll(lev[:, 256:], LEV0 - 95, 1))
        west = jnp.where(lane < LEV0, rhs[:, :128], roll(lev[:, :128], LEV0, 1))
        east = jnp.where(lane < TR0, east, 0.0)
        west = jnp.where(lane < TR0, west, 0.0)
        for k in range(KL):
            t2 = roll(widen(t_s[k, here, 256:W], 128), TR0 + k - 103, 1)
            u2 = roll(widen(u_s[k, here, 256:W], 128), VE0 + k - 103, 1)
            t0 = roll(t_s[k, here, :128], TR0 + k, 1)
            east = jnp.where(lane == TR0 + k, t2, east)
            east = jnp.where(lane == VE0 + k, u2, east)
            west = jnp.where(lane == TR0 + k, t0, west)
        if r < 16:
            for at, src, base in ((C_T0, row_s, 0), (C_T1, row_n, 0), (C_V1, row_n, 16)):
                inside = (lane >= at) & (lane < at + 8)
                piece = src[base + r : base + r + 8, :]
                east = jnp.where(inside, roll(piece[:, 256:], at - 96, 1), east)
                west = jnp.where(inside, roll(piece[:, :128], at, 1), west)
        msg_e[here, :] = east
        msg_w[here, :] = west

    def drain(k, carry):
        store(k).wait()
        return carry

    lax.fori_loop(0, KL, drain, 0)


def tracer_part(mask, kmt, forcing, tracer, east, north):
    vmem = pl.BlockSpec(memory_space=pltpu.VMEM)
    hbm = pl.BlockSpec(memory_space=pl.ANY)
    shape = jax.ShapeDtypeStruct
    return pl.pallas_call(
        tracer_kernel,
        out_shape=[
            shape((KL, H, W), F32),
            shape((H, LW), F32),
            shape((H, LW), F32),
            shape((H, 128), F32),
            shape((H, 128), F32),
            shape((32, LW), F32),
            shape((16, LW), F32),
        ],
        in_specs=[pl.BlockSpec(memory_space=pltpu.SMEM), vmem, vmem, hbm, hbm, hbm],
        out_specs=[hbm] + [vmem] * 6,
        scratch_shapes=[pltpu.VMEM((KL, H, W), F32)] * 4
        + [pltpu.VMEM((H, LW), F32)] * 3
        + [pltpu.SemaphoreType.DMA((3, KL)), pltpu.SemaphoreType.DMA((KL,))],
        compiler_params=pltpu.CompilerParams(vmem_limit_bytes=VMEM_LIMIT),
        name="tracer",
    )(mask, kmt, forcing, tracer, east, north)


def sides_kernel(
    from_w, from_e, own_e, own_w, rhs_ref, lev_ref, row_n, row_s,
    rhs_x, lev_x, msg_n, msg_s, flux_e, flux_w,
):
    lane = lanes((8, 128))
    kf = (lane - TR0).astype(F32)
    inside = (lane >= TR0) & (lane < TR0 + KL)
    weight = ROOT * thickness(kf)
    for r in range(0, H, 8):
        here = slice(r, r + 8)
        mw, me = from_w[here, :], from_e[here, :]
        mine_e, mine_w = own_e[here, :], own_w[here, :]
        lev0 = jnp.minimum(mw[:, LEV0 + 8 : LEV0 + 9], mine_w[:, LEV0 : LEV0 + 1])
        lev1 = jnp.minimum(me[:, LEV0 : LEV0 + 1], mine_e[:, LEV0 + 8 : LEV0 + 9])
        f_w = GRAD * (mine_w - mw) - (ADV * roll(mw, TR0 - VE0, 1)) * (mine_w + mw)
        f_e = GRAD * (me - mine_e) - (ADV * roll(mine_e, TR0 - VE0, 1)) * (me + mine_e)
        f_w = jnp.where(inside & (lev0 > kf), f_w, 0.0)
        f_e = jnp.where(inside & (lev1 > kf), f_e, 0.0)
        flux_w[here, :] = f_w
        flux_e[here, :] = f_e
        c_w = jnp.sum(weight * f_w, axis=1, keepdims=True)
        c_e = jnp.sum(weight * f_e, axis=1, keepdims=True)
        rhs_x[here, :128] = rhs_ref[here, :128] - jnp.where(lane == 0, c_w, 0.0)
        rhs_x[here, 128:256] = rhs_ref[here, 128:256]
        last = rhs_ref[here, 256:]
        last = jnp.where((lane >= 104) & (lane < 112), roll(me, 104, 1), last)
        last = jnp.where(lane >= 120, roll(mw, 120, 1), last)
        last = last + jnp.where(lane == 103, c_e, 0.0) - jnp.where(lane == 104, c_e, 0.0)
        rhs_x[here, 256:] = last + jnp.where(lane == 127, c_w, 0.0)
        lev_x[here, :256] = lev_ref[here, :256]
        last = lev_ref[here, 256:]
        last = jnp.where((lane >= 104) & (lane < 113), roll(me, 104 - LEV0, 1), last)
        last = jnp.where(lane >= 119, roll(mw, 119 - LEV0, 1), last)
        lev_x[here, 256:] = last
    msg_n[0:8, :] = rhs_x[H - 8 : H, :]
    msg_s[0:8, :] = rhs_x[0:8, :]
    msg_n[R_LEV : R_LEV + 16, :] = lev_x[H - 16 : H, :]
    msg_s[R_LEV : R_LEV + 16, :] = lev_x[0:16, :]
    for dst, at, src, base, lane0 in (
        (msg_s, R_TR, row_s, 0, C_T0), (msg_n, R_TR, row_n, 0, C_T1), (msg_n, R_VE, row_n, 16, C_V1),
    ):
        for r in (0, 8):
            mw, me = from_w[r : r + 8, :], from_e[r : r + 8, :]
            piece = src[base + r : base + r + 8, :]
            last = piece[:, 256:]
            last = jnp.where((lane >= 104) & (lane < 112), roll(me, 104 - lane0, 1), last)
            last = jnp.where(lane >= 120, roll(mw, 120 - lane0, 1), last)
            dst[at + r : at + r + 8, :256] = piece[:, :256]
            dst[at + r : at + r + 8, 256:] = last


def sides_part(from_w, from_e, own_e, own_w, rhs, lev, row_n, row_s):
    vmem = pl.BlockSpec(memory_space=pltpu.VMEM)
    shape = jax.ShapeDtypeStruct
    return pl.pallas_call(
        sides_kernel,
        out_shape=[
            shape((H, LW), F32),
            shape((H, LW), F32),
            shape((56, LW), F32),
            shape((40, LW), F32),
            shape((H, 128), F32),
            shape((H, 128), F32),
        ],
        in_specs=[vmem] * 8,
        out_specs=[vmem] * 6,
        compiler_params=pltpu.CompilerParams(vmem_limit_bytes=VMEM_LIMIT),
        name="sides",
    )(from_w, from_e, own_e, own_w, rhs, lev, row_n, row_s)


def basis_kernel(
    from_s, from_n, own_n, own_s, rhs_ref, lev_ref,
    basis, diag, sums, flux_n, flux_s,
    depth, face_e, face_n, w_e, w_w, w_n, w_s, weight, parts,
):
    lev_row = rows((16, LW))
    kf = lev_row.astype(F32)
    factor = ROOT * thickness(kf)

    def face(t_from, t_to, vel, lev):
        flux = GRAD * (t_to - t_from) - (ADV * vel) * (t_from + t_to)
        return jnp.where((lev_row < KL) & (lev > kf), flux, 0.0)

    tr = slice(R_TR, R_TR + 16)
    ve = slice(R_VE, R_VE + 16)
    lev_n = jnp.minimum(lev_ref[H - 1 : H, :], from_n[R_LEV : R_LEV + 1, :])
    lev_s = jnp.minimum(lev_ref[0:1, :], from_s[R_LEV + 15 : R_LEV + 16, :])
    f_n = face(own_n[tr, :], from_n[tr, :], own_n[ve, :], lev_n)
    f_s = face(from_s[tr, :], own_s[tr, :], from_s[ve, :], lev_s)
    flux_n[...] = f_n
    flux_s[...] = f_s
    c_n = jnp.sum(factor * f_n, axis=0, keepdims=True)
    c_s = jnp.sum(factor * f_s, axis=0, keepdims=True)

    row = rows((8, LW))
    lane = lanes((8, LW))

    def level_rows(r):
        if r < H:
            return lev_ref[r : r + 8, :]
        if r == H:
            return from_n[R_LEV : R_LEV + 8, :]
        if r == H + 8:
            first = from_n[R_LEV + 8 : R_LEV + 9, :]
            last = from_s[R_LEV + 7 : R_LEV + 8, :]
            return jnp.where(row == 0, first, jnp.where(row == 7, last, 0.0))
        return from_s[R_LEV + 8 : R_LEV + 16, :]

    def rhs_rows(r):
        if r < H:
            value = rhs_ref[r : r + 8, :]
            if r == 0:
                value = value - jnp.where(row == 0, c_s, 0.0)
            if r == H - 8:
                value = value + jnp.where(row == 7, c_n, 0.0)
            return value
        if r == H:
            return from_n[0:8, :] - jnp.where(row == 0, c_n, 0.0)
        if r == H + 8:
            return jnp.zeros((8, LW), F32)
        return from_s[0:8, :] + jnp.where(row == 7, c_s, 0.0)

    def north(ref, r):
        if r + 8 < EH:
            return ref[r + 1 : r + 9, :]
        return jnp.where(row == 7, roll(ref[0:8, :], -1, 0), roll(ref[r : r + 8, :], -1, 0))

    def south(ref, r):
        if r > 0:
            return ref[r - 1 : r + 7, :]
        return jnp.where(row == 0, roll(ref[EH - 8 : EH, :], 1, 0), roll(ref[0:8, :], 1, 0))

    for r in range(0, EH, 8):
        lev = level_rows(r)
        depth[r : r + 8, :] = lev + lev * (lev - 1.0) * (0.25 / KL)
    for r in range(0, EH, 8):
        here = slice(r, r + 8)
        d = depth[here, :]
        d_e, d_n = roll(d, -1, 1), north(depth, r)
        face_e[here, :] = jnp.where((d > 0.0) & (d_e > 0.0), 0.5 * (d + d_e), 0.0)
        face_n[here, :] = jnp.where((d > 0.0) & (d_n > 0.0), 0.5 * (d + d_n), 0.0)
    lone = jnp.zeros((8, LW), F32)
    for r in range(0, EH, 8):
        here = slice(r, r + 8)
        d = depth[here, :]
        e, n = face_e[here, :], face_n[here, :]
        w = roll(e, 1, 1)
        s = south(face_n, r)
        faces = e + w + n + s
        dg = jnp.where(d > 0.0, SHIFT * d + faces, 1.0)
        inv = 1.0 / dg
        z = rhs_rows(r) * inv
        basis[0, here, :] = z
        w_e[here, :] = e * inv
        w_w[here, :] = w * inv
        w_n[here, :] = n * inv
        w_s[here, :] = s * inv
        if r < H:
            diag[here, :] = dg
            own = jnp.where(lane < W, dg, 0.0)
            joined = faces > 0.0
            weight[here, :] = jnp.where(joined, own, 0.0)
            lone = lone + jnp.where(joined, 0.0, own * z * z)

    def fold(x):
        return jnp.sum(x[:, :128] + x[:, 128:256] + x[:, 256:], axis=0, keepdims=True)

    parts[...] = jnp.zeros((24, 128), F32)
    parts[16:17, :] = fold(lone)

    def step(k, carry):
        first = k == 1
        twice = jnp.where(first, 1.0, 2.0)
        keep = jnp.where(first, 0.0, 1.0)
        older = jnp.maximum(k - 2, 0)
        now = basis.at[k - 1]
        even = jnp.zeros((8, LW), F32)
        odd = jnp.zeros((8, LW), F32)
        for r in range(0, EH, 8):
            here = slice(r, r + 8)
            c = now[here, :]
            image = w_e[here, :] * roll(c, -1, 1) + w_w[here, :] * roll(c, 1, 1)
            image = image + (w_n[here, :] * north(now, r) + w_s[here, :] * south(now, r))
            value = twice * image - keep * basis[older, here, :]
            basis[k, here, :] = value
            if r < H:
                scaled = weight[here, :] * c
                even = even + scaled * c
                odd = odd + scaled * value
        parts[pl.ds(2 * k - 2, 1), :] = fold(even)
        parts[pl.ds(2 * k - 1, 1), :] = fold(odd)
        return carry

    lax.fori_loop(1, ITERS + 1, step, 0)

    total = jnp.sum(parts[...], axis=1, keepdims=True)
    prow = rows((24, 128))
    plane = lanes((24, 128))
    place = (prow < 16) & ((plane == prow) | (plane == 128 - prow)) | (prow == 16) & (plane == 64)
    line = jnp.sum(jnp.where(place, total, 0.0), axis=0, keepdims=True)
    sums[...] = jnp.broadcast_to(line, sums.shape)


def basis_part(from_s, from_n, own_n, own_s, rhs, lev, count):
    vmem = pl.BlockSpec(memory_space=pltpu.VMEM)
    shape = jax.ShapeDtypeStruct
    return pl.pallas_call(
        basis_kernel,
        out_shape=[
            shape((ITERS + 1, EH, LW), F32),
            shape((H, LW), F32),
            shape((count, 128), F32),
            shape((16, LW), F32),
            shape((16, LW), F32),
        ],
        in_specs=[vmem] * 6,
        out_specs=[vmem] * 5,
        scratch_shapes=[pltpu.VMEM((EH, LW), F32)] * 8 + [pltpu.VMEM((24, 128), F32)],
        compiler_params=pltpu.CompilerParams(vmem_limit_bytes=VMEM_LIMIT),
        name="basis",
    )(from_s, from_n, own_n, own_s, rhs, lev)


def polynomials(gathered):
    sums = jnp.sum(gathered, axis=0, keepdims=True)
    lane = lanes((1, 128))
    alone = sums[:, 64:65]
    distance = jnp.minimum(lane, 128 - lane)
    odd = lax.rem(lane, 2) == 1
    base = jnp.where(odd, sums[:, 1:2], sums[:, 0:1])
    moments = jnp.where(distance < 2, sums, jnp.where(distance < 16, 2.0 * sums - base, 0.0))
    row = rows((8, 128))
    lane = lanes((8, 128))
    quarter = lax.rem(lane, 4)
    origin = jnp.where(quarter == 0, alone, jnp.where(quarter == 2, -alone, 0.0))
    now = jnp.where(row == 0, moments, 0.0)
    now = jnp.where((row == 1) & (lane == 0), 2.0, now)
    now = jnp.where(row == 3, 1.0, now)
    now = jnp.where(row == 4, origin, now)
    before = jnp.zeros((8, 128), F32)
    corner = (row == 2) & (lane == 0)
    last_inv = last_ratio = None
    for k in range(ITERS):
        both = now[0:1, :] + now[4:5, :]
        size = both[:, k : k + 1]
        inv = 1.0 / size
        ratio = both[:, k + 1 : k + 2] * inv * (1.0 if k == 0 else 0.5)
        image = 0.5 * (roll(now, 1, 1) + roll(now, -1, 1))
        image = image + jnp.where(corner, 2.0 * now[3:4, 0:1], 0.0)
        if k == 0:
            after = image - ratio * now
        else:
            shrink = size * last_inv * (1.0 if k == 1 else 0.5)
            after = image - (ratio - last_ratio) * now - shrink * before
        last_inv = inv
        last_ratio = ratio
        before, now = now, after
    scale = 1.0 / now[3:4, 0:1]
    half = jnp.where(lanes((1, 128)) == 0, 0.5, 1.0)
    return now[2:3, :] * half * scale, now[1:2, :] * half * scale


def finish_kernel(gathered, basis, diag, sea, residual):
    lift, rest = polynomials(gathered[...])
    lift = [lift[:, j : j + 1] for j in range(ITERS)]
    rest = [rest[:, j : j + 1] for j in range(ITERS + 1)]
    for r in range(0, H, 8):
        here = slice(r, r + 8)
        c = basis[0, here, :]
        a, b = lift[0] * c, rest[0] * c
        for j in range(1, ITERS + 1):
            c = basis[j, here, :]
            b = b + rest[j] * c
            if j < ITERS:
                a = a + lift[j] * c
        sea[here, :] = a[:, :W]
        residual[here, :] = (diag[here, :] * b)[:, :W]


def finish_part(gathered, basis, diag):
    vmem = pl.BlockSpec(memory_space=pltpu.VMEM)
    shape = jax.ShapeDtypeStruct
    return pl.pallas_call(
        finish_kernel,
        out_shape=[shape((H, W), F32), shape((H, W), F32)],
        in_specs=[vmem] * 3,
        out_specs=[vmem] * 2,
        compiler_params=pltpu.CompilerParams(vmem_limit_bytes=VMEM_LIMIT),
        name="finish",
    )(gathered, basis, diag)


def edges_kernel(partial, flux_e, flux_w, flux_n, flux_s, out):
    k = pl.program_id(0)
    lane = lanes((8, 128))
    wide = lanes((8, W))
    f_n = flux_n[pl.ds(k, 1), :][:, :W]
    f_s = flux_s[pl.ds(k, 1), :][:, :W]
    row = rows((8, W))
    for r in range(0, H, 8):
        here = slice(r, r + 8)
        pick = lane == TR0 + k
        f_e = jnp.sum(jnp.where(pick, flux_e[here, :], 0.0), axis=1, keepdims=True)
        f_w = jnp.sum(jnp.where(pick, flux_w[here, :], 0.0), axis=1, keepdims=True)
        value = partial[0, here, :]
        value = value + jnp.where(wide == W - 1, f_e, 0.0) - jnp.where(wide == 0, f_w, 0.0)
        if r == 0:
            value = value - jnp.where(row == 0, f_s, 0.0)
        if r == H - 8:
            value = value + jnp.where(row == 7, f_n, 0.0)
        out[0, here, :] = value


def edges_part(partial, flux_e, flux_w, flux_n, flux_s):
    level = pl.BlockSpec((1, H, W), lambda k: (k, 0, 0))

    def whole(x):
        return pl.BlockSpec(x.shape, lambda k: (0, 0))

    return pl.pallas_call(
        edges_kernel,
        grid=(KL,),
        out_shape=jax.ShapeDtypeStruct((KL, H, W), F32),
        in_specs=[level] + [whole(x) for x in (flux_e, flux_w, flux_n, flux_s)],
        out_specs=level,
        input_output_aliases={0: 0},
        compiler_params=pltpu.CompilerParams(vmem_limit_bytes=VMEM_LIMIT),
        name="edges",
    )(partial, flux_e, flux_w, flux_n, flux_s)


def shards(tracer, east_velocity, north_velocity, kmt, block_mask, surface_forcing):
    nx, ny = lax.axis_size("gx"), lax.axis_size("gy")
    partial, rhs, lev, msg_e, msg_w, row_n, row_s = tracer_part(
        block_mask, kmt, surface_forcing, tracer, east_velocity, north_velocity
    )
    from_w = lax.ppermute(msg_e, "gx", [(i, (i + 1) % nx) for i in range(nx)])
    from_e = lax.ppermute(msg_w, "gx", [((i + 1) % nx, i) for i in range(nx)])
    rhs_x, lev_x, msg_n, msg_s, flux_e, flux_w = sides_part(
        from_w, from_e, msg_e, msg_w, rhs, lev, row_n, row_s
    )
    from_s = lax.ppermute(msg_n, "gy", [(i, i + 1) for i in range(ny - 1)])
    from_n = lax.ppermute(msg_s, "gy", [(i + 1, i) for i in range(ny - 1)])
    basis, diag, sums, flux_n, flux_s = basis_part(
        from_s, from_n, msg_n, msg_s, rhs_x, lev_x, nx * ny
    )
    updated = edges_part(partial, flux_e, flux_w, flux_n, flux_s)
    gathered = lax.all_to_all(sums, ("gx", "gy"), 0, 0, tiled=True)
    sea_level, residual = finish_part(gathered, basis, diag)
    return (updated, sea_level, residual)


def solution(mesh):
    in_specs = (
        P(None, "gy", "gx"),
        P(None, "gy", "gx"),
        P(None, "gy", "gx"),
        P("gy", "gx"),
        P("gy", "gx"),
        P("gy", "gx"),
    )
    out_specs = (P(None, "gy", "gx"), P("gy", "gx"), P("gy", "gx"))
    return jax.shard_map(shards, mesh=mesh, in_specs=in_specs, out_specs=out_specs, check_vma=False)
```

time: 1190 us -> 77.4 us (0.07)
  blocking collectives: 947 us -> 0 us
  waiting for transfers between devices: 62 us -> 6.42 us
  other arithmetic: 50.5 us -> 0 us
  Pallas kernels: 0 us -> 40.1 us
  local copies, waits for them, and re-layouts: 47.1 us -> 7.39 us
  starting transfers between devices: 56.7 us -> 22.3 us
  between operations: 20.8 us -> 0.69 us
    psum x15 -> x0, blocking collectives: 947 us -> none  [the longest x8 503 us: weighted_sum(): return lax.psum(jnp.sum(value), ('gx', 'gy'))]
    ppermute x40 -> x4, waiting for transfers between devices: 62 us -> 5.15 us  [the longest x1 3.61 us: shards(): from_n = lax.ppermute(msg_s, 'gy', [(i + 1, i) for i in range(ny - 1)])]
    ppermute x40 -> x4, starting transfers between devices: 56.7 us -> 12.9 us  [the longest x1 5.11 us: shards(): from_s = lax.ppermute(msg_n, 'gy', [(i, i + 1) for i in range(ny - 1)])]
    pallas_call x0 -> x5, Pallas kernels: none -> 40.1 us  [the longest x1 15.1 us: tracer_part(): pl.pallas_call(tracer_kernel, out_shape=[shape((KL, H, W), F32), shape((H...]
    slice x15 -> x0, local copies, waits for them, and re-layouts: 22.7 us -> none  [the longest x11 17 us: extended(): last = lax.slice_in_dim(array, length - width, length, axis=dim)]
    reduce_sum x17 -> x0, other arithmetic: 20.2 us -> none  [the longest x8 9.63 us: solve(): alpha = norm_now / lax.psum(jnp.sum(direction * image), ('gx', 'gy'))]
    concatenate x2 -> x0, other arithmetic: 15.5 us -> none  [extended(): array = jnp.concatenate([before, array, after], axis=dim)]
  transfers between devices with their start and end apart: 40 -> 5, of which waited for: 26 -> 3; matrix products, arithmetic and copies ran while one was open for 2% -> 0% of each run, Pallas kernels for 0% -> 10%
where the time goes in v1:
time: 77.4 us; the launch traced here: 76.9 us
  Pallas kernels  40.1 us (52%)
  starting transfers between devices  22.3 us (29%)
  local copies, waits for them, and re-layouts  7.39 us (10%)
  waiting for transfers between devices  6.42 us (8%)
    pallas_call x1, Pallas kernels, tracer_part(): pl.pallas_call(tracer_kernel, out_shape=[shape((KL, H, W), F32), shape((H...  15.1 us
    pallas_call x1, Pallas kernels, basis_part(): pl.pallas_call(basis_kernel, out_shape=[shape((ITERS + 1, EH, LW), F32),...  12.7 us
    all_to_all x1, starting transfers between devices, shards(): gathered = lax.all_to_all(sums, ('gx', 'gy'), 0, 0, tiled=True)  9.37 us
    pallas_call x1, Pallas kernels, edges_part(): pl.pallas_call(edges_kernel, grid=(KL,), out_shape=jax.ShapeDtypeStruct((...  8.06 us
    unnamed x12, local copies, waits for them, and re-layouts  7.39 us
    ppermute x1, starting transfers between devices, shards(): from_s = lax.ppermute(msg_n, 'gy', [(i, i + 1) for i in range(ny - 1)])  5.11 us
    ppermute x1, starting transfers between devices, shards(): from_e = lax.ppermute(msg_w, 'gx', [((i + 1) % nx, i) for i in range(nx)])  3.8 us
    ppermute x1, waiting for transfers between devices, shards(): from_n = lax.ppermute(msg_s, 'gy', [(i + 1, i) for i in range(ny - 1)])  3.61 us
  transfers between devices with their start and end apart: 5, of which 3 were waited for; matrix products, arithmetic and copies ran while one was open for 0% of the time, Pallas kernels for 10%

profile of v1, /device:TPU:1, one launch (start us, length us, event | category | flops | bytes accessed | tf_op | source)
XLA Modules:
  0.0 76.9 jit_solution(8974322407084504055)
XLA Ops:
  0.6 0.0 copy-start
  0.6 1.6 %copy-done = f32[12,120,360]{2,1,0:T(8,128)S(1)} copy-done((f32[12,120,360]{2,1,0:T(8,128)S(1)}, f32[12,120,360]{2,1,0:T(8,128)}, u32[]{:S(2)}) %copy-start) | copy-done | bytes 2073624
  2.3 0.0 copy-start.1
  2.3 1.6 %copy-done.1 = f32[12,120,360]{2,1,0:T(8,128)S(1)} copy-done((f32[12,120,360]{2,1,0:T(8,128)S(1)}, f32[12,120,360]{2,1,0:T(8,128)}, u32[]{:S(2)}) %copy-start.1) | copy-done | bytes 2073624
  3.9 0.0 copy-start.2
  3.9 1.6 %copy-done.2 = f32[12,120,360]{2,1,0:T(8,128)S(1)} copy-done((f32[12,120,360]{2,1,0:T(8,128)S(1)}, f32[12,120,360]{2,1,0:T(8,128)}, u32[]{:S(2)}) %copy-start.2) | copy-done | bytes 2073624
  5.5 0.0 copy-start.3
  5.5 0.9 %copy-done.3 = s32[120,360]{1,0:T(8,128)S(1)} copy-done((s32[120,360]{1,0:T(8,128)S(1)}, s32[120,360]{1,0:T(8,128)}, u32[]{:S(2)}) %copy-start.3) | copy-done | bytes 172824
  6.4 0.0 copy-start.4
  6.4 0.9 %copy-done.4 = f32[120,360]{1,0:T(8,128)S(1)} copy-done((f32[120,360]{1,0:T(8,128)S(1)}, f32[120,360]{1,0:T(8,128)}, u32[]{:S(2)}) %copy-start.4) | copy-done | bytes 172824
  7.4 0.0 copy-start.5
  7.4 0.7 copy-done.5
  8.0 15.1 %tracer.1 = (f32[12,120,360]{2,1,0:T(8,128)}, f32[120,384]{1,0:T(8,128)S(1)}, f32[120,384]{1,0:T(8,128)S(1)}, f32[120,128]{1,0:T(8,128)S(1)}, f32[120,128]{1,0:T...) custom-call(s32[2,4]{1,0:T(2,128)S(1)} %copy-done.5, s32[120,360]{1,0:T(8,128)S(1)} %copy-done.3, ...), custom_call_target="tpu_custom_call" | custom-call | tf_op jit(solution)/shard_map/tracer/pallas_call | solution.py:190
  23.1 2.1 %collective-permute-start = (f32[120,128]{1,0:T(8,128)S(1)}, f32[120,128]{1,0:T(8,128)S(1)}, u32[]{:S(2)}, u32[]{:S(2)}) collective-permute-start(f32[120,128]{1,0:T(8,128)S(1)} %get-tuple-element.24.own_e), channel_id=1, source_target_pairs={{0,8},{8,16},{16,24},{24,32},{32,40},{40,48},{48,56},{56,64},{64,7... | collective-permute-start | bytes 184328 | tf_op jit(solution)/shard_map/ppermute | solution.py:548
  25.2 3.8 %collective-permute-start.1 = (f32[120,128]{1,0:T(8,128)S(1)}, f32[120,128]{1,0:T(8,128)S(1)}, u32[]{:S(2)}, u32[]{:S(2)}) collective-permute-start(f32[120,128]{1,0:T(8,128)S(1)} %get-tuple-element.25.own_w), channel_id=1, source_target_pairs={{8,0},{16,8},{24,16},{32,24},{40,32},{48,40},{56,48},{64,56},{72,6... | collective-permute-start | bytes 184328 | tf_op jit(solution)/shard_map/ppermute | solution.py:549
  29.0 1.5 %collective-permute-done.from_w = f32[120,128]{1,0:T(8,128)S(1)} collective-permute-done((f32[120,128]{1,0:T(8,128)S(1)}, f32[120,128]{1,0:T(8,128)S(1)}, u32[]{:S(2)}, u32[]{:S(2)}) %collective-permute-start) | collective-permute-done | bytes 61472 | tf_op jit(solution)/shard_map/ppermute | solution.py:548
  30.6 0.0 collective-permute-done.1.from_e
  30.6 1.6 %sides.1 = (f32[120,384]{1,0:T(8,128)S(1)}, f32[120,384]{1,0:T(8,128)S(1)}, f32[56,384]{1,0:T(8,128)S(1)}, f32[40,384]{1,0:T(8,128)S(1)}, f32[120,128]{1,0:T(8,128)S(1)}, /*index=5*/f32[120,128]{1,0:T(8,128)S(1)}) custom-call(f32[120,128]{1,0:T(8,128)S(1)} %collective-permute-done.from_w, f32[120,128]{1,0:T(8,128)S(1)} %collective-permute-done.1.from_e, ...), custom_call_target="tpu_custom_call" | custom-call | tf_op jit(solution)/shard_map/sides/pallas_call | solution.py:265
  32.2 5.1 %collective-permute-start.2 = (f32[56,384]{1,0:T(8,128)S(1)}, f32[56,384]{1,0:T(8,128)S(1)}, u32[]{:S(2)}, u32[]{:S(2)}) collective-permute-start(f32[56,384]{1,0:T(8,128)S(1)} %get-tuple-element.32.own_n), channel_id=1, source_target_pairs={{0,1},{1,2},{2,3},{3,4},{4,5},{5,6},{6,7},{8,9},{9,10},{10,11},{11... | collective-permute-start | bytes 258056 | tf_op jit(solution)/shard_map/ppermute | solution.py:553
  37.3 1.9 %collective-permute-start.3 = (f32[40,384]{1,0:T(8,128)S(1)}, f32[40,384]{1,0:T(8,128)S(1)}, u32[]{:S(2)}, u32[]{:S(2)}) collective-permute-start(f32[40,384]{1,0:T(8,128)S(1)} %get-tuple-element.33.own_s), channel_id=1, source_target_pairs={{1,0},{2,1},{3,2},{4,3},{5,4},{6,5},{7,6},{9,8},{10,9},{11,10},{12... | collective-permute-start | bytes 184328 | tf_op jit(solution)/shard_map/ppermute | solution.py:554
  39.2 3.6 %collective-permute-done.3.from_n = f32[40,384]{1,0:T(8,128)S(1)} collective-permute-done((f32[40,384]{1,0:T(8,128)S(1)}, f32[40,384]{1,0:T(8,128)S(1)}, u32[]{:S(2)}, u32[]{:S(2)}) %collective-permute-start.3) | collective-permute-done | bytes 61472 | tf_op jit(solution)/shard_map/ppermute | solution.py:554
  42.8 0.0 collective-permute-done.2.from_s
  42.8 12.7 %basis.1 = (f32[9,144,384]{2,1,0:T(8,128)S(1)}, f32[120,384]{1,0:T(8,128)S(1)}, f32[128,128]{1,0:T(8,128)}, f32[16,384]{1,0:T(8,128)S(1)}, f32[16,384]{1,0:T(8,128)S(1)}) custom-call(f32[56,384]{1,0:T(8,128)S(1)} %collective-permute-done.2.from_s, f32[40,384]{1,0:T(8,128)S(1)} %collective-permute-done.3.from_n, f32[56,384]{1,0:T(8,128)S(1)} %get-tuple-element.32.own_n, ...), custom_call_target="tpu_custom_call" | custom-call | tf_op jit(solution)/shard_map/basis/pallas_call | solution.py:418
  55.5 9.4 %all-to-all-start = ((f32[128,1,128]{2,1,0:T(1,128)}), f32[128,1,128]{2,1,0:T(1,128)S(1)}, u32[]{:S(2)}, u32[]{:S(2)}) async-start(f32[128,1,128]{2,1,0:T(1,128)} %bitcast.1), calls=%async_computation | async-start | bytes 131072 | tf_op jit(solution)/shard_map/all_to_all | solution.py:559
  64.9 8.1 %edges.1 = f32[12,120,360]{2,1,0:T(8,128)} custom-call(f32[12,120,360]{2,1,0:T(8,128)} %get-tuple-element.23.partial, f32[120,128]{1,0:T(8,128)S(1)} %get-tuple-element.30.flux_e, f32[120,128]{1,0:T(8,128)S(1)} %get-tuple-element.31.flux_w, f32[16,384]{1,0:T(8,128)S(1)} %get-tuple-element.36.flux_n, ...), custom_call_target="tpu_custom_call", output_to_operand_aliasing={{}: (0, {})} | custom-call | tf_op jit(solution)/shard_map/edges/pallas_call | solution.py:531
  72.9 1.3 %all-to-all-done = f32[128,1,128]{2,1,0:T(1,128)S(1)} async-done(((f32[128,1,128]{2,1,0:T(1,128)}), f32[128,1,128]{2,1,0:T(1,128)S(1)}, u32[]{:S(2)}, u32[]{:S(2)}) %all-to-all-start) | async-done | bytes 65568 | tf_op jit(solution)/shard_map/all_to_all | solution.py:559
  74.2 2.7 %finish.1 = (f32[120,360]{1,0:T(8,128)}, f32[120,360]{1,0:T(8,128)}) custom-call(f32[128,128]{1,0:T(8,128)S(1)} %bitcast.4, f32[9,144,384]{2,1,0:T(8,128)S(1)} %get-tuple-element.39.basis, f32[120,384]{1,0:T(8,128)S(1)} %get-tuple-element.40.diag), custom_call_target="tpu_custom_call" | custom-call | tf_op jit(solution)/shard_map/finish/pallas_call | solution.py:494
Async XLA Ops:
  0.6 1.6 %copy-start = (f32[12,120,360]{2,1,0:T(8,128)S(1)}, f32[12,120,360]{2,1,0:T(8,128)}, u32[]{:S(2)}) copy-start(f32[12,120,360]{2,1,0:T(8,128)} %t_hbm.1) | copy-start | bytes 6220804
  2.3 1.6 %copy-start.1 = (f32[12,120,360]{2,1,0:T(8,128)S(1)}, f32[12,120,360]{2,1,0:T(8,128)}, u32[]{:S(2)}) copy-start(f32[12,120,360]{2,1,0:T(8,128)} %u_hbm.1) | copy-start | bytes 6220804
  3.9 1.6 %copy-start.2 = (f32[12,120,360]{2,1,0:T(8,128)S(1)}, f32[12,120,360]{2,1,0:T(8,128)}, u32[]{:S(2)}) copy-start(f32[12,120,360]{2,1,0:T(8,128)} %v_hbm.1) | copy-start | bytes 6220804
  5.5 0.9 %copy-start.3 = (s32[120,360]{1,0:T(8,128)S(1)}, s32[120,360]{1,0:T(8,128)}, u32[]{:S(2)}) copy-start(s32[120,360]{1,0:T(8,128)} %kmt_ref.1) | copy-start | bytes 518404
  6.4 0.9 %copy-start.4 = (f32[120,360]{1,0:T(8,128)S(1)}, f32[120,360]{1,0:T(8,128)}, u32[]{:S(2)}) copy-start(f32[120,360]{1,0:T(8,128)} %forcing_ref.1) | copy-start | bytes 518404
  7.4 0.7 copy-start.5
  23.1 7.4 %collective-permute-start = (f32[120,128]{1,0:T(8,128)S(1)}, f32[120,128]{1,0:T(8,128)S(1)}, u32[]{:S(2)}, u32[]{:S(2)}) collective-permute-start(f32[120,128]{1,0:T(8,128)S(1)} %get-tuple-element.24.own_e), channel_id=1, source_target_pairs={{0,8},{8,16},{16,24},{24,32},{32,40},{40,48},{48,56},{56,64},{64,7... | collective-permute-start | bytes 184328 | tf_op jit(solution)/shard_map/ppermute | solution.py:548
  25.2 5.3 %collective-permute-start.1 = (f32[120,128]{1,0:T(8,128)S(1)}, f32[120,128]{1,0:T(8,128)S(1)}, u32[]{:S(2)}, u32[]{:S(2)}) collective-permute-start(f32[120,128]{1,0:T(8,128)S(1)} %get-tuple-element.25.own_w), channel_id=1, source_target_pairs={{8,0},{16,8},{24,16},{32,24},{40,32},{48,40},{56,48},{64,56},{72,6... | collective-permute-start | bytes 184328 | tf_op jit(solution)/shard_map/ppermute | solution.py:549
  32.2 10.7 %collective-permute-start.2 = (f32[56,384]{1,0:T(8,128)S(1)}, f32[56,384]{1,0:T(8,128)S(1)}, u32[]{:S(2)}, u32[]{:S(2)}) collective-permute-start(f32[56,384]{1,0:T(8,128)S(1)} %get-tuple-element.32.own_n), channel_id=1, source_target_pairs={{0,1},{1,2},{2,3},{3,4},{4,5},{5,6},{6,7},{8,9},{9,10},{10,11},{11... | collective-permute-start | bytes 258056 | tf_op jit(solution)/shard_map/ppermute | solution.py:553
  37.3 5.5 %collective-permute-start.3 = (f32[40,384]{1,0:T(8,128)S(1)}, f32[40,384]{1,0:T(8,128)S(1)}, u32[]{:S(2)}, u32[]{:S(2)}) collective-permute-start(f32[40,384]{1,0:T(8,128)S(1)} %get-tuple-element.33.own_s), channel_id=1, source_target_pairs={{1,0},{2,1},{3,2},{4,3},{5,4},{6,5},{7,6},{9,8},{10,9},{11,10},{12... | collective-permute-start | bytes 184328 | tf_op jit(solution)/shard_map/ppermute | solution.py:554
  55.5 18.7 %all-to-all-start = ((f32[128,1,128]{2,1,0:T(1,128)}), f32[128,1,128]{2,1,0:T(1,128)S(1)}, u32[]{:S(2)}, u32[]{:S(2)}) async-start(f32[128,1,128]{2,1,0:T(1,128)} %bitcast.1), calls=%async_computation | async-start | bytes 131072 | tf_op jit(solution)/shard_map/all_to_all | solution.py:559

commit v2 on v1

--- a/solution.py
+++ b/solution.py
@@ -22,6 +22,8 @@
 LW = 384
 EH = 144
 
+EB = EH // 8
+
 GRAD = DT_STEP * KAPPA_H
 ADV = DT_STEP * 0.5
 VERT = DT_STEP * KAPPA_V
@@ -59,14 +61,28 @@
     return x if shift == 0 else pltpu.roll(x, shift, axis)
 
 
+def strided(ref, i, step):
+    return jnp.concatenate([ref[j, pl.ds(i, 8, step), :] for j in range(3)], axis=1)
+
+
+def put_strided(ref, i, step, value):
+    for j in range(3):
+        ref[j, pl.ds(i, 8, step), :] = value[:, 128 * j : 128 * j + 128]
+
+
+def tiles(ref, here, value):
+    for j in range(3):
+        ref[j, here, :] = value[:, 128 * j : 128 * j + 128]
+
+
 def thickness(level):
     return 1.0 + (0.5 / KL) * level
 
 
 def tracer_kernel(
-    mask_ref, kmt_ref, forcing_ref, t_hbm, u_hbm, v_hbm,
+    mask_hbm, kmt_hbm, forcing_hbm, t_hbm, u_hbm, v_hbm,
     upd_hbm, rhs_ref, lev_ref, msg_e, msg_w, row_n, row_s,
-    t_s, u_s, v_s, o_s, min_e, min_n, col, sem_in, sem_out,
+    t_s, u_s, v_s, o_s, kmt, forcing, mask, min_e, min_n, col, sem_in, sem_out, sem_2d,
 ):
     def load(i, k):
         src, dst = ((t_hbm, t_s), (u_hbm, u_s), (v_hbm, v_s))[i]
@@ -75,29 +91,38 @@
     def store(k):
         return pltpu.make_async_copy(o_s.at[k], upd_hbm.at[k], sem_out.at[k])
 
+    load_mask = pltpu.make_async_copy(mask_hbm, mask, sem_2d.at[0])
+    load_kmt = pltpu.make_async_copy(kmt_hbm, kmt, sem_2d.at[1])
+    load_forcing = pltpu.make_async_copy(forcing_hbm, forcing, sem_2d.at[2])
+    load_mask.start()
+    load_kmt.start()
     for k in range(KL):
         for i in range(3):
             load(i, k).start()
+    load_forcing.start()
 
     lane = lanes((8, LW))
     row = rows((8, LW))
+    load_mask.wait()
+    load_kmt.wait()
     for r in range(0, H, 8):
         keep = jnp.zeros((8, LW), jnp.int32)
         for b in range(W // BSX):
             inside = (lane >= b * BSX) & (lane < (b + 1) * BSX)
-            upper = jnp.where(row + r < BSY, mask_ref[0, b], mask_ref[1, b])
+            upper = jnp.where(row + r < BSY, mask[0, b], mask[1, b])
             keep = jnp.where(inside, upper, keep)
-        lev = widen(kmt_ref[r : r + 8, :], LW) * keep
+        lev = widen(kmt[r : r + 8, :], LW) * keep
         lev_ref[r : r + 8, :] = lev.astype(F32)
     for r in range(0, H, 8):
-        lev = lev_ref[r : r + 8, :]
+        here = slice(r, r + 8)
+        lev = lev_ref[here, :]
         if r + 8 < H:
             north = lev_ref[r + 1 : r + 9, :]
         else:
             north = jnp.where(row == 7, 0.0, roll(lev, -1, 0))
-        min_e[r : r + 8, :] = jnp.minimum(lev, roll(lev, -1, 1))
-        min_n[r : r + 8, :] = jnp.minimum(lev, north)
-        col[r : r + 8, :] = jnp.zeros((8, LW), F32)
+        min_e[here, :] = jnp.minimum(lev, roll(lev, -1, 1))
+        min_n[here, :] = jnp.minimum(lev, north)
+        col[here, :] = jnp.zeros((8, LW), F32)
     row_n[...] = jnp.zeros((32, LW), F32)
     row_s[...] = jnp.zeros((16, LW), F32)
 
@@ -116,30 +141,35 @@
         load(2, k).wait()
         kf = k.astype(F32)
         thick = thickness(kf)
-        before = jnp.zeros((8, W), F32)
+        f_low = jnp.zeros((8, W), F32)
+        t = t_s[k, 0:8, :]
+        t_turned = roll(t, -1, 0)
         for r in range(0, H, 8):
             here = slice(r, r + 8)
-            t = t_s[k, here, :]
+            if r + 8 < H:
+                ahead = t_s[k, r + 8 : r + 16, :]
+                ahead_turned = roll(ahead, -1, 0)
+                t_n = jnp.where(row360 == 7, ahead_turned, t_turned)
+            else:
+                ahead = ahead_turned = None
+                t_n = t_turned
             t_e = roll(widen(t, LW), -1, 1)[:, :W]
-            if r + 8 < H:
-                t_n = t_s[k, r + 1 : r + 9, :]
-            else:
-                t_n = roll(t, -1, 0)
-            u = u_s[k, here, :]
-            v = v_s[k, here, :]
             lev = lev_ref[here, :W]
-            f_e = jnp.where(min_e[here, :W] > kf, GRAD * (t_e - t) - (ADV * u) * (t + t_e), 0.0)
-            f_n = jnp.where(min_n[here, :W] > kf, GRAD * (t_n - t) - (ADV * v) * (t + t_n), 0.0)
+            f_e = GRAD * (t_e - t) - (ADV * u_s[k, here, :]) * (t + t_e)
+            f_n = GRAD * (t_n - t) - (ADV * v_s[k, here, :]) * (t + t_n)
+            f_e = jnp.where(min_e[here, :W] > kf, f_e, 0.0)
+            f_n = jnp.where(min_n[here, :W] > kf, f_n, 0.0)
             f_w = roll(widen(f_e, LW), 1, 1)[:, :W]
-            shifted = roll(f_n, 1, 0)
-            f_s = jnp.where(row360 == 0, before, shifted)
-            before = shifted
+            f_turned = roll(f_n, 1, 0)
+            f_s = jnp.where(row360 == 0, f_low, f_turned)
+            f_low = f_turned
             wet = lev > kf
             up = jnp.where(lev > kf + 1.0, t_s[above, here, :] - t, 0.0)
             down = jnp.where(wet, t - t_s[below, here, :], 0.0)
             updated = t + ((f_e - f_w) + (f_n - f_s) + VERT * (up - down))
             o_s[k, here, :] = updated
             col[here, :W] += jnp.where(wet, thick * updated, 0.0)
+            t, t_turned = ahead, ahead_turned
         store(k).start()
         row_s[pl.ds(k, 1), :] = widen(t_s[k, 0:1, :], LW)
         row_n[pl.ds(k, 1), :] = widen(t_s[k, H - 1 : H, :], LW)
@@ -148,13 +178,13 @@
 
     lax.fori_loop(0, KL, level, 0)
 
+    load_forcing.wait()
     lane = lanes((8, 128))
     for r in range(0, H, 8):
         here = slice(r, r + 8)
         lev = lev_ref[here, :]
-        rhs = jnp.where(
-            lev > 0.0, ROOT * col[here, :] + widen(forcing_ref[here, :], LW), 0.0
-        )
+        rhs = ROOT * col[here, :W] + forcing[here, :]
+        rhs = widen(jnp.where(lev[:, :W] > 0.0, rhs, 0.0), LW)
         rhs_ref[here, :] = rhs
         east = jnp.where(lane < LEV0, roll(rhs[:, 256:], 32, 1), roll(lev[:, 256:], LEV0 - 95, 1))
         west = jnp.where(lane < LEV0, rhs[:, :128], roll(lev[:, :128], LEV0, 1))
@@ -185,7 +215,7 @@
 
 def tracer_part(mask, kmt, forcing, tracer, east, north):
     vmem = pl.BlockSpec(memory_space=pltpu.VMEM)
-    hbm = pl.BlockSpec(memory_space=pl.ANY)
+    hbm = pl.BlockSpec(memory_space=pltpu.HBM)
     shape = jax.ShapeDtypeStruct
     return pl.pallas_call(
         tracer_kernel,
@@ -198,14 +228,19 @@
             shape((32, LW), F32),
             shape((16, LW), F32),
         ],
-        in_specs=[pl.BlockSpec(memory_space=pltpu.SMEM), vmem, vmem, hbm, hbm, hbm],
+        in_specs=[hbm] * 6,
         out_specs=[hbm] + [vmem] * 6,
         scratch_shapes=[pltpu.VMEM((KL, H, W), F32)] * 4
+        + [pltpu.VMEM((H, W), jnp.int32), pltpu.VMEM((H, W), F32), pltpu.SMEM(mask.shape, jnp.int32)]
         + [pltpu.VMEM((H, LW), F32)] * 3
-        + [pltpu.SemaphoreType.DMA((3, KL)), pltpu.SemaphoreType.DMA((KL,))],
+        + [
+            pltpu.SemaphoreType.DMA((3, KL)),
+            pltpu.SemaphoreType.DMA((KL,)),
+            pltpu.SemaphoreType.DMA((3,)),
+        ],
         compiler_params=pltpu.CompilerParams(vmem_limit_bytes=VMEM_LIMIT),
         name="tracer",
-    )(mask, kmt, forcing, tracer, east, north)
+    )(*(pltpu.with_memory_space_constraint(x, pltpu.HBM) for x in (mask, kmt, forcing, tracer, east, north)))
 
 
 def sides_kernel(
@@ -280,98 +315,92 @@
 
 
 def basis_kernel(
-    from_s, from_n, own_n, own_s, rhs_ref, lev_ref,
-    basis, diag, sums, flux_n, flux_s,
-    depth, face_e, face_n, w_e, w_w, w_n, w_s, weight, parts,
+    from_s, from_n, own_n, own_s, rhs_ref, lev_ref, partial,
+    basis, diag, sums, updated,
+    lev_x, rhs_x, w_e, w_w, w_n, w_s, weight, parts, slab_n, slab_s, sem,
 ):
+    high, low = pl.ds(H - 8, 8), pl.ds(0, 8)
+    loads = (
+        pltpu.make_async_copy(partial.at[:, high, :], slab_n, sem.at[0]),
+        pltpu.make_async_copy(partial.at[:, low, :], slab_s, sem.at[1]),
+    )
+    stores = (
+        pltpu.make_async_copy(slab_n, updated.at[:, high, :], sem.at[2]),
+        pltpu.make_async_copy(slab_s, updated.at[:, low, :], sem.at[3]),
+    )
+    for load in loads:
+        load.start()
     lev_row = rows((16, LW))
     kf = lev_row.astype(F32)
     factor = ROOT * thickness(kf)
 
-    def face(t_from, t_to, vel, lev):
-        flux = GRAD * (t_to - t_from) - (ADV * vel) * (t_from + t_to)
-        return jnp.where((lev_row < KL) & (lev > kf), flux, 0.0)
+    def flux(t_from, t_to, vel, lev):
+        value = GRAD * (t_to - t_from) - (ADV * vel) * (t_from + t_to)
+        return jnp.where((lev_row < KL) & (lev > kf), value, 0.0)
 
     tr = slice(R_TR, R_TR + 16)
     ve = slice(R_VE, R_VE + 16)
     lev_n = jnp.minimum(lev_ref[H - 1 : H, :], from_n[R_LEV : R_LEV + 1, :])
     lev_s = jnp.minimum(lev_ref[0:1, :], from_s[R_LEV + 15 : R_LEV + 16, :])
-    f_n = face(own_n[tr, :], from_n[tr, :], own_n[ve, :], lev_n)
-    f_s = face(from_s[tr, :], own_s[tr, :], from_s[ve, :], lev_s)
-    flux_n[...] = f_n
-    flux_s[...] = f_s
+    f_n = flux(own_n[tr, :], from_n[tr, :], own_n[ve, :], lev_n)
+    f_s = flux(from_s[tr, :], own_s[tr, :], from_s[ve, :], lev_s)
     c_n = jnp.sum(factor * f_n, axis=0, keepdims=True)
     c_s = jnp.sum(factor * f_s, axis=0, keepdims=True)
 
     row = rows((8, LW))
+    ninth = jnp.where(row == 7, from_s[R_LEV : R_LEV + 8, :], 0.0)
+    ninth = jnp.where(row == 0, from_n[R_LEV + 8 : R_LEV + 16, :], ninth)
+    tiles(lev_x, slice(0, H), lev_ref[...])
+    tiles(lev_x, slice(H, H + 8), from_n[R_LEV : R_LEV + 8, :])
+    tiles(lev_x, slice(H + 8, H + 16), ninth)
+    tiles(lev_x, slice(H + 16, EH), from_s[R_LEV + 8 : R_LEV + 16, :])
+    tiles(rhs_x, slice(0, 8), rhs_ref[0:8, :] - jnp.where(row == 0, c_s, 0.0))
+    tiles(rhs_x, slice(8, H - 8), rhs_ref[8 : H - 8, :])
+    tiles(rhs_x, slice(H - 8, H), rhs_ref[H - 8 : H, :] + jnp.where(row == 7, c_n, 0.0))
+    tiles(rhs_x, slice(H, H + 8), from_n[0:8, :] - jnp.where(row == 0, c_n, 0.0))
+    tiles(rhs_x, slice(H + 8, H + 16), jnp.zeros((8, LW), F32))
+    tiles(rhs_x, slice(H + 16, EH), from_s[0:8, :] + jnp.where(row == 7, c_s, 0.0))
+
+    def depth_of(i):
+        lev = strided(lev_x, i, EB)
+        return lev + lev * (lev - 1.0) * (0.25 / KL)
+
+    def face(d, other):
+        return jnp.where((d > 0.0) & (other > 0.0), 0.5 * (d + other), 0.0)
+
     lane = lanes((8, LW))
-
-    def level_rows(r):
-        if r < H:
-            return lev_ref[r : r + 8, :]
-        if r == H:
-            return from_n[R_LEV : R_LEV + 8, :]
-        if r == H + 8:
-            first = from_n[R_LEV + 8 : R_LEV + 9, :]
-            last = from_s[R_LEV + 7 : R_LEV + 8, :]
-            return jnp.where(row == 0, first, jnp.where(row == 7, last, 0.0))
-        return from_s[R_LEV + 8 : R_LEV + 16, :]
-
-    def rhs_rows(r):
-        if r < H:
-            value = rhs_ref[r : r + 8, :]
-            if r == 0:
-                value = value - jnp.where(row == 0, c_s, 0.0)
-            if r == H - 8:
-                value = value + jnp.where(row == 7, c_n, 0.0)
-            return value
-        if r == H:
-            return from_n[0:8, :] - jnp.where(row == 0, c_n, 0.0)
-        if r == H + 8:
-            return jnp.zeros((8, LW), F32)
-        return from_s[0:8, :] + jnp.where(row == 7, c_s, 0.0)
-
-    def north(ref, r):
-        if r + 8 < EH:
-            return ref[r + 1 : r + 9, :]
-        return jnp.where(row == 7, roll(ref[0:8, :], -1, 0), roll(ref[r : r + 8, :], -1, 0))
-
-    def south(ref, r):
-        if r > 0:
-            return ref[r - 1 : r + 7, :]
-        return jnp.where(row == 0, roll(ref[EH - 8 : EH, :], 1, 0), roll(ref[0:8, :], 1, 0))
-
-    for r in range(0, EH, 8):
-        lev = level_rows(r)
-        depth[r : r + 8, :] = lev + lev * (lev - 1.0) * (0.25 / KL)
-    for r in range(0, EH, 8):
-        here = slice(r, r + 8)
-        d = depth[here, :]
-        d_e, d_n = roll(d, -1, 1), north(depth, r)
-        face_e[here, :] = jnp.where((d > 0.0) & (d_e > 0.0), 0.5 * (d + d_e), 0.0)
-        face_n[here, :] = jnp.where((d > 0.0) & (d_n > 0.0), 0.5 * (d + d_n), 0.0)
+    first = depth_of(0)
+    last = depth_of(EB - 1)
+    beyond = roll(first, -1, 0)
+    n_last = face(last, beyond)
+    s = roll(n_last, 1, 0)
     lone = jnp.zeros((8, LW), F32)
-    for r in range(0, EH, 8):
-        here = slice(r, r + 8)
-        d = depth[here, :]
-        e, n = face_e[here, :], face_n[here, :]
+    d = first
+    for i in range(EB):
+        if i < EB - 1:
+            d_n = last if i == EB - 2 else depth_of(i + 1)
+            n = face(d, d_n)
+        else:
+            d_n, n = beyond, n_last
+        e = face(d, roll(d, -1, 1))
         w = roll(e, 1, 1)
-        s = south(face_n, r)
-        faces = e + w + n + s
+        faces = (e + w) + (n + s)
         dg = jnp.where(d > 0.0, SHIFT * d + faces, 1.0)
         inv = 1.0 / dg
-        z = rhs_rows(r) * inv
-        basis[0, here, :] = z
-        w_e[here, :] = e * inv
-        w_w[here, :] = w * inv
-        w_n[here, :] = n * inv
-        w_s[here, :] = s * inv
-        if r < H:
-            diag[here, :] = dg
-            own = jnp.where(lane < W, dg, 0.0)
-            joined = faces > 0.0
-            weight[here, :] = jnp.where(joined, own, 0.0)
-            lone = lone + jnp.where(joined, 0.0, own * z * z)
+        z = strided(rhs_x, i, EB) * inv
+        basis[0, i] = z
+        inv = 2.0 * inv
+        w_e[i] = e * inv
+        w_w[i] = w * inv
+        w_n[i] = n * inv
+        w_s[i] = s * inv
+        diag[i] = dg
+        own = (lane < W) & (row * EB + i < H)
+        own = jnp.where(own, dg, 0.0)
+        joined = faces > 0.0
+        weight[i] = jnp.where(joined, own, 0.0)
+        lone = lone + jnp.where(joined, 0.0, own * z * z)
+        d, s = d_n, n
 
     def fold(x):
         return jnp.sum(x[:, :128] + x[:, 128:256] + x[:, 256:], axis=0, keepdims=True)
@@ -379,30 +408,47 @@
     parts[...] = jnp.zeros((24, 128), F32)
     parts[16:17, :] = fold(lone)
 
-    def step(k, carry):
-        first = k == 1
-        twice = jnp.where(first, 1.0, 2.0)
-        keep = jnp.where(first, 0.0, 1.0)
-        older = jnp.maximum(k - 2, 0)
+    def step(k, older):
         now = basis.at[k - 1]
         even = jnp.zeros((8, LW), F32)
         odd = jnp.zeros((8, LW), F32)
-        for r in range(0, EH, 8):
-            here = slice(r, r + 8)
-            c = now[here, :]
-            image = w_e[here, :] * roll(c, -1, 1) + w_w[here, :] * roll(c, 1, 1)
-            image = image + (w_n[here, :] * north(now, r) + w_s[here, :] * south(now, r))
-            value = twice * image - keep * basis[older, here, :]
-            basis[k, here, :] = value
-            if r < H:
-                scaled = weight[here, :] * c
-                even = even + scaled * c
-                odd = odd + scaled * value
+        first = now[0]
+        last = now[EB - 1]
+        beyond = roll(first, -1, 0)
+        c_s = roll(last, 1, 0)
+        c = first
+        for i in range(EB):
+            if i < EB - 1:
+                c_n = last if i == EB - 2 else now[i + 1]
+            else:
+                c_n = beyond
+            image = w_e[i] * roll(c, -1, 1) + w_w[i] * roll(c, 1, 1)
+            image = image + (w_n[i] * c_n + w_s[i] * c_s)
+            value = 0.5 * image if older is None else image - basis[older, i]
+            basis[k, i] = value
+            scaled = weight[i] * c
+            even = even + scaled * c
+            odd = odd + scaled * value
+            c_s, c = c, c_n
         parts[pl.ds(2 * k - 2, 1), :] = fold(even)
         parts[pl.ds(2 * k - 1, 1), :] = fold(odd)
+
+    def later_step(k, carry):
+        step(k, k - 2)
         return carry
 
-    lax.fori_loop(1, ITERS + 1, step, 0)
+    step(1, None)
+    row360 = rows((8, W))
+    for load in loads:
+        load.wait()
+    for k in range(KL):
+        at_n = jnp.where(row360 == 7, f_n[k : k + 1, :W], 0.0)
+        at_s = jnp.where(row360 == 0, f_s[k : k + 1, :W], 0.0)
+        slab_n[k] = slab_n[k] + at_n
+        slab_s[k] = slab_s[k] - at_s
+    for store in stores:
+        store.start()
+    lax.fori_loop(2, ITERS + 1, later_step, 0)
 
     total = jnp.sum(parts[...], axis=1, keepdims=True)
     prow = rows((24, 128))
@@ -410,26 +456,33 @@
     place = (prow < 16) & ((plane == prow) | (plane == 128 - prow)) | (prow == 16) & (plane == 64)
     line = jnp.sum(jnp.where(place, total, 0.0), axis=0, keepdims=True)
     sums[...] = jnp.broadcast_to(line, sums.shape)
-
-
-def basis_part(from_s, from_n, own_n, own_s, rhs, lev, count):
+    for store in stores:
+        store.wait()
+
+
+def basis_part(from_s, from_n, own_n, own_s, rhs, lev, partial, count):
     vmem = pl.BlockSpec(memory_space=pltpu.VMEM)
+    hbm = pl.BlockSpec(memory_space=pltpu.HBM)
     shape = jax.ShapeDtypeStruct
     return pl.pallas_call(
         basis_kernel,
         out_shape=[
-            shape((ITERS + 1, EH, LW), F32),
-            shape((H, LW), F32),
+            shape((ITERS + 1, EB, 8, LW), F32),
+            shape((EB, 8, LW), F32),
             shape((count, 128), F32),
-            shape((16, LW), F32),
-            shape((16, LW), F32),
+            shape((KL, H, W), F32),
         ],
-        in_specs=[vmem] * 6,
-        out_specs=[vmem] * 5,
-        scratch_shapes=[pltpu.VMEM((EH, LW), F32)] * 8 + [pltpu.VMEM((24, 128), F32)],
+        in_specs=[vmem] * 6 + [hbm],
+        out_specs=[vmem] * 3 + [hbm],
+        input_output_aliases={6: 3},
+        scratch_shapes=[pltpu.VMEM((3, EH, 128), F32)] * 2
+        + [pltpu.VMEM((EB, 8, LW), F32)] * 5
+        + [pltpu.VMEM((24, 128), F32)]
+        + [pltpu.VMEM((KL, 8, W), F32)] * 2
+        + [pltpu.SemaphoreType.DMA((4,))],
         compiler_params=pltpu.CompilerParams(vmem_limit_bytes=VMEM_LIMIT),
         name="basis",
-    )(from_s, from_n, own_n, own_s, rhs, lev)
+    )(from_s, from_n, own_n, own_s, rhs, lev, partial)
 
 
 def polynomials(gathered):
@@ -471,21 +524,25 @@
     return now[2:3, :] * half * scale, now[1:2, :] * half * scale
 
 
-def finish_kernel(gathered, basis, diag, sea, residual):
+def finish_kernel(gathered, basis, diag, sea, residual, sea_t, residual_t):
     lift, rest = polynomials(gathered[...])
     lift = [lift[:, j : j + 1] for j in range(ITERS)]
     rest = [rest[:, j : j + 1] for j in range(ITERS + 1)]
-    for r in range(0, H, 8):
-        here = slice(r, r + 8)
-        c = basis[0, here, :]
+    for i in range(EB):
+        c = basis[0, i]
         a, b = lift[0] * c, rest[0] * c
         for j in range(1, ITERS + 1):
-            c = basis[j, here, :]
+            c = basis[j, i]
             b = b + rest[j] * c
             if j < ITERS:
                 a = a + lift[j] * c
-        sea[here, :] = a[:, :W]
-        residual[here, :] = (diag[here, :] * b)[:, :W]
+        b = diag[i] * b
+        put_strided(sea_t, i, EB, a)
+        put_strided(residual_t, i, EB, b)
+    for out, by_tile in ((sea, sea_t), (residual, residual_t)):
+        out[:, 0:128] = by_tile[0, :H, :]
+        out[:, 128:256] = by_tile[1, :H, :]
+        out[:, 256:W] = by_tile[2, :H, : W - 256]
 
 
 def finish_part(gathered, basis, diag):
@@ -496,48 +553,54 @@
         out_shape=[shape((H, W), F32), shape((H, W), F32)],
         in_specs=[vmem] * 3,
         out_specs=[vmem] * 2,
+        scratch_shapes=[pltpu.VMEM((3, EH, 128), F32)] * 2,
         compiler_params=pltpu.CompilerParams(vmem_limit_bytes=VMEM_LIMIT),
         name="finish",
     )(gathered, basis, diag)
 
 
-def edges_kernel(partial, flux_e, flux_w, flux_n, flux_s, out):
-    k = pl.program_id(0)
+def edges_kernel(flux_e, flux_w, src, dst, level, sem_in, sem_out):
+    def load(k):
+        return pltpu.make_async_copy(src.at[k], level.at[k], sem_in.at[k])
+
+    def store(k):
+        return pltpu.make_async_copy(level.at[k], dst.at[k], sem_out.at[k])
+
+    for k in range(KL):
+        load(k).start()
     lane = lanes((8, 128))
-    wide = lanes((8, W))
-    f_n = flux_n[pl.ds(k, 1), :][:, :W]
-    f_s = flux_s[pl.ds(k, 1), :][:, :W]
-    row = rows((8, W))
-    for r in range(0, H, 8):
-        here = slice(r, r + 8)
-        pick = lane == TR0 + k
-        f_e = jnp.sum(jnp.where(pick, flux_e[here, :], 0.0), axis=1, keepdims=True)
-        f_w = jnp.sum(jnp.where(pick, flux_w[here, :], 0.0), axis=1, keepdims=True)
-        value = partial[0, here, :]
-        value = value + jnp.where(wide == W - 1, f_e, 0.0) - jnp.where(wide == 0, f_w, 0.0)
-        if r == 0:
-            value = value - jnp.where(row == 0, f_s, 0.0)
-        if r == H - 8:
-            value = value + jnp.where(row == 7, f_n, 0.0)
-        out[0, here, :] = value
-
-
-def edges_part(partial, flux_e, flux_w, flux_n, flux_s):
-    level = pl.BlockSpec((1, H, W), lambda k: (k, 0, 0))
-
-    def whole(x):
-        return pl.BlockSpec(x.shape, lambda k: (0, 0))
-
+    lane_e = lanes((8, W - 256))
+    for k in range(KL):
+        load(k).wait()
+        for r in range(0, H, 8):
+            here = slice(r, r + 8)
+            at_w = jnp.where(lane == 0, roll(flux_w[here, :], -TR0 - k, 1), 0.0)
+            at_e = roll(flux_e[here, :], W - 257 - TR0 - k, 1)[:, : W - 256]
+            at_e = jnp.where(lane_e == W - 257, at_e, 0.0)
+            level[k, here, :128] = level[k, here, :128] - at_w
+            level[k, here, 256:W] = level[k, here, 256:W] + at_e
+        store(k).start()
+    for k in range(KL):
+        store(k).wait()
+
+
+def edges_part(partial, flux_e, flux_w):
+    vmem = pl.BlockSpec(memory_space=pltpu.VMEM)
+    hbm = pl.BlockSpec(memory_space=pltpu.HBM)
     return pl.pallas_call(
         edges_kernel,
-        grid=(KL,),
         out_shape=jax.ShapeDtypeStruct((KL, H, W), F32),
-        in_specs=[level] + [whole(x) for x in (flux_e, flux_w, flux_n, flux_s)],
-        out_specs=level,
-        input_output_aliases={0: 0},
+        in_specs=[vmem, vmem, hbm],
+        out_specs=hbm,
+        input_output_aliases={2: 0},
+        scratch_shapes=[
+            pltpu.VMEM((KL, H, W), F32),
+            pltpu.SemaphoreType.DMA((KL,)),
+            pltpu.SemaphoreType.DMA((KL,)),
+        ],
         compiler_params=pltpu.CompilerParams(vmem_limit_bytes=VMEM_LIMIT),
         name="edges",
-    )(partial, flux_e, flux_w, flux_n, flux_s)
+    )(flux_e, flux_w, partial)
 
 
 def shards(tracer, east_velocity, north_velocity, kmt, block_mask, surface_forcing):
@@ -552,10 +615,10 @@
     )
     from_s = lax.ppermute(msg_n, "gy", [(i, i + 1) for i in range(ny - 1)])
     from_n = lax.ppermute(msg_s, "gy", [(i + 1, i) for i in range(ny - 1)])
-    basis, diag, sums, flux_n, flux_s = basis_part(
-        from_s, from_n, msg_n, msg_s, rhs_x, lev_x, nx * ny
+    partial = edges_part(partial, flux_e, flux_w)
+    basis, diag, sums, updated = basis_part(
+        from_s, from_n, msg_n, msg_s, rhs_x, lev_x, partial, nx * ny
     )
-    updated = edges_part(partial, flux_e, flux_w, flux_n, flux_s)
     gathered = lax.all_to_all(sums, ("gx", "gy"), 0, 0, tiled=True)
     sea_level, residual = finish_part(gathered, basis, diag)
     return (updated, sea_level, residual)

time: 77.4 us -> 56.8 us (0.73)
  blocking collectives: 0 us -> 18.6 us
  Pallas kernels: 40.1 us -> 22.3 us
  starting transfers between devices: 22.3 us -> 12.9 us
  local copies, waits for them, and re-layouts: 7.39 us -> 0 us
  waiting for transfers between devices: 6.42 us -> 2.07 us
    all_to_all x0 -> x1, blocking collectives: none -> 18.6 us  [shards(): gathered = lax.all_to_all(sums, ('gx', 'gy'), 0, 0, tiled=True)]
    pallas_call x2, Pallas kernels: 20.7 us -> 9.58 us  [the longest x1 6.51 us: basis_part(): pl.pallas_call(basis_kernel, out_shape=[shape((ITERS + 1, EB, 8, LW), F32...]
    all_to_all x1 -> x0, starting transfers between devices: 9.37 us -> none  [shards(): gathered = lax.all_to_all(sums, ('gx', 'gy'), 0, 0, tiled=True)]
    unnamed x12 -> x0, local copies, waits for them, and re-layouts: 7.39 us -> none
    pallas_call x1, Pallas kernels: 15.1 us -> 8.37 us  [tracer_part(): pl.pallas_call(tracer_kernel, out_shape=[shape((KL, H, W), F32), shape((H...]
    ppermute x1, waiting for transfers between devices: 3.61 us -> 0.54 us  [shards(): from_n = lax.ppermute(msg_s, 'gy', [(i + 1, i) for i in range(ny - 1)])]
    all_to_all x1 -> x0, waiting for transfers between devices: 1.27 us -> none  [shards(): gathered = lax.all_to_all(sums, ('gx', 'gy'), 0, 0, tiled=True)]
  transfers between devices with their start and end apart: 5 -> 4, of which waited for: 3 -> 2; matrix products, arithmetic and copies ran while one was open for 0% -> 0% of each run, Pallas kernels for 10% -> 5%
where the time goes in v2:
time: 56.8 us; the launch traced here: 56.6 us
  Pallas kernels  22.3 us (39%)
  blocking collectives  18.6 us (33%)
  starting transfers between devices  12.9 us (23%)
  waiting for transfers between devices  2.07 us (4%)
  between operations  0.68 us (1%)
    all_to_all x1, blocking collectives, shards(): gathered = lax.all_to_all(sums, ('gx', 'gy'), 0, 0, tiled=True)  18.6 us
    pallas_call x1, Pallas kernels, tracer_part(): pl.pallas_call(tracer_kernel, out_shape=[shape((KL, H, W), F32), shape((H...  8.37 us
    pallas_call x1, Pallas kernels, basis_part(): pl.pallas_call(basis_kernel, out_shape=[shape((ITERS + 1, EB, 8, LW), F32...  6.51 us
    ppermute x1, starting transfers between devices, shards(): from_s = lax.ppermute(msg_n, 'gy', [(i, i + 1) for i in range(ny - 1)])  5.11 us
    ppermute x1, starting transfers between devices, shards(): from_e = lax.ppermute(msg_w, 'gx', [((i + 1) % nx, i) for i in range(nx)])  3.8 us
    pallas_call x1, Pallas kernels, edges_part(): pl.pallas_call(edges_kernel, out_shape=jax.ShapeDtypeStruct((KL, H, W), F...  3.07 us
    pallas_call x1, Pallas kernels, finish_part(): pl.pallas_call(finish_kernel, out_shape=[shape((H, W), F32), shape((H, W)...  2.73 us
    ppermute x1, starting transfers between devices, shards(): from_w = lax.ppermute(msg_e, 'gx', [(i, (i + 1) % nx) for i in range(nx)])  2.11 us
  transfers between devices with their start and end apart: 4, of which 2 were waited for; matrix products, arithmetic and copies ran while one was open for 0% of the time, Pallas kernels for 5%

profile of v2, /device:TPU:1, one launch (start us, length us, event | category | flops | bytes accessed | tf_op | source)
XLA Modules:
  0.0 56.6 jit_solution(12470728455364648886)
XLA Ops:
  0.6 8.4 %tracer.1 = (f32[12,120,360]{2,1,0:T(8,128)}, f32[120,384]{1,0:T(8,128)S(1)}, f32[120,384]{1,0:T(8,128)S(1)}, f32[120,128]{1,0:T(8,128)S(1)}, f32[120,128]{1,0:T...) custom-call(s32[2,4]{1,0:T(2,128)} %mask_hbm.1, s32[120,360]{1,0:T(8,128)} %kmt_hbm.1, f32[120,360]{1,0:T(8,128)} %forcing_hbm.1, ...), custom_call_target="tpu_custom_call" | custom-call | tf_op jit(solution)/shard_map/tracer/pallas_call | solution.py:220
  9.0 2.1 %collective-permute-start = (f32[120,128]{1,0:T(8,128)S(1)}, f32[120,128]{1,0:T(8,128)S(1)}, u32[]{:S(2)}, u32[]{:S(2)}) collective-permute-start(f32[120,128]{1,0:T(8,128)S(1)} %get-tuple-element.22.own_e), channel_id=1, source_target_pairs={{0,8},{8,16},{16,24},{24,32},{32,40},{40,48},{48,56},{56,64},{64,7... | collective-permute-start | bytes 184328 | tf_op jit(solution)/shard_map/ppermute | solution.py:611
  11.1 3.8 %collective-permute-start.1 = (f32[120,128]{1,0:T(8,128)S(1)}, f32[120,128]{1,0:T(8,128)S(1)}, u32[]{:S(2)}, u32[]{:S(2)}) collective-permute-start(f32[120,128]{1,0:T(8,128)S(1)} %get-tuple-element.23.own_w), channel_id=1, source_target_pairs={{8,0},{16,8},{24,16},{32,24},{40,32},{48,40},{56,48},{64,56},{72,6... | collective-permute-start | bytes 184328 | tf_op jit(solution)/shard_map/ppermute | solution.py:612
  14.9 1.5 %collective-permute-done.from_w = f32[120,128]{1,0:T(8,128)S(1)} collective-permute-done((f32[120,128]{1,0:T(8,128)S(1)}, f32[120,128]{1,0:T(8,128)S(1)}, u32[]{:S(2)}, u32[]{:S(2)}) %collective-permute-start) | collective-permute-done | bytes 61472 | tf_op jit(solution)/shard_map/ppermute | solution.py:611
  16.5 0.0 collective-permute-done.1.from_e
  16.5 1.6 %sides.1 = (f32[120,384]{1,0:T(8,128)S(1)}, f32[120,384]{1,0:T(8,128)S(1)}, f32[56,384]{1,0:T(8,128)S(1)}, f32[40,384]{1,0:T(8,128)S(1)}, f32[120,128]{1,0:T(8,128)S(1)}, /*index=5*/f32[120,128]{1,0:T(8,128)S(1)}) custom-call(f32[120,128]{1,0:T(8,128)S(1)} %collective-permute-done.from_w, f32[120,128]{1,0:T(8,128)S(1)} %collective-permute-done.1.from_e, ...), custom_call_target="tpu_custom_call" | custom-call | tf_op jit(solution)/shard_map/sides/pallas_call | solution.py:300
  18.1 5.1 %collective-permute-start.2 = (f32[56,384]{1,0:T(8,128)S(1)}, f32[56,384]{1,0:T(8,128)S(1)}, u32[]{:S(2)}, u32[]{:S(2)}) collective-permute-start(f32[56,384]{1,0:T(8,128)S(1)} %get-tuple-element.28.own_n), channel_id=1, source_target_pairs={{0,1},{1,2},{2,3},{3,4},{4,5},{5,6},{6,7},{8,9},{9,10},{10,11},{11... | collective-permute-start | bytes 258056 | tf_op jit(solution)/shard_map/ppermute | solution.py:616
  23.2 1.9 %collective-permute-start.3 = (f32[40,384]{1,0:T(8,128)S(1)}, f32[40,384]{1,0:T(8,128)S(1)}, u32[]{:S(2)}, u32[]{:S(2)}) collective-permute-start(f32[40,384]{1,0:T(8,128)S(1)} %get-tuple-element.29.own_s), channel_id=1, source_target_pairs={{1,0},{2,1},{3,2},{4,3},{5,4},{6,5},{7,6},{9,8},{10,9},{11,10},{12... | collective-permute-start | bytes 184328 | tf_op jit(solution)/shard_map/ppermute | solution.py:617
  25.1 3.1 %edges.1.partial = f32[12,120,360]{2,1,0:T(8,128)} custom-call(f32[120,128]{1,0:T(8,128)S(1)} %get-tuple-element.32.flux_e, f32[120,128]{1,0:T(8,128)S(1)} %get-tuple-element.33.flux_w, f32[12,120,360]{2,1,0:T(8,128)} %get-tuple-element.34.src), custom_call_target="tpu_custom_call", output_to_operand_aliasing={{}: (2, {})} | custom-call | tf_op jit(solution)/shard_map/edges/pallas_call | solution.py:590
  28.2 0.5 collective-permute-done.3.from_n
  28.7 0.0 collective-permute-done.2.from_s
  28.8 6.5 %basis.1 = (f32[9,18,8,384]{3,2,1,0:T(8,128)S(1)}, f32[18,8,384]{2,1,0:T(8,128)S(1)}, f32[128,128]{1,0:T(8,128)S(1)}, f32[12,120,360]{2,1,0:T(8,128)}) custom-call(f32[56,384]{1,0:T(8,128)S(1)} %collective-permute-done.2.from_s, f32[40,384]{1,0:T(8,128)S(1)} %collective-permute-done.3.from_n, ...), custom_call_target="tpu_custom_call", output_to_operand_aliasing={{3}: (6, {})} | custom-call | tf_op jit(solution)/shard_map/basis/pallas_call | solution.py:467
  35.3 18.6 %all_to_all.11 = f32[128,1,128]{2,1,0:T(1,128)S(1)} all-to-all(f32[128,1,128]{2,1,0:T(1,128)S(1)} %bitcast.5), channel_id=1, replica_groups=mesh['gx'=16,'gy'=8] {'gx','gy'}, dimensions={0} | all-to-all | bytes 131072 | tf_op jit(solution)/shard_map/all_to_all | solution.py:622
  53.9 2.7 %finish.1 = (f32[120,360]{1,0:T(8,128)}, f32[120,360]{1,0:T(8,128)}) custom-call(f32[128,128]{1,0:T(8,128)S(1)} %bitcast.4, f32[9,18,8,384]{3,2,1,0:T(8,128)S(1)} %get-tuple-element.37.basis, f32[18,8,384]{2,1,0:T(8,128)S(1)} %get-tuple-element.38.diag), custom_call_target="tpu_custom_call" | custom-call | tf_op jit(solution)/shard_map/finish/pallas_call | solution.py:551
Async XLA Ops:
  9.0 7.4 %collective-permute-start = (f32[120,128]{1,0:T(8,128)S(1)}, f32[120,128]{1,0:T(8,128)S(1)}, u32[]{:S(2)}, u32[]{:S(2)}) collective-permute-start(f32[120,128]{1,0:T(8,128)S(1)} %get-tuple-element.22.own_e), channel_id=1, source_target_pairs={{0,8},{8,16},{16,24},{24,32},{32,40},{40,48},{48,56},{56,64},{64,7... | collective-permute-start | bytes 184328 | tf_op jit(solution)/shard_map/ppermute | solution.py:611
  11.1 5.3 %collective-permute-start.1 = (f32[120,128]{1,0:T(8,128)S(1)}, f32[120,128]{1,0:T(8,128)S(1)}, u32[]{:S(2)}, u32[]{:S(2)}) collective-permute-start(f32[120,128]{1,0:T(8,128)S(1)} %get-tuple-element.23.own_w), channel_id=1, source_target_pairs={{8,0},{16,8},{24,16},{32,24},{40,32},{48,40},{56,48},{64,56},{72,6... | collective-permute-start | bytes 184328 | tf_op jit(solution)/shard_map/ppermute | solution.py:612
  18.1 10.7 %collective-permute-start.2 = (f32[56,384]{1,0:T(8,128)S(1)}, f32[56,384]{1,0:T(8,128)S(1)}, u32[]{:S(2)}, u32[]{:S(2)}) collective-permute-start(f32[56,384]{1,0:T(8,128)S(1)} %get-tuple-element.28.own_n), channel_id=1, source_target_pairs={{0,1},{1,2},{2,3},{3,4},{4,5},{5,6},{6,7},{8,9},{9,10},{10,11},{11... | collective-permute-start | bytes 258056 | tf_op jit(solution)/shard_map/ppermute | solution.py:616
  23.2 5.5 %collective-permute-start.3 = (f32[40,384]{1,0:T(8,128)S(1)}, f32[40,384]{1,0:T(8,128)S(1)}, u32[]{:S(2)}, u32[]{:S(2)}) collective-permute-start(f32[40,384]{1,0:T(8,128)S(1)} %get-tuple-element.29.own_s), channel_id=1, source_target_pairs={{1,0},{2,1},{3,2},{4,3},{5,4},{6,5},{7,6},{9,8},{10,9},{11,10},{12... | collective-permute-start | bytes 184328 | tf_op jit(solution)/shard_map/ppermute | solution.py:617

commit v3 on v2

--- a/solution.py
+++ b/solution.py
@@ -81,15 +81,12 @@
 
 def tracer_kernel(
     mask_hbm, kmt_hbm, forcing_hbm, t_hbm, u_hbm, v_hbm,
-    upd_hbm, rhs_ref, lev_ref, msg_e, msg_w, row_n, row_s,
-    t_s, u_s, v_s, o_s, kmt, forcing, mask, min_e, min_n, col, sem_in, sem_out, sem_2d,
+    o_s, rhs_ref, lev_ref, msg_e, msg_w, row_n, row_s,
+    t_s, u_s, v_s, kmt, forcing, mask, min_e, min_n, col, drop, sem_in, sem_2d,
 ):
     def load(i, k):
         src, dst = ((t_hbm, t_s), (u_hbm, u_s), (v_hbm, v_s))[i]
         return pltpu.make_async_copy(src.at[k], dst.at[k], sem_in.at[i, k])
-
-    def store(k):
-        return pltpu.make_async_copy(o_s.at[k], upd_hbm.at[k], sem_out.at[k])
 
     load_mask = pltpu.make_async_copy(mask_hbm, mask, sem_2d.at[0])
     load_kmt = pltpu.make_async_copy(kmt_hbm, kmt, sem_2d.at[1])
@@ -98,8 +95,8 @@
     load_kmt.start()
     for k in range(KL):
         for i in range(3):
-            load(i, k).start()
-    load_forcing.start()
+            load(i, k).start(priority=0 if k < 4 else 1)
+    load_forcing.start(priority=1)
 
     lane = lanes((8, LW))
     row = rows((8, LW))
@@ -122,25 +119,18 @@
             north = jnp.where(row == 7, 0.0, roll(lev, -1, 0))
         min_e[here, :] = jnp.minimum(lev, roll(lev, -1, 1))
         min_n[here, :] = jnp.minimum(lev, north)
-        col[here, :] = jnp.zeros((8, LW), F32)
     row_n[...] = jnp.zeros((32, LW), F32)
     row_s[...] = jnp.zeros((16, LW), F32)
 
     load(0, 0).wait()
     row360 = rows((8, W))
 
-    def level(k, carry):
-        above = jnp.minimum(k + 1, KL - 1)
-        below = jnp.maximum(k - 1, 0)
-
-        @pl.when(k < KL - 1)
-        def _():
-            load(0, above).wait()
-
+    for k in range(KL):
+        if k + 1 < KL:
+            load(0, k + 1).wait()
         load(1, k).wait()
         load(2, k).wait()
-        kf = k.astype(F32)
-        thick = thickness(kf)
+        kf = float(k)
         f_low = jnp.zeros((8, W), F32)
         t = t_s[k, 0:8, :]
         t_turned = roll(t, -1, 0)
@@ -154,29 +144,32 @@
                 ahead = ahead_turned = None
                 t_n = t_turned
             t_e = roll(widen(t, LW), -1, 1)[:, :W]
-            lev = lev_ref[here, :W]
-            f_e = GRAD * (t_e - t) - (ADV * u_s[k, here, :]) * (t + t_e)
-            f_n = GRAD * (t_n - t) - (ADV * v_s[k, here, :]) * (t + t_n)
+            f_e = (t_e - t) - (ADV / GRAD * u_s[k, here, :]) * (t + t_e)
+            f_n = (t_n - t) - (ADV / GRAD * v_s[k, here, :]) * (t + t_n)
             f_e = jnp.where(min_e[here, :W] > kf, f_e, 0.0)
             f_n = jnp.where(min_n[here, :W] > kf, f_n, 0.0)
             f_w = roll(widen(f_e, LW), 1, 1)[:, :W]
             f_turned = roll(f_n, 1, 0)
             f_s = jnp.where(row360 == 0, f_low, f_turned)
             f_low = f_turned
-            wet = lev > kf
-            up = jnp.where(lev > kf + 1.0, t_s[above, here, :] - t, 0.0)
-            down = jnp.where(wet, t - t_s[below, here, :], 0.0)
-            updated = t + ((f_e - f_w) + (f_n - f_s) + VERT * (up - down))
+            lev = lev_ref[here, :W]
+            gain = (f_e - f_w) + (f_n - f_s)
+            if k + 1 < KL:
+                step = VERT / GRAD * (t_s[k + 1, here, :] - t)
+                step = jnp.where(lev > kf + 1.0, step, 0.0)
+                gain = gain + step
+            if k > 0:
+                gain = gain - drop[here, :W]
+            if k + 1 < KL:
+                drop[here, :W] = step
+            updated = t + GRAD * gain
             o_s[k, here, :] = updated
-            col[here, :W] += jnp.where(wet, thick * updated, 0.0)
+            share = jnp.where(lev > kf, thickness(kf) * updated, 0.0)
+            col[here, :W] = share if k == 0 else col[here, :W] + share
             t, t_turned = ahead, ahead_turned
-        store(k).start()
-        row_s[pl.ds(k, 1), :] = widen(t_s[k, 0:1, :], LW)
-        row_n[pl.ds(k, 1), :] = widen(t_s[k, H - 1 : H, :], LW)
-        row_n[pl.ds(16 + k, 1), :] = widen(v_s[k, H - 1 : H, :], LW)
-        return carry
-
-    lax.fori_loop(0, KL, level, 0)
+        row_s[k : k + 1, :] = widen(t_s[k, 0:1, :], LW)
+        row_n[k : k + 1, :] = widen(t_s[k, H - 1 : H, :], LW)
+        row_n[16 + k : 17 + k, :] = widen(v_s[k, H - 1 : H, :], LW)
 
     load_forcing.wait()
     lane = lanes((8, 128))
@@ -206,12 +199,6 @@
         msg_e[here, :] = east
         msg_w[here, :] = west
 
-    def drain(k, carry):
-        store(k).wait()
-        return carry
-
-    lax.fori_loop(0, KL, drain, 0)
-
 
 def tracer_part(mask, kmt, forcing, tracer, east, north):
     vmem = pl.BlockSpec(memory_space=pltpu.VMEM)
@@ -229,13 +216,12 @@
             shape((16, LW), F32),
         ],
         in_specs=[hbm] * 6,
-        out_specs=[hbm] + [vmem] * 6,
-        scratch_shapes=[pltpu.VMEM((KL, H, W), F32)] * 4
+        out_specs=[vmem] * 7,
+        scratch_shapes=[pltpu.VMEM((KL, H, W), F32)] * 3
         + [pltpu.VMEM((H, W), jnp.int32), pltpu.VMEM((H, W), F32), pltpu.SMEM(mask.shape, jnp.int32)]
-        + [pltpu.VMEM((H, LW), F32)] * 3
+        + [pltpu.VMEM((H, LW), F32)] * 4
         + [
             pltpu.SemaphoreType.DMA((3, KL)),
-            pltpu.SemaphoreType.DMA((KL,)),
             pltpu.SemaphoreType.DMA((3,)),
         ],
         compiler_params=pltpu.CompilerParams(vmem_limit_bytes=VMEM_LIMIT),
@@ -246,25 +232,39 @@
 def sides_kernel(
     from_w, from_e, own_e, own_w, rhs_ref, lev_ref, row_n, row_s,
     rhs_x, lev_x, msg_n, msg_s, flux_e, flux_w,
+    sum_e, sum_w,
 ):
-    lane = lanes((8, 128))
+    from_lane = rows((128, 128))
+
+    def spread(x, first, count, precision):
+        chosen = (from_lane >= first) & (from_lane < first + count)
+        return jnp.dot(
+            x, jnp.where(chosen, 1.0, 0.0), precision=precision, preferred_element_type=F32
+        )
+
+    def level_at(ref, at):
+        return spread(ref[...], at, 1, lax.Precision.DEFAULT)
+
+    lane = lanes((H, 128))
     kf = (lane - TR0).astype(F32)
     inside = (lane >= TR0) & (lane < TR0 + KL)
     weight = ROOT * thickness(kf)
+    lev_w = jnp.minimum(level_at(from_w, LEV0 + 8), level_at(own_w, LEV0))
+    lev_e = jnp.minimum(level_at(from_e, LEV0), level_at(own_e, LEV0 + 8))
+    mw, me, mine_w, mine_e = from_w[...], from_e[...], own_w[...], own_e[...]
+    f_w = GRAD * (mine_w - mw) - (ADV * roll(mw, TR0 - VE0, 1)) * (mine_w + mw)
+    f_e = GRAD * (me - mine_e) - (ADV * roll(mine_e, TR0 - VE0, 1)) * (me + mine_e)
+    f_w = jnp.where(inside & (lev_w > kf), f_w, 0.0)
+    f_e = jnp.where(inside & (lev_e > kf), f_e, 0.0)
+    flux_w[...] = f_w
+    flux_e[...] = f_e
+    sum_w[...] = spread(weight * f_w, TR0, KL, lax.Precision.HIGHEST)
+    sum_e[...] = spread(weight * f_e, TR0, KL, lax.Precision.HIGHEST)
+    lane = lanes((8, 128))
     for r in range(0, H, 8):
         here = slice(r, r + 8)
         mw, me = from_w[here, :], from_e[here, :]
-        mine_e, mine_w = own_e[here, :], own_w[here, :]
-        lev0 = jnp.minimum(mw[:, LEV0 + 8 : LEV0 + 9], mine_w[:, LEV0 : LEV0 + 1])
-        lev1 = jnp.minimum(me[:, LEV0 : LEV0 + 1], mine_e[:, LEV0 + 8 : LEV0 + 9])
-        f_w = GRAD * (mine_w - mw) - (ADV * roll(mw, TR0 - VE0, 1)) * (mine_w + mw)
-        f_e = GRAD * (me - mine_e) - (ADV * roll(mine_e, TR0 - VE0, 1)) * (me + mine_e)
-        f_w = jnp.where(inside & (lev0 > kf), f_w, 0.0)
-        f_e = jnp.where(inside & (lev1 > kf), f_e, 0.0)
-        flux_w[here, :] = f_w
-        flux_e[here, :] = f_e
-        c_w = jnp.sum(weight * f_w, axis=1, keepdims=True)
-        c_e = jnp.sum(weight * f_e, axis=1, keepdims=True)
+        c_w, c_e = sum_w[here, :], sum_e[here, :]
         rhs_x[here, :128] = rhs_ref[here, :128] - jnp.where(lane == 0, c_w, 0.0)
         rhs_x[here, 128:256] = rhs_ref[here, 128:256]
         last = rhs_ref[here, 256:]
@@ -309,6 +309,7 @@
         ],
         in_specs=[vmem] * 8,
         out_specs=[vmem] * 6,
+        scratch_shapes=[pltpu.VMEM((H, 128), F32)] * 2,
         compiler_params=pltpu.CompilerParams(vmem_limit_bytes=VMEM_LIMIT),
         name="sides",
     )(from_w, from_e, own_e, own_w, rhs, lev, row_n, row_s)
@@ -430,12 +431,8 @@
             even = even + scaled * c
             odd = odd + scaled * value
             c_s, c = c, c_n
-        parts[pl.ds(2 * k - 2, 1), :] = fold(even)
-        parts[pl.ds(2 * k - 1, 1), :] = fold(odd)
-
-    def later_step(k, carry):
-        step(k, k - 2)
-        return carry
+        parts[2 * k - 2 : 2 * k - 1, :] = fold(even)
+        parts[2 * k - 1 : 2 * k, :] = fold(odd)
 
     step(1, None)
     row360 = rows((8, W))
@@ -448,7 +445,8 @@
         slab_s[k] = slab_s[k] - at_s
     for store in stores:
         store.start()
-    lax.fori_loop(2, ITERS + 1, later_step, 0)
+    for k in range(2, ITERS + 1):
+        step(k, k - 2)
 
     total = jnp.sum(parts[...], axis=1, keepdims=True)
     prow = rows((24, 128))
@@ -486,59 +484,84 @@
 
 
 def polynomials(gathered):
-    sums = jnp.sum(gathered, axis=0, keepdims=True)
-    lane = lanes((1, 128))
-    alone = sums[:, 64:65]
-    distance = jnp.minimum(lane, 128 - lane)
-    odd = lax.rem(lane, 2) == 1
-    base = jnp.where(odd, sums[:, 1:2], sums[:, 0:1])
-    moments = jnp.where(distance < 2, sums, jnp.where(distance < 16, 2.0 * sums - base, 0.0))
-    row = rows((8, 128))
-    lane = lanes((8, 128))
-    quarter = lax.rem(lane, 4)
-    origin = jnp.where(quarter == 0, alone, jnp.where(quarter == 2, -alone, 0.0))
-    now = jnp.where(row == 0, moments, 0.0)
-    now = jnp.where((row == 1) & (lane == 0), 2.0, now)
-    now = jnp.where(row == 3, 1.0, now)
-    now = jnp.where(row == 4, origin, now)
-    before = jnp.zeros((8, 128), F32)
-    corner = (row == 2) & (lane == 0)
+    sums = jnp.broadcast_to(jnp.sum(gathered, axis=0, keepdims=True), (8, 128))
+
+    def pick(lane):
+        return jnp.broadcast_to(sums[:, lane : lane + 1], (8, 128))
+
+    moments = [pick(j) for j in range(2 * ITERS)]
+    alone = pick(64)
+    now = [x if j < 2 else 2.0 * x - moments[j % 2] for j, x in enumerate(moments)]
+    before = [0.0] * len(now)
+    one = jnp.ones((8, 128), F32)
+    rest, rest_before = [one], []
+    lift, lift_before = [], []
+    at0, at0_before = alone, 0.0
+    at1, at1_before = one, 0.0
+
+    def coefficient(p, j):
+        return p[j] if 0 <= j < len(p) else None
+
+    def total(terms):
+        terms = [x for x in terms if x is not None]
+        return sum(terms[1:], terms[0]) if terms else jnp.zeros((8, 128), F32)
+
+    def advance(p, p_before, a, b, count, constant=None):
+        out = []
+        for j in range(count):
+            terms = [constant if j == 0 else None]
+            below, above = coefficient(p, j - 1), coefficient(p, j + 1)
+            if below is not None:
+                terms.append(below if j == 1 else 0.5 * below)
+            if above is not None:
+                terms.append(0.5 * above)
+            if coefficient(p, j) is not None:
+                terms.append(-(a * p[j]))
+            if coefficient(p_before, j) is not None:
+                terms.append(-(b * p_before[j]))
+            out.append(total(terms))
+        return out
+
+    def lone_part(j):
+        return (at0, None, -at0, None)[j % 4]
+
     last_inv = last_ratio = None
     for k in range(ITERS):
-        both = now[0:1, :] + now[4:5, :]
-        size = both[:, k : k + 1]
+        size = total([now[k], lone_part(k)])
+        cross = total([now[k + 1], lone_part(k + 1)])
         inv = 1.0 / size
-        ratio = both[:, k + 1 : k + 2] * inv * (1.0 if k == 0 else 0.5)
-        image = 0.5 * (roll(now, 1, 1) + roll(now, -1, 1))
-        image = image + jnp.where(corner, 2.0 * now[3:4, 0:1], 0.0)
+        ratio = cross * inv * (1.0 if k == 0 else 0.5)
         if k == 0:
-            after = image - ratio * now
+            a, b = ratio, jnp.zeros((8, 128), F32)
         else:
-            shrink = size * last_inv * (1.0 if k == 1 else 0.5)
-            after = image - (ratio - last_ratio) * now - shrink * before
-        last_inv = inv
-        last_ratio = ratio
+            a, b = ratio - last_ratio, size * last_inv * (1.0 if k == 1 else 0.5)
+        last_inv, last_ratio = inv, ratio
+        after = [None] * len(now)
+        for j in range(k + 1, 2 * ITERS - 1 - k):
+            after[j] = 0.5 * (now[j - 1] + now[j + 1]) - a * now[j] - b * before[j]
         before, now = now, after
-    scale = 1.0 / now[3:4, 0:1]
-    half = jnp.where(lanes((1, 128)) == 0, 0.5, 1.0)
-    return now[2:3, :] * half * scale, now[1:2, :] * half * scale
+        lift, lift_before = advance(lift, lift_before, a, b, k + 1, at1), lift
+        rest, rest_before = advance(rest, rest_before, a, b, k + 2), rest
+        at0, at0_before = -(a * at0) - b * at0_before, at0
+        at1, at1_before = (1.0 - a) * at1 - b * at1_before, at1
+    scale = 1.0 / at1
+    return [x * scale for x in lift], [x * scale for x in rest]
 
 
 def finish_kernel(gathered, basis, diag, sea, residual, sea_t, residual_t):
     lift, rest = polynomials(gathered[...])
-    lift = [lift[:, j : j + 1] for j in range(ITERS)]
-    rest = [rest[:, j : j + 1] for j in range(ITERS + 1)]
     for i in range(EB):
-        c = basis[0, i]
-        a, b = lift[0] * c, rest[0] * c
-        for j in range(1, ITERS + 1):
-            c = basis[j, i]
-            b = b + rest[j] * c
-            if j < ITERS:
-                a = a + lift[j] * c
-        b = diag[i] * b
-        put_strided(sea_t, i, EB, a)
-        put_strided(residual_t, i, EB, b)
+        for j in range(3):
+            here = slice(128 * j, 128 * j + 128)
+            c = basis[0, i, :, here]
+            a, b = lift[0] * c, rest[0] * c
+            for k in range(1, ITERS + 1):
+                c = basis[k, i, :, here]
+                b = b + rest[k] * c
+                if k < ITERS:
+                    a = a + lift[k] * c
+            sea_t[j, pl.ds(i, 8, EB), :] = a
+            residual_t[j, pl.ds(i, 8, EB), :] = diag[i, :, here] * b
     for out, by_tile in ((sea, sea_t), (residual, residual_t)):
         out[:, 0:128] = by_tile[0, :H, :]
         out[:, 128:256] = by_tile[1, :H, :]
@@ -559,26 +582,21 @@
     )(gathered, basis, diag)
 
 
-def edges_kernel(flux_e, flux_w, src, dst, level, sem_in, sem_out):
-    def load(k):
-        return pltpu.make_async_copy(src.at[k], level.at[k], sem_in.at[k])
-
+def edges_kernel(partial, flux_e, flux_w, dst, level, sem):
     def store(k):
-        return pltpu.make_async_copy(level.at[k], dst.at[k], sem_out.at[k])
-
-    for k in range(KL):
-        load(k).start()
+        return pltpu.make_async_copy(level.at[k], dst.at[k], sem.at[k])
+
     lane = lanes((8, 128))
     lane_e = lanes((8, W - 256))
     for k in range(KL):
-        load(k).wait()
         for r in range(0, H, 8):
             here = slice(r, r + 8)
             at_w = jnp.where(lane == 0, roll(flux_w[here, :], -TR0 - k, 1), 0.0)
             at_e = roll(flux_e[here, :], W - 257 - TR0 - k, 1)[:, : W - 256]
             at_e = jnp.where(lane_e == W - 257, at_e, 0.0)
-            level[k, here, :128] = level[k, here, :128] - at_w
-            level[k, here, 256:W] = level[k, here, 256:W] + at_e
+            level[k, here, :128] = partial[k, here, :128] - at_w
+            level[k, here, 128:256] = partial[k, here, 128:256]
+            level[k, here, 256:W] = partial[k, here, 256:W] + at_e
         store(k).start()
     for k in range(KL):
         store(k).wait()
@@ -590,17 +608,12 @@
     return pl.pallas_call(
         edges_kernel,
         out_shape=jax.ShapeDtypeStruct((KL, H, W), F32),
-        in_specs=[vmem, vmem, hbm],
+        in_specs=[vmem] * 3,
         out_specs=hbm,
-        input_output_aliases={2: 0},
-        scratch_shapes=[
-            pltpu.VMEM((KL, H, W), F32),
-            pltpu.SemaphoreType.DMA((KL,)),
-            pltpu.SemaphoreType.DMA((KL,)),
-        ],
+        scratch_shapes=[pltpu.VMEM((KL, H, W), F32), pltpu.SemaphoreType.DMA((KL,))],
         compiler_params=pltpu.CompilerParams(vmem_limit_bytes=VMEM_LIMIT),
         name="edges",
-    )(flux_e, flux_w, partial)
+    )(partial, flux_e, flux_w)
 
 
 def shards(tracer, east_velocity, north_velocity, kmt, block_mask, surface_forcing):

time: 56.8 us -> 48.9 us (0.86)
  Pallas kernels: 22.3 us -> 12.9 us
  waiting for transfers between devices: 2.07 us -> 3.59 us
    pallas_call x1, Pallas kernels: 6.51 us -> 2.95 us  [basis_part(): pl.pallas_call(basis_kernel, out_shape=[shape((ITERS + 1, EB, 8, LW), F32...]
    pallas_call x1, Pallas kernels: 8.37 us -> 6.67 us  [tracer_part(): pl.pallas_call(tracer_kernel, out_shape=[shape((KL, H, W), F32), shape((H...]
    ppermute x1, waiting for transfers between devices: 0.54 us -> 2.06 us  [shards(): from_n = lax.ppermute(msg_s, 'gy', [(i + 1, i) for i in range(ny - 1)])]
    pallas_call x1, Pallas kernels: 3.07 us -> 1.55 us  [edges_part(): pl.pallas_call(edges_kernel, out_shape=jax.ShapeDtypeStruct((KL, H, W), F...]
    pallas_call x1, Pallas kernels: 2.73 us -> 1.24 us  [finish_part(): pl.pallas_call(finish_kernel, out_shape=[shape((H, W), F32), shape((H, W)...]
    pallas_call x1, Pallas kernels: 1.63 us -> 0.5 us  [sides_part(): pl.pallas_call(sides_kernel, out_shape=[shape((H, LW), F32), shape((H, LW...]
  transfers between devices with their start and end apart: 4 -> 4, of which waited for: 2 -> 2; matrix products, arithmetic and copies ran while one was open for 0% -> 0% of each run, Pallas kernels for 5% -> 3%
where the time goes in v3:
time: 48.9 us; the launch traced here: 48.7 us
  blocking collectives  18.6 us (38%)
  Pallas kernels  12.9 us (26%)
  starting transfers between devices  12.9 us (26%)
  waiting for transfers between devices  3.59 us (7%)
  between operations  0.68 us (1%)
    all_to_all x1, blocking collectives, shards(): gathered = lax.all_to_all(sums, ('gx', 'gy'), 0, 0, tiled=True)  18.6 us
    pallas_call x1, Pallas kernels, tracer_part(): pl.pallas_call(tracer_kernel, out_shape=[shape((KL, H, W), F32), shape((H...  6.67 us
    ppermute x1, starting transfers between devices, shards(): from_s = lax.ppermute(msg_n, 'gy', [(i, i + 1) for i in range(ny - 1)])  5.11 us
    ppermute x1, starting transfers between devices, shards(): from_e = lax.ppermute(msg_w, 'gx', [((i + 1) % nx, i) for i in range(nx)])  3.8 us
    pallas_call x1, Pallas kernels, basis_part(): pl.pallas_call(basis_kernel, out_shape=[shape((ITERS + 1, EB, 8, LW), F32...  2.95 us
    ppermute x1, starting transfers between devices, shards(): from_w = lax.ppermute(msg_e, 'gx', [(i, (i + 1) % nx) for i in range(nx)])  2.11 us
    ppermute x1, waiting for transfers between devices, shards(): from_n = lax.ppermute(msg_s, 'gy', [(i + 1, i) for i in range(ny - 1)])  2.06 us
    ppermute x1, starting transfers between devices, shards(): from_n = lax.ppermute(msg_s, 'gy', [(i + 1, i) for i in range(ny - 1)])  1.92 us
  transfers between devices with their start and end apart: 4, of which 2 were waited for; matrix products, arithmetic and copies ran while one was open for 0% of the time, Pallas kernels for 3%

profile of v3, /device:TPU:1, one launch (start us, length us, event | category | flops | bytes accessed | tf_op | source)
XLA Modules:
  0.0 48.7 jit_solution(7816407418702410010)
XLA Ops:
  0.6 6.7 %tracer.1 = (f32[12,120,360]{2,1,0:T(8,128)S(1)}, f32[120,384]{1,0:T(8,128)S(1)}, f32[120,384]{1,0:T(8,128)S(1)}, f32[120,128]{1,0:T(8,128)S(1)}, f32[120,128]{1...) custom-call(s32[2,4]{1,0:T(2,128)} %mask_hbm.1, s32[120,360]{1,0:T(8,128)} %kmt_hbm.1, ...), custom_call_target="tpu_custom_call" | custom-call | tf_op jit(solution)/shard_map/tracer/pallas_call | solution.py:207
  7.3 2.1 %collective-permute-start = (f32[120,128]{1,0:T(8,128)S(1)}, f32[120,128]{1,0:T(8,128)S(1)}, u32[]{:S(2)}, u32[]{:S(2)}) collective-permute-start(f32[120,128]{1,0:T(8,128)S(1)} %get-tuple-element.22.own_e), channel_id=1, source_target_pairs={{0,8},{8,16},{16,24},{24,32},{32,40},{40,48},{48,56},{56,64},{64,7... | collective-permute-start | bytes 184328 | tf_op jit(solution)/shard_map/ppermute | solution.py:624
  9.4 3.8 %collective-permute-start.1 = (f32[120,128]{1,0:T(8,128)S(1)}, f32[120,128]{1,0:T(8,128)S(1)}, u32[]{:S(2)}, u32[]{:S(2)}) collective-permute-start(f32[120,128]{1,0:T(8,128)S(1)} %get-tuple-element.23.own_w), channel_id=1, source_target_pairs={{8,0},{16,8},{24,16},{32,24},{40,32},{48,40},{56,48},{64,56},{72,6... | collective-permute-start | bytes 184328 | tf_op jit(solution)/shard_map/ppermute | solution.py:625
  13.2 1.5 %collective-permute-done.from_w = f32[120,128]{1,0:T(8,128)S(1)} collective-permute-done((f32[120,128]{1,0:T(8,128)S(1)}, f32[120,128]{1,0:T(8,128)S(1)}, u32[]{:S(2)}, u32[]{:S(2)}) %collective-permute-start) | collective-permute-done | bytes 61472 | tf_op jit(solution)/shard_map/ppermute | solution.py:624
  14.8 0.0 collective-permute-done.1.from_e
  14.8 0.5 %sides.1 = (f32[120,384]{1,0:T(8,128)S(1)}, f32[120,384]{1,0:T(8,128)S(1)}, f32[56,384]{1,0:T(8,128)S(1)}, f32[40,384]{1,0:T(8,128)S(1)}, f32[120,128]{1,0:T(8,128)S(1)}, /*index=5*/f32[120,128]{1,0:T(8,128)S(1)}) custom-call(f32[120,128]{1,0:T(8,128)S(1)} %collective-permute-done.from_w, f32[120,128]{1,0:T(8,128)S(1)} %collective-permute-done.1.from_e, ...), custom_call_target="tpu_custom_call" | custom-call | tf_op jit(solution)/shard_map/sides/pallas_call | solution.py:300
  15.3 5.1 %collective-permute-start.2 = (f32[56,384]{1,0:T(8,128)S(1)}, f32[56,384]{1,0:T(8,128)S(1)}, u32[]{:S(2)}, u32[]{:S(2)}) collective-permute-start(f32[56,384]{1,0:T(8,128)S(1)} %get-tuple-element.28.own_n), channel_id=1, source_target_pairs={{0,1},{1,2},{2,3},{3,4},{4,5},{5,6},{6,7},{8,9},{9,10},{10,11},{11... | collective-permute-start | bytes 258056 | tf_op jit(solution)/shard_map/ppermute | solution.py:629
  20.4 1.9 %collective-permute-start.3 = (f32[40,384]{1,0:T(8,128)S(1)}, f32[40,384]{1,0:T(8,128)S(1)}, u32[]{:S(2)}, u32[]{:S(2)}) collective-permute-start(f32[40,384]{1,0:T(8,128)S(1)} %get-tuple-element.29.own_s), channel_id=1, source_target_pairs={{1,0},{2,1},{3,2},{4,3},{5,4},{6,5},{7,6},{9,8},{10,9},{11,10},{12... | collective-permute-start | bytes 184328 | tf_op jit(solution)/shard_map/ppermute | solution.py:630
  22.3 1.5 %edges.1.partial = f32[12,120,360]{2,1,0:T(8,128)} custom-call(f32[12,120,360]{2,1,0:T(8,128)S(1)} %get-tuple-element.32.partial, f32[120,128]{1,0:T(8,128)S(1)} %get-tuple-element.33.flux_e, f32[120,128]{1,0:T(8,128)S(1)} %get-tuple-element.34.flux_w), custom_call_target="tpu_custom_call" | custom-call | tf_op jit(solution)/shard_map/edges/pallas_call | solution.py:608
  23.9 2.1 %collective-permute-done.3.from_n = f32[40,384]{1,0:T(8,128)S(1)} collective-permute-done((f32[40,384]{1,0:T(8,128)S(1)}, f32[40,384]{1,0:T(8,128)S(1)}, u32[]{:S(2)}, u32[]{:S(2)}) %collective-permute-start.3) | collective-permute-done | bytes 61472 | tf_op jit(solution)/shard_map/ppermute | solution.py:630
  25.9 0.0 collective-permute-done.2.from_s
  25.9 3.0 %basis.1 = (f32[9,18,8,384]{3,2,1,0:T(8,128)S(1)}, f32[18,8,384]{2,1,0:T(8,128)S(1)}, f32[128,128]{1,0:T(8,128)S(1)}, f32[12,120,360]{2,1,0:T(8,128)}) custom-call(f32[56,384]{1,0:T(8,128)S(1)} %collective-permute-done.2.from_s, f32[40,384]{1,0:T(8,128)S(1)} %collective-permute-done.3.from_n, ...), custom_call_target="tpu_custom_call", output_to_operand_aliasing={{3}: (6, {})} | custom-call | tf_op jit(solution)/shard_map/basis/pallas_call | solution.py:465
  28.9 18.6 %all_to_all.11 = f32[128,1,128]{2,1,0:T(1,128)S(1)} all-to-all(f32[128,1,128]{2,1,0:T(1,128)S(1)} %bitcast.5), channel_id=1, replica_groups=mesh['gx'=16,'gy'=8] {'gx','gy'}, dimensions={0} | all-to-all | bytes 131072 | tf_op jit(solution)/shard_map/all_to_all | solution.py:635
  47.5 1.2 %finish.1 = (f32[120,360]{1,0:T(8,128)}, f32[120,360]{1,0:T(8,128)}) custom-call(f32[128,128]{1,0:T(8,128)S(1)} %bitcast.4, f32[9,18,8,384]{3,2,1,0:T(8,128)S(1)} %get-tuple-element.37.basis, f32[18,8,384]{2,1,0:T(8,128)S(1)} %get-tuple-element.38.diag), custom_call_target="tpu_custom_call" | custom-call | tf_op jit(solution)/shard_map/finish/pallas_call | solution.py:574
Async XLA Ops:
  7.3 7.4 %collective-permute-start = (f32[120,128]{1,0:T(8,128)S(1)}, f32[120,128]{1,0:T(8,128)S(1)}, u32[]{:S(2)}, u32[]{:S(2)}) collective-permute-start(f32[120,128]{1,0:T(8,128)S(1)} %get-tuple-element.22.own_e), channel_id=1, source_target_pairs={{0,8},{8,16},{16,24},{24,32},{32,40},{40,48},{48,56},{56,64},{64,7... | collective-permute-start | bytes 184328 | tf_op jit(solution)/shard_map/ppermute | solution.py:624
  9.4 5.3 %collective-permute-start.1 = (f32[120,128]{1,0:T(8,128)S(1)}, f32[120,128]{1,0:T(8,128)S(1)}, u32[]{:S(2)}, u32[]{:S(2)}) collective-permute-start(f32[120,128]{1,0:T(8,128)S(1)} %get-tuple-element.23.own_w), channel_id=1, source_target_pairs={{8,0},{16,8},{24,16},{32,24},{40,32},{48,40},{56,48},{64,56},{72,6... | collective-permute-start | bytes 184328 | tf_op jit(solution)/shard_map/ppermute | solution.py:625
  15.3 10.7 %collective-permute-start.2 = (f32[56,384]{1,0:T(8,128)S(1)}, f32[56,384]{1,0:T(8,128)S(1)}, u32[]{:S(2)}, u32[]{:S(2)}) collective-permute-start(f32[56,384]{1,0:T(8,128)S(1)} %get-tuple-element.28.own_n), channel_id=1, source_target_pairs={{0,1},{1,2},{2,3},{3,4},{4,5},{5,6},{6,7},{8,9},{9,10},{10,11},{11... | collective-permute-start | bytes 258056 | tf_op jit(solution)/shard_map/ppermute | solution.py:629
  20.4 5.5 %collective-permute-start.3 = (f32[40,384]{1,0:T(8,128)S(1)}, f32[40,384]{1,0:T(8,128)S(1)}, u32[]{:S(2)}, u32[]{:S(2)}) collective-permute-start(f32[40,384]{1,0:T(8,128)S(1)} %get-tuple-element.29.own_s), channel_id=1, source_target_pairs={{1,0},{2,1},{3,2},{4,3},{5,4},{6,5},{7,6},{9,8},{10,9},{11,10},{12... | collective-permute-start | bytes 184328 | tf_op jit(solution)/shard_map/ppermute | solution.py:630

commit v4 on v3

--- a/solution.py
+++ b/solution.py
@@ -79,10 +79,61 @@
     return 1.0 + (0.5 / KL) * level
 
 
-def tracer_kernel(
+def tile(ref, j, *at):
+    if ref.shape[-1] == LW or j < 2:
+        return ref[(*at, slice(128 * j, 128 * j + 128))]
+    return widen(ref[(*at, slice(256, W))], 128)
+
+
+def sweep_level(k, j, t_s, u_s, v_s, lev_ref, min_e, min_n, drop, col, put):
+    static = isinstance(k, int)
+    kf = float(k) if static else k.astype(F32)
+    first, last = static and k == 0, static and k == KL - 1
+    above = min(k + 1, KL - 1) if static else jnp.minimum(k + 1, KL - 1)
+    lane = lanes((8, 128))
+    row = rows((8, 128))
+    f_low = jnp.zeros((8, 128), F32)
+    t = tile(t_s, j, k, slice(0, 8))
+    t_turned = roll(t, -1, 0)
+    for r in range(0, H, 8):
+        here = slice(r, r + 8)
+        if r + 8 < H:
+            ahead = tile(t_s, j, k, slice(r + 8, r + 16))
+            ahead_turned = roll(ahead, -1, 0)
+            t_n = jnp.where(row == 7, ahead_turned, t_turned)
+        else:
+            ahead = ahead_turned = None
+            t_n = t_turned
+        t_e = roll(t, -1, 1)
+        f_e = (t_e - t) - (ADV / GRAD * tile(u_s, j, k, here)) * (t + t_e)
+        f_n = (t_n - t) - (ADV / GRAD * tile(v_s, j, k, here)) * (t + t_n)
+        f_e = jnp.where(tile(min_e, j, here) > kf, f_e, 0.0)
+        f_n = jnp.where(tile(min_n, j, here) > kf, f_n, 0.0)
+        f_w = roll(f_e, 1, 1)
+        f_turned = roll(f_n, 1, 0)
+        f_s = jnp.where(row == 0, f_low, f_turned)
+        f_low = f_turned
+        lev = tile(lev_ref, j, here)
+        gain = (f_e - f_w) + (f_n - f_s)
+        if not last:
+            step = VERT / GRAD * (tile(t_s, j, above, here) - t)
+            step = jnp.where(lev > kf + 1.0, step, 0.0)
+            gain = gain + step
+        if not first:
+            gain = gain - tile(drop, j, here)
+        if not last:
+            drop[here, 128 * j : 128 * j + 128] = step
+        updated = t + GRAD * gain
+        put(here, updated)
+        share = jnp.where(lev > kf, thickness(kf) * updated, 0.0)
+        col[here, 128 * j : 128 * j + 128] = share if first else tile(col, j, here) + share
+        t, t_turned = ahead, ahead_turned
+
+
+def outer_kernel(
     mask_hbm, kmt_hbm, forcing_hbm, t_hbm, u_hbm, v_hbm,
-    o_s, rhs_ref, lev_ref, msg_e, msg_w, row_n, row_s,
-    t_s, u_s, v_s, kmt, forcing, mask, min_e, min_n, col, drop, sem_in, sem_2d,
+    t_s, u_s, v_s, forcing, outer, rhs_ref, lev_ref, min_e, min_in, min_n, msg_e, msg_w, row_n, row_s,
+    kmt, mask, col, drop, sem_in, sem_2d,
 ):
     def load(i, k):
         src, dst = ((t_hbm, t_s), (u_hbm, u_s), (v_hbm, v_s))[i]
@@ -110,6 +161,7 @@
             keep = jnp.where(inside, upper, keep)
         lev = widen(kmt[r : r + 8, :], LW) * keep
         lev_ref[r : r + 8, :] = lev.astype(F32)
+    inner = (lane != 127) & (lane != 255)
     for r in range(0, H, 8):
         here = slice(r, r + 8)
         lev = lev_ref[here, :]
@@ -117,56 +169,25 @@
             north = lev_ref[r + 1 : r + 9, :]
         else:
             north = jnp.where(row == 7, 0.0, roll(lev, -1, 0))
-        min_e[here, :] = jnp.minimum(lev, roll(lev, -1, 1))
+        east = jnp.minimum(lev, roll(lev, -1, 1))
+        min_e[here, :] = east
+        min_in[here, :] = jnp.where(inner, east, 0.0)
         min_n[here, :] = jnp.minimum(lev, north)
     row_n[...] = jnp.zeros((32, LW), F32)
     row_s[...] = jnp.zeros((16, LW), F32)
 
     load(0, 0).wait()
-    row360 = rows((8, W))
-
     for k in range(KL):
         if k + 1 < KL:
             load(0, k + 1).wait()
         load(1, k).wait()
         load(2, k).wait()
-        kf = float(k)
-        f_low = jnp.zeros((8, W), F32)
-        t = t_s[k, 0:8, :]
-        t_turned = roll(t, -1, 0)
-        for r in range(0, H, 8):
-            here = slice(r, r + 8)
-            if r + 8 < H:
-                ahead = t_s[k, r + 8 : r + 16, :]
-                ahead_turned = roll(ahead, -1, 0)
-                t_n = jnp.where(row360 == 7, ahead_turned, t_turned)
-            else:
-                ahead = ahead_turned = None
-                t_n = t_turned
-            t_e = roll(widen(t, LW), -1, 1)[:, :W]
-            f_e = (t_e - t) - (ADV / GRAD * u_s[k, here, :]) * (t + t_e)
-            f_n = (t_n - t) - (ADV / GRAD * v_s[k, here, :]) * (t + t_n)
-            f_e = jnp.where(min_e[here, :W] > kf, f_e, 0.0)
-            f_n = jnp.where(min_n[here, :W] > kf, f_n, 0.0)
-            f_w = roll(widen(f_e, LW), 1, 1)[:, :W]
-            f_turned = roll(f_n, 1, 0)
-            f_s = jnp.where(row360 == 0, f_low, f_turned)
-            f_low = f_turned
-            lev = lev_ref[here, :W]
-            gain = (f_e - f_w) + (f_n - f_s)
-            if k + 1 < KL:
-                step = VERT / GRAD * (t_s[k + 1, here, :] - t)
-                step = jnp.where(lev > kf + 1.0, step, 0.0)
-                gain = gain + step
-            if k > 0:
-                gain = gain - drop[here, :W]
-            if k + 1 < KL:
-                drop[here, :W] = step
-            updated = t + GRAD * gain
-            o_s[k, here, :] = updated
-            share = jnp.where(lev > kf, thickness(kf) * updated, 0.0)
-            col[here, :W] = share if k == 0 else col[here, :W] + share
-            t, t_turned = ahead, ahead_turned
+        for j in (0, 2):
+
+            def put(here, updated, k=k, j=j):
+                outer[k, here, 64 * j : 64 * j + 128] = updated
+
+            sweep_level(k, j, t_s, u_s, v_s, lev_ref, min_in, min_n, drop, col, put)
         row_s[k : k + 1, :] = widen(t_s[k, 0:1, :], LW)
         row_n[k : k + 1, :] = widen(t_s[k, H - 1 : H, :], LW)
         row_n[16 + k : 17 + k, :] = widen(v_s[k, H - 1 : H, :], LW)
@@ -175,18 +196,19 @@
     lane = lanes((8, 128))
     for r in range(0, H, 8):
         here = slice(r, r + 8)
-        lev = lev_ref[here, :]
-        rhs = ROOT * col[here, :W] + forcing[here, :]
-        rhs = widen(jnp.where(lev[:, :W] > 0.0, rhs, 0.0), LW)
-        rhs_ref[here, :] = rhs
-        east = jnp.where(lane < LEV0, roll(rhs[:, 256:], 32, 1), roll(lev[:, 256:], LEV0 - 95, 1))
-        west = jnp.where(lane < LEV0, rhs[:, :128], roll(lev[:, :128], LEV0, 1))
+        lev0, lev2 = tile(lev_ref, 0, here), tile(lev_ref, 2, here)
+        rhs0 = jnp.where(lev0 > 0.0, ROOT * tile(col, 0, here) + tile(forcing, 0, here), 0.0)
+        rhs2 = jnp.where(lev2 > 0.0, ROOT * tile(col, 2, here) + tile(forcing, 2, here), 0.0)
+        rhs_ref[here, :128] = rhs0
+        rhs_ref[here, 128:] = rhs2
+        east = jnp.where(lane < LEV0, roll(rhs2, 32, 1), roll(lev2, LEV0 - 95, 1))
+        west = jnp.where(lane < LEV0, rhs0, roll(lev0, LEV0, 1))
         east = jnp.where(lane < TR0, east, 0.0)
         west = jnp.where(lane < TR0, west, 0.0)
         for k in range(KL):
-            t2 = roll(widen(t_s[k, here, 256:W], 128), TR0 + k - 103, 1)
-            u2 = roll(widen(u_s[k, here, 256:W], 128), VE0 + k - 103, 1)
-            t0 = roll(t_s[k, here, :128], TR0 + k, 1)
+            t2 = roll(tile(t_s, 2, k, here), TR0 + k - 103, 1)
+            u2 = roll(tile(u_s, 2, k, here), VE0 + k - 103, 1)
+            t0 = roll(tile(t_s, 0, k, here), TR0 + k, 1)
             east = jnp.where(lane == TR0 + k, t2, east)
             east = jnp.where(lane == VE0 + k, u2, east)
             west = jnp.where(lane == TR0 + k, t0, west)
@@ -200,14 +222,19 @@
         msg_w[here, :] = west
 
 
-def tracer_part(mask, kmt, forcing, tracer, east, north):
+def outer_part(mask, kmt, forcing, tracer, east, north):
     vmem = pl.BlockSpec(memory_space=pltpu.VMEM)
     hbm = pl.BlockSpec(memory_space=pltpu.HBM)
     shape = jax.ShapeDtypeStruct
     return pl.pallas_call(
-        tracer_kernel,
-        out_shape=[
-            shape((KL, H, W), F32),
+        outer_kernel,
+        out_shape=[shape((KL, H, W), F32)] * 3
+        + [
+            shape((H, W), F32),
+            shape((KL, H, 256), F32),
+            shape((H, 256), F32),
+            shape((H, LW), F32),
+            shape((H, LW), F32),
             shape((H, LW), F32),
             shape((H, LW), F32),
             shape((H, 128), F32),
@@ -216,17 +243,74 @@
             shape((16, LW), F32),
         ],
         in_specs=[hbm] * 6,
-        out_specs=[vmem] * 7,
-        scratch_shapes=[pltpu.VMEM((KL, H, W), F32)] * 3
-        + [pltpu.VMEM((H, W), jnp.int32), pltpu.VMEM((H, W), F32), pltpu.SMEM(mask.shape, jnp.int32)]
-        + [pltpu.VMEM((H, LW), F32)] * 4
-        + [
-            pltpu.SemaphoreType.DMA((3, KL)),
-            pltpu.SemaphoreType.DMA((3,)),
-        ],
+        out_specs=[vmem] * 14,
+        scratch_shapes=[pltpu.VMEM((H, W), jnp.int32), pltpu.SMEM(mask.shape, jnp.int32)]
+        + [pltpu.VMEM((H, LW), F32)] * 2
+        + [pltpu.SemaphoreType.DMA((3, KL)), pltpu.SemaphoreType.DMA((3,))],
         compiler_params=pltpu.CompilerParams(vmem_limit_bytes=VMEM_LIMIT),
-        name="tracer",
+        name="outer",
     )(*(pltpu.with_memory_space_constraint(x, pltpu.HBM) for x in (mask, kmt, forcing, tracer, east, north)))
+
+
+def middle_kernel(
+    t_s, u_s, v_s, forcing, outer, rhs_outer, lev_ref, min_e, min_in, min_n,
+    partial, rhs_ref, min_w, col, col_w, col_e, drop,
+):
+    lane = lanes((8, 128))
+    for r in range(0, H, 8):
+        here = slice(r, r + 8)
+        min_w[here, :] = roll(tile(min_e, 0, here), 1, 1)
+        for total in (col_w, col_e):
+            total[here, :] = jnp.zeros((8, 128), F32)
+        for total in (col, drop):
+            total[here, 128:256] = jnp.zeros((8, 128), F32)
+
+    def level(k, carry):
+        kf = k.astype(F32)
+
+        def put(here, updated):
+            t = t_s[k, here, 128:256]
+            t_w = roll(t_s[k, here, :128], 1, 1)
+            u_w = roll(u_s[k, here, :128], 1, 1)
+            t_e = roll(tile(t_s, 2, k, here), -1, 1)
+            f_w = (t - t_w) - (ADV / GRAD * u_w) * (t_w + t)
+            f_e = (t_e - t) - (ADV / GRAD * u_s[k, here, 128:256]) * (t + t_e)
+            f_w = jnp.where((lane == 0) & (min_w[here, :] > kf), GRAD * f_w, 0.0)
+            f_e = jnp.where((lane == 127) & (tile(min_e, 1, here) > kf), GRAD * f_e, 0.0)
+            col_w[here, :] = col_w[here, :] + thickness(kf) * f_w
+            col_e[here, :] = col_e[here, :] + thickness(kf) * f_e
+            partial[k, here, :128] = outer[k, here, :128] + roll(f_w, -1, 1)
+            partial[k, here, 128:256] = updated + (f_e - f_w)
+            partial[k, here, 256:W] = (outer[k, here, 128:] - roll(f_e, 1, 1))[:, : W - 256]
+
+        sweep_level(k, 1, t_s, u_s, v_s, lev_ref, min_in, min_n, drop, col, put)
+        return carry
+
+    lax.fori_loop(0, KL, level, 0)
+    for r in range(0, H, 8):
+        here = slice(r, r + 8)
+        c_w, c_e = ROOT * col_w[here, :], ROOT * col_e[here, :]
+        rhs = ROOT * tile(col, 1, here) + tile(forcing, 1, here) + (c_e - c_w)
+        rhs_ref[here, :128] = rhs_outer[here, :128] + roll(c_w, -1, 1)
+        rhs_ref[here, 128:256] = jnp.where(tile(lev_ref, 1, here) > 0.0, rhs, 0.0)
+        rhs_ref[here, 256:] = rhs_outer[here, 128:] - roll(c_e, 1, 1)
+
+
+def middle_part(t_s, u_s, v_s, forcing, outer, rhs_outer, lev, min_e, min_in, min_n):
+    vmem = pl.BlockSpec(memory_space=pltpu.VMEM)
+    shape = jax.ShapeDtypeStruct
+    return pl.pallas_call(
+        middle_kernel,
+        out_shape=[shape((KL, H, W), F32), shape((H, LW), F32)],
+        in_specs=[vmem] * 10,
+        out_specs=[vmem] * 2,
+        scratch_shapes=[pltpu.VMEM((H, 128), F32)]
+        + [pltpu.VMEM((H, LW), F32)]
+        + [pltpu.VMEM((H, 128), F32)] * 2
+        + [pltpu.VMEM((H, LW), F32)],
+        compiler_params=pltpu.CompilerParams(vmem_limit_bytes=VMEM_LIMIT),
+        name="middle",
+    )(t_s, u_s, v_s, forcing, outer, rhs_outer, lev, min_e, min_in, min_n)
 
 
 def sides_kernel(
@@ -618,16 +702,17 @@
 
 def shards(tracer, east_velocity, north_velocity, kmt, block_mask, surface_forcing):
     nx, ny = lax.axis_size("gx"), lax.axis_size("gy")
-    partial, rhs, lev, msg_e, msg_w, row_n, row_s = tracer_part(
+    *fields, lev, min_e, min_in, min_n, msg_e, msg_w, row_n, row_s = outer_part(
         block_mask, kmt, surface_forcing, tracer, east_velocity, north_velocity
     )
     from_w = lax.ppermute(msg_e, "gx", [(i, (i + 1) % nx) for i in range(nx)])
     from_e = lax.ppermute(msg_w, "gx", [((i + 1) % nx, i) for i in range(nx)])
+    partial, rhs = middle_part(*fields, lev, min_e, min_in, min_n)
     rhs_x, lev_x, msg_n, msg_s, flux_e, flux_w = sides_part(
         from_w, from_e, msg_e, msg_w, rhs, lev, row_n, row_s
     )
-    from_s = lax.ppermute(msg_n, "gy", [(i, i + 1) for i in range(ny - 1)])
-    from_n = lax.ppermute(msg_s, "gy", [(i + 1, i) for i in range(ny - 1)])
+    from_s = lax.ppermute(msg_n, "gy", [(i, (i + 1) % ny) for i in range(ny)])
+    from_n = lax.ppermute(msg_s, "gy", [((i + 1) % ny, i) for i in range(ny)])
     partial = edges_part(partial, flux_e, flux_w)
     basis, diag, sums, updated = basis_part(
         from_s, from_n, msg_n, msg_s, rhs_x, lev_x, partial, nx * ny

time: 48.9 us -> 43.9 us (0.90)
  starting transfers between devices: 12.9 us -> 8.45 us
  Pallas kernels: 12.9 us -> 14.6 us
  waiting for transfers between devices: 3.59 us -> 2.1 us
  blocking collectives: 18.6 us -> 17.9 us
    ppermute x2, starting transfers between devices: 7.03 us -> 2.54 us  [the longest x1 2.54 us: shards(): from_s = lax.ppermute(msg_n, 'gy', [(i, (i + 1) % ny) for i in range(ny)])]
    pallas_call x1 -> x2, Pallas kernels: 6.67 us -> 8.38 us  [the longest x1 5.56 us: outer_part(): pl.pallas_call(outer_kernel, out_shape=[shape((KL, H, W), F32)] * 3 + [sh...]
    ppermute x1, waiting for transfers between devices: 1.53 us -> 0.01 us  [shards(): from_w = lax.ppermute(msg_e, 'gx', [(i, (i + 1) % nx) for i in range(nx)])]
    all_to_all x1, blocking collectives: 18.6 us -> 17.9 us  [shards(): gathered = lax.all_to_all(sums, ('gx', 'gy'), 0, 0, tiled=True)]
  transfers between devices with their start and end apart: 4 -> 4, of which waited for: 2 -> 1; matrix products, arithmetic and copies ran while one was open for 0% -> 0% of each run, Pallas kernels for 3% -> 10%
where the time goes in v4:
time: 43.9 us; the launch traced here: 43.8 us
  blocking collectives  17.9 us (41%)
  Pallas kernels  14.6 us (33%)
  starting transfers between devices  8.45 us (19%)
  waiting for transfers between devices  2.1 us (5%)
  between operations  0.69 us (2%)
    all_to_all x1, blocking collectives, shards(): gathered = lax.all_to_all(sums, ('gx', 'gy'), 0, 0, tiled=True)  17.9 us
    pallas_call x1, Pallas kernels, outer_part(): pl.pallas_call(outer_kernel, out_shape=[shape((KL, H, W), F32)] * 3 + [sh...  5.56 us
    ppermute x1, starting transfers between devices, shards(): from_e = lax.ppermute(msg_w, 'gx', [((i + 1) % nx, i) for i in range(nx)])  3.8 us
    pallas_call x1, Pallas kernels, basis_part(): pl.pallas_call(basis_kernel, out_shape=[shape((ITERS + 1, EB, 8, LW), F32...  2.95 us
    pallas_call x1, Pallas kernels, middle_part(): pl.pallas_call(middle_kernel, out_shape=[shape((KL, H, W), F32), shape((H...  2.82 us
    ppermute x1, starting transfers between devices, shards(): from_s = lax.ppermute(msg_n, 'gy', [(i, (i + 1) % ny) for i in range(ny)])  2.54 us
    ppermute x1, starting transfers between devices, shards(): from_w = lax.ppermute(msg_e, 'gx', [(i, (i + 1) % nx) for i in range(nx)])  2.11 us
    ppermute x1, waiting for transfers between devices, shards(): from_n = lax.ppermute(msg_s, 'gy', [((i + 1) % ny, i) for i in range(ny)])  2.09 us
  transfers between devices with their start and end apart: 4, of which 1 were waited for; matrix products, arithmetic and copies ran while one was open for 0% of the time, Pallas kernels for 10%

profile of v4, /device:TPU:1, one launch (start us, length us, event | category | flops | bytes accessed | tf_op | source)
XLA Modules:
  0.0 43.8 jit_solution(16332015886178071572)
XLA Ops:
  0.6 5.6 %outer.1 = (f32[12,120,360]{2,1,0:T(8,128)S(1)}, f32[12,120,360]{2,1,0:T(8,128)S(1)}, f32[12,120,360]{2,1,0:T(8,128)S(1)}, f32[120,360]{1,0:T(8,128)S(1)}, f32[1...) custom-call(s32[2,4]{1,0:T(2,128)} %mask_hbm.1, ...), custom_call_target="tpu_custom_call" | custom-call | tf_op jit(solution)/shard_map/outer/pallas_call | solution.py:229
  6.2 2.1 %collective-permute-start = (f32[120,128]{1,0:T(8,128)S(1)}, f32[120,128]{1,0:T(8,128)S(1)}, u32[]{:S(2)}, u32[]{:S(2)}) collective-permute-start(f32[120,128]{1,0:T(8,128)S(1)} %get-tuple-element.31.own_e), channel_id=1, source_target_pairs={{0,8},{8,16},{16,24},{24,32},{32,40},{40,48},{48,56},{56,64},{64,7... | collective-permute-start | bytes 184328 | tf_op jit(solution)/shard_map/ppermute | solution.py:708
  8.3 3.8 %collective-permute-start.1 = (f32[120,128]{1,0:T(8,128)S(1)}, f32[120,128]{1,0:T(8,128)S(1)}, u32[]{:S(2)}, u32[]{:S(2)}) collective-permute-start(f32[120,128]{1,0:T(8,128)S(1)} %get-tuple-element.32.own_w), channel_id=1, source_target_pairs={{8,0},{16,8},{24,16},{32,24},{40,32},{48,40},{56,48},{64,56},{72,6... | collective-permute-start | bytes 184328 | tf_op jit(solution)/shard_map/ppermute | solution.py:709
  12.1 2.8 %middle.1 = (f32[12,120,360]{2,1,0:T(8,128)S(1)}, f32[120,384]{1,0:T(8,128)S(1)}) custom-call(f32[12,120,360]{2,1,0:T(8,128)S(1)} %get-tuple-element.33.t_s, f32[12,120,360]{2,1,0:T(8,128)S(1)} %get-tuple-element.34.u_s, f32[12,120,360]{2,1,0:T(8,128)S(1)} %get-tuple-element.35.v_s, f32[120,360]{1,0:T(8,128)S(1)} %get-tuple-element.36.forcing, ...), custom_call_target="tpu_custom_call" | custom-call | tf_op jit(solution)/shard_map/middle/pallas_call | solution.py:302
  14.9 0.0 collective-permute-done.from_w
  15.0 0.0 collective-permute-done.1.from_e
  15.0 0.5 %sides.1 = (f32[120,384]{1,0:T(8,128)S(1)}, f32[120,384]{1,0:T(8,128)S(1)}, f32[56,384]{1,0:T(8,128)S(1)}, f32[40,384]{1,0:T(8,128)S(1)}, f32[120,128]{1,0:T(8,128)S(1)}, /*index=5*/f32[120,128]{1,0:T(8,128)S(1)}) custom-call(f32[120,128]{1,0:T(8,128)S(1)} %collective-permute-done.from_w, f32[120,128]{1,0:T(8,128)S(1)} %collective-permute-done.1.from_e, ...), custom_call_target="tpu_custom_call" | custom-call | tf_op jit(solution)/shard_map/sides/pallas_call | solution.py:384
  15.5 2.5 %collective-permute-start.2 = (f32[56,384]{1,0:T(8,128)S(1)}, f32[56,384]{1,0:T(8,128)S(1)}, u32[]{:S(2)}, u32[]{:S(2)}) collective-permute-start(f32[56,384]{1,0:T(8,128)S(1)} %get-tuple-element.46.own_n), channel_id=1, source_target_pairs={{0,1},{1,2},{2,3},{3,4},{4,5},{5,6},{6,7},{7,0},{8,9},{9,10},{10,1... | collective-permute-start | bytes 258056 | tf_op jit(solution)/shard_map/ppermute | solution.py:714
  18.0 0.0 collective-permute-start.3
  18.0 1.5 %edges.1.partial = f32[12,120,360]{2,1,0:T(8,128)} custom-call(f32[12,120,360]{2,1,0:T(8,128)S(1)} %get-tuple-element.50.partial, f32[120,128]{1,0:T(8,128)S(1)} %get-tuple-element.51.flux_e, f32[120,128]{1,0:T(8,128)S(1)} %get-tuple-element.52.flux_w), custom_call_target="tpu_custom_call" | custom-call | tf_op jit(solution)/shard_map/edges/pallas_call | solution.py:692
  19.6 2.1 %collective-permute-done.3.from_n = f32[40,384]{1,0:T(8,128)S(1)} collective-permute-done((f32[40,384]{1,0:T(8,128)S(1)}, f32[40,384]{1,0:T(8,128)S(1)}, u32[]{:S(2)}, u32[]{:S(2)}) %collective-permute-start.3) | collective-permute-done | bytes 61472 | tf_op jit(solution)/shard_map/ppermute | solution.py:715
  21.7 0.0 collective-permute-done.2.from_s
  21.7 3.0 %basis.1 = (f32[9,18,8,384]{3,2,1,0:T(8,128)S(1)}, f32[18,8,384]{2,1,0:T(8,128)S(1)}, f32[128,128]{1,0:T(8,128)S(1)}, f32[12,120,360]{2,1,0:T(8,128)}) custom-call(f32[56,384]{1,0:T(8,128)S(1)} %collective-permute-done.2.from_s, f32[40,384]{1,0:T(8,128)S(1)} %collective-permute-done.3.from_n, ...), custom_call_target="tpu_custom_call", output_to_operand_aliasing={{3}: (6, {})} | custom-call | tf_op jit(solution)/shard_map/basis/pallas_call | solution.py:549
  24.6 17.9 %all_to_all.11 = f32[128,1,128]{2,1,0:T(1,128)S(1)} all-to-all(f32[128,1,128]{2,1,0:T(1,128)S(1)} %bitcast.5), channel_id=1, replica_groups=mesh['gx'=16,'gy'=8] {'gx','gy'}, dimensions={0} | all-to-all | bytes 131072 | tf_op jit(solution)/shard_map/all_to_all | solution.py:720
  42.6 1.2 %finish.1 = (f32[120,360]{1,0:T(8,128)}, f32[120,360]{1,0:T(8,128)}) custom-call(f32[128,128]{1,0:T(8,128)S(1)} %bitcast.4, f32[9,18,8,384]{3,2,1,0:T(8,128)S(1)} %get-tuple-element.55.basis, f32[18,8,384]{2,1,0:T(8,128)S(1)} %get-tuple-element.56.diag), custom_call_target="tpu_custom_call" | custom-call | tf_op jit(solution)/shard_map/finish/pallas_call | solution.py:658
Async XLA Ops:
  6.2 8.7 %collective-permute-start = (f32[120,128]{1,0:T(8,128)S(1)}, f32[120,128]{1,0:T(8,128)S(1)}, u32[]{:S(2)}, u32[]{:S(2)}) collective-permute-start(f32[120,128]{1,0:T(8,128)S(1)} %get-tuple-element.31.own_e), channel_id=1, source_target_pairs={{0,8},{8,16},{16,24},{24,32},{32,40},{40,48},{48,56},{56,64},{64,7... | collective-permute-start | bytes 184328 | tf_op jit(solution)/shard_map/ppermute | solution.py:708
  8.3 6.6 %collective-permute-start.1 = (f32[120,128]{1,0:T(8,128)S(1)}, f32[120,128]{1,0:T(8,128)S(1)}, u32[]{:S(2)}, u32[]{:S(2)}) collective-permute-start(f32[120,128]{1,0:T(8,128)S(1)} %get-tuple-element.32.own_w), channel_id=1, source_target_pairs={{8,0},{16,8},{24,16},{32,24},{40,32},{48,40},{56,48},{64,56},{72,6... | collective-permute-start | bytes 184328 | tf_op jit(solution)/shard_map/ppermute | solution.py:709
  15.5 6.2 %collective-permute-start.2 = (f32[56,384]{1,0:T(8,128)S(1)}, f32[56,384]{1,0:T(8,128)S(1)}, u32[]{:S(2)}, u32[]{:S(2)}) collective-permute-start(f32[56,384]{1,0:T(8,128)S(1)} %get-tuple-element.46.own_n), channel_id=1, source_target_pairs={{0,1},{1,2},{2,3},{3,4},{4,5},{5,6},{6,7},{7,0},{8,9},{9,10},{10,1... | collective-permute-start | bytes 258056 | tf_op jit(solution)/shard_map/ppermute | solution.py:714
  18.0 3.6 %collective-permute-start.3 = (f32[40,384]{1,0:T(8,128)S(1)}, f32[40,384]{1,0:T(8,128)S(1)}, u32[]{:S(2)}, u32[]{:S(2)}) collective-permute-start(f32[40,384]{1,0:T(8,128)S(1)} %get-tuple-element.47.own_s), channel_id=1, source_target_pairs={{1,0},{2,1},{3,2},{4,3},{5,4},{6,5},{7,6},{0,7},{9,8},{10,9},{11,1... | collective-permute-start | bytes 184328 | tf_op jit(solution)/shard_map/ppermute | solution.py:715

commit v5 on v4

--- a/solution.py
+++ b/solution.py
@@ -35,6 +35,12 @@
 C_T0 = 48
 C_T1 = 56
 C_V1 = 64
+
+THIRD = H // 3
+WIDTH = 42
+
+CHUNKS = (0, 1, 3, 6, 9, 12)
+EARLY = 8
 
 R_LEV = 8
 R_TR = 24
@@ -132,21 +138,22 @@
 
 def outer_kernel(
     mask_hbm, kmt_hbm, forcing_hbm, t_hbm, u_hbm, v_hbm,
-    t_s, u_s, v_s, forcing, outer, rhs_ref, lev_ref, min_e, min_in, min_n, msg_e, msg_w, row_n, row_s,
+    t_s, u_s, v_s, forcing, outer, rhs_ref, lev_ref, min_e, min_in, min_n, msg_e, msg_w, out_e, out_w, row_n, row_s,
     kmt, mask, col, drop, sem_in, sem_2d,
 ):
     def load(i, k):
         src, dst = ((t_hbm, t_s), (u_hbm, u_s), (v_hbm, v_s))[i]
-        return pltpu.make_async_copy(src.at[k], dst.at[k], sem_in.at[i, k])
+        here = slice(CHUNKS[k], CHUNKS[k + 1])
+        return pltpu.make_async_copy(src.at[here], dst.at[here], sem_in.at[i, k])
 
     load_mask = pltpu.make_async_copy(mask_hbm, mask, sem_2d.at[0])
     load_kmt = pltpu.make_async_copy(kmt_hbm, kmt, sem_2d.at[1])
     load_forcing = pltpu.make_async_copy(forcing_hbm, forcing, sem_2d.at[2])
     load_mask.start()
     load_kmt.start()
-    for k in range(KL):
+    for k in range(len(CHUNKS) - 1):
         for i in range(3):
-            load(i, k).start(priority=0 if k < 4 else 1)
+            load(i, k).start(priority=0 if k == 0 else 1)
     load_forcing.start(priority=1)
 
     lane = lanes((8, LW))
@@ -176,12 +183,30 @@
     row_n[...] = jnp.zeros((32, LW), F32)
     row_s[...] = jnp.zeros((16, LW), F32)
 
+    lane128 = lanes((8, 128))
+
+    def pack(levels, r, east, west):
+        here = slice(r, r + 8)
+        for k in levels:
+            t2 = roll(tile(t_s, 2, k, here), TR0 + k - 103, 1)
+            u2 = roll(tile(u_s, 2, k, here), VE0 + k - 103, 1)
+            t0 = roll(tile(t_s, 0, k, here), TR0 + k, 1)
+            east = jnp.where(lane128 == TR0 + k, t2, east)
+            east = jnp.where(lane128 == VE0 + k, u2, east)
+            west = jnp.where(lane128 == TR0 + k, t0, west)
+        return east, west
+
     load(0, 0).wait()
     for k in range(KL):
-        if k + 1 < KL:
-            load(0, k + 1).wait()
-        load(1, k).wait()
-        load(2, k).wait()
+        if k + 1 in CHUNKS[:-1]:
+            load(0, CHUNKS.index(k + 1)).wait()
+        if k in CHUNKS:
+            load(1, CHUNKS.index(k)).wait()
+            load(2, CHUNKS.index(k)).wait()
+        if k == EARLY:
+            for r in range(0, H, 8):
+                zero = jnp.zeros((8, 128), F32)
+                msg_e[r : r + 8, :], msg_w[r : r + 8, :] = pack(range(EARLY), r, zero, zero)
         for j in (0, 2):
 
             def put(here, updated, k=k, j=j):
@@ -193,7 +218,7 @@
         row_n[16 + k : 17 + k, :] = widen(v_s[k, H - 1 : H, :], LW)
 
     load_forcing.wait()
-    lane = lanes((8, 128))
+    lane = lane128
     for r in range(0, H, 8):
         here = slice(r, r + 8)
         lev0, lev2 = tile(lev_ref, 0, here), tile(lev_ref, 2, here)
@@ -201,17 +226,11 @@
         rhs2 = jnp.where(lev2 > 0.0, ROOT * tile(col, 2, here) + tile(forcing, 2, here), 0.0)
         rhs_ref[here, :128] = rhs0
         rhs_ref[here, 128:] = rhs2
-        east = jnp.where(lane < LEV0, roll(rhs2, 32, 1), roll(lev2, LEV0 - 95, 1))
-        west = jnp.where(lane < LEV0, rhs0, roll(lev0, LEV0, 1))
-        east = jnp.where(lane < TR0, east, 0.0)
-        west = jnp.where(lane < TR0, west, 0.0)
-        for k in range(KL):
-            t2 = roll(tile(t_s, 2, k, here), TR0 + k - 103, 1)
-            u2 = roll(tile(u_s, 2, k, here), VE0 + k - 103, 1)
-            t0 = roll(tile(t_s, 0, k, here), TR0 + k, 1)
-            east = jnp.where(lane == TR0 + k, t2, east)
-            east = jnp.where(lane == VE0 + k, u2, east)
-            west = jnp.where(lane == TR0 + k, t0, west)
+        east, west = pack(range(EARLY, KL), r, msg_e[here, :], msg_w[here, :])
+        head_e = jnp.where(lane < LEV0, roll(rhs2, 32, 1), roll(lev2, LEV0 - 95, 1))
+        head_w = jnp.where(lane < LEV0, rhs0, roll(lev0, LEV0, 1))
+        east = jnp.where(lane < TR0, head_e, east)
+        west = jnp.where(lane < TR0, head_w, west)
         if r < 16:
             for at, src, base in ((C_T0, row_s, 0), (C_T1, row_n, 0), (C_V1, row_n, 16)):
                 inside = (lane >= at) & (lane < at + 8)
@@ -220,6 +239,14 @@
                 west = jnp.where(inside, roll(piece[:, :128], at, 1), west)
         msg_e[here, :] = east
         msg_w[here, :] = west
+    for dst, src in ((out_e, msg_e), (out_w, msg_w)):
+        for r in range(0, THIRD, 8):
+            value = src[r : r + 8, :]
+            for i in (1, 2):
+                part = roll(src[r + THIRD * i : r + THIRD * i + 8, :], WIDTH * i, 1)
+                value = jnp.where(lane < WIDTH * i, value, part)
+            dst[r : r + 8, :] = value
+        dst[THIRD : THIRD + 16, :] = src[0:16, :]
 
 
 def outer_part(mask, kmt, forcing, tracer, east, north):
@@ -239,14 +266,16 @@
             shape((H, LW), F32),
             shape((H, 128), F32),
             shape((H, 128), F32),
+            shape((THIRD + 16, 128), F32),
+            shape((THIRD + 16, 128), F32),
             shape((32, LW), F32),
             shape((16, LW), F32),
         ],
         in_specs=[hbm] * 6,
-        out_specs=[vmem] * 14,
+        out_specs=[vmem] * 16,
         scratch_shapes=[pltpu.VMEM((H, W), jnp.int32), pltpu.SMEM(mask.shape, jnp.int32)]
         + [pltpu.VMEM((H, LW), F32)] * 2
-        + [pltpu.SemaphoreType.DMA((3, KL)), pltpu.SemaphoreType.DMA((3,))],
+        + [pltpu.SemaphoreType.DMA((3, len(CHUNKS) - 1)), pltpu.SemaphoreType.DMA((3,))],
         compiler_params=pltpu.CompilerParams(vmem_limit_bytes=VMEM_LIMIT),
         name="outer",
     )(*(pltpu.with_memory_space_constraint(x, pltpu.HBM) for x in (mask, kmt, forcing, tracer, east, north)))
@@ -314,10 +343,13 @@
 
 
 def sides_kernel(
-    from_w, from_e, own_e, own_w, rhs_ref, lev_ref, row_n, row_s,
+    sent_w, sent_e, own_e, own_w, rhs_ref, lev_ref, row_n, row_s,
     rhs_x, lev_x, msg_n, msg_s, flux_e, flux_w,
-    sum_e, sum_w,
+    from_w, from_e, sum_e, sum_w,
 ):
+    for dst, src in ((from_w, sent_w), (from_e, sent_e)):
+        for i in range(3):
+            dst[THIRD * i : THIRD * i + THIRD, :] = roll(src[0:THIRD, :], -WIDTH * i, 1)
     from_lane = rows((128, 128))
 
     def spread(x, first, count, precision):
@@ -369,7 +401,8 @@
         (msg_s, R_TR, row_s, 0, C_T0), (msg_n, R_TR, row_n, 0, C_T1), (msg_n, R_VE, row_n, 16, C_V1),
     ):
         for r in (0, 8):
-            mw, me = from_w[r : r + 8, :], from_e[r : r + 8, :]
+            corner = slice(THIRD + r, THIRD + r + 8)
+            mw, me = sent_w[corner, :], sent_e[corner, :]
             piece = src[base + r : base + r + 8, :]
             last = piece[:, 256:]
             last = jnp.where((lane >= 104) & (lane < 112), roll(me, 104 - lane0, 1), last)
@@ -393,7 +426,7 @@
         ],
         in_specs=[vmem] * 8,
         out_specs=[vmem] * 6,
-        scratch_shapes=[pltpu.VMEM((H, 128), F32)] * 2,
+        scratch_shapes=[pltpu.VMEM((H, 128), F32)] * 4,
         compiler_params=pltpu.CompilerParams(vmem_limit_bytes=VMEM_LIMIT),
         name="sides",
     )(from_w, from_e, own_e, own_w, rhs, lev, row_n, row_s)
@@ -702,11 +735,11 @@
 
 def shards(tracer, east_velocity, north_velocity, kmt, block_mask, surface_forcing):
     nx, ny = lax.axis_size("gx"), lax.axis_size("gy")
-    *fields, lev, min_e, min_in, min_n, msg_e, msg_w, row_n, row_s = outer_part(
+    *fields, lev, min_e, min_in, min_n, msg_e, msg_w, out_e, out_w, row_n, row_s = outer_part(
         block_mask, kmt, surface_forcing, tracer, east_velocity, north_velocity
     )
-    from_w = lax.ppermute(msg_e, "gx", [(i, (i + 1) % nx) for i in range(nx)])
-    from_e = lax.ppermute(msg_w, "gx", [((i + 1) % nx, i) for i in range(nx)])
+    from_w = lax.ppermute(out_e, "gx", [(i, (i + 1) % nx) for i in range(nx)])
+    from_e = lax.ppermute(out_w, "gx", [((i + 1) % nx, i) for i in range(nx)])
     partial, rhs = middle_part(*fields, lev, min_e, min_in, min_n)
     rhs_x, lev_x, msg_n, msg_s, flux_e, flux_w = sides_part(
         from_w, from_e, msg_e, msg_w, rhs, lev, row_n, row_s

time: 43.9 us -> 42.8 us (0.975)
  Pallas kernels: 14.6 us -> 13.8 us
    pallas_call x1, Pallas kernels: 5.56 us -> 4.68 us  [outer_part(): pl.pallas_call(outer_kernel, out_shape=[shape((KL, H, W), F32)] * 3 + [sh...]
where the time goes in v5:
time: 42.8 us; the launch traced here: 42.6 us
  blocking collectives  17.6 us (41%)
  Pallas kernels  13.8 us (32%)
  starting transfers between devices  8.46 us (20%)
  waiting for transfers between devices  2.1 us (5%)
  between operations  0.69 us (2%)
    all_to_all x1, blocking collectives, shards(): gathered = lax.all_to_all(sums, ('gx', 'gy'), 0, 0, tiled=True)  17.6 us
    pallas_call x1, Pallas kernels, outer_part(): pl.pallas_call(outer_kernel, out_shape=[shape((KL, H, W), F32)] * 3 + [sh...  4.68 us
    ppermute x1, starting transfers between devices, shards(): from_e = lax.ppermute(out_w, 'gx', [((i + 1) % nx, i) for i in range(nx)])  3.8 us
    pallas_call x1, Pallas kernels, basis_part(): pl.pallas_call(basis_kernel, out_shape=[shape((ITERS + 1, EB, 8, LW), F32...  2.95 us
    pallas_call x1, Pallas kernels, middle_part(): pl.pallas_call(middle_kernel, out_shape=[shape((KL, H, W), F32), shape((H...  2.82 us
    ppermute x1, starting transfers between devices, shards(): from_s = lax.ppermute(msg_n, 'gy', [(i, (i + 1) % ny) for i in range(ny)])  2.55 us
    ppermute x1, starting transfers between devices, shards(): from_w = lax.ppermute(out_e, 'gx', [(i, (i + 1) % nx) for i in range(nx)])  2.11 us
    ppermute x1, waiting for transfers between devices, shards(): from_n = lax.ppermute(msg_s, 'gy', [((i + 1) % ny, i) for i in range(ny)])  2.09 us
  transfers between devices with their start and end apart: 4, of which 1 were waited for; matrix products, arithmetic and copies ran while one was open for 0% of the time, Pallas kernels for 10%

profile of v5, /device:TPU:1, one launch (start us, length us, event | category | flops | bytes accessed | tf_op | source)
XLA Modules:
  0.0 42.6 jit_solution(2629088266048912958)
XLA Ops:
  0.6 4.7 %outer.1 = (f32[12,120,360]{2,1,0:T(8,128)S(1)}, f32[12,120,360]{2,1,0:T(8,128)S(1)}, f32[12,120,360]{2,1,0:T(8,128)S(1)}, f32[120,360]{1,0:T(8,128)S(1)}, f32[1...) custom-call(s32[2,4]{1,0:T(2,128)} %mask_hbm.1, ...), custom_call_target="tpu_custom_call" | custom-call | tf_op jit(solution)/shard_map/outer/pallas_call | solution.py:256
  5.3 2.1 %collective-permute-start = (f32[56,128]{1,0:T(8,128)S(1)}, f32[56,128]{1,0:T(8,128)S(1)}, u32[]{:S(2)}, u32[]{:S(2)}) collective-permute-start(f32[56,128]{1,0:T(8,128)S(1)} %get-tuple-element.33), channel_id=1, source_target_pairs={{0,8},{8,16},{16,24},{24,32},{32,40},{40,48},{48,56},{56,64},{64,7... | collective-permute-start | bytes 86024 | tf_op jit(solution)/shard_map/ppermute | solution.py:741
  7.4 3.8 %collective-permute-start.1 = (f32[56,128]{1,0:T(8,128)S(1)}, f32[56,128]{1,0:T(8,128)S(1)}, u32[]{:S(2)}, u32[]{:S(2)}) collective-permute-start(f32[56,128]{1,0:T(8,128)S(1)} %get-tuple-element.34), channel_id=1, source_target_pairs={{8,0},{16,8},{24,16},{32,24},{40,32},{48,40},{56,48},{64,56},{72,6... | collective-permute-start | bytes 86024 | tf_op jit(solution)/shard_map/ppermute | solution.py:742
  11.2 2.8 %middle.1 = (f32[12,120,360]{2,1,0:T(8,128)S(1)}, f32[120,384]{1,0:T(8,128)S(1)}) custom-call(f32[12,120,360]{2,1,0:T(8,128)S(1)} %get-tuple-element.37.t_s, f32[12,120,360]{2,1,0:T(8,128)S(1)} %get-tuple-element.38.u_s, f32[12,120,360]{2,1,0:T(8,128)S(1)} %get-tuple-element.39.v_s, f32[120,360]{1,0:T(8,128)S(1)} %get-tuple-element.40.forcing, ...), custom_call_target="tpu_custom_call" | custom-call | tf_op jit(solution)/shard_map/middle/pallas_call | solution.py:331
  14.1 0.0 collective-permute-done.sent_w
  14.1 0.0 collective-permute-done.1.sent_e
  14.1 0.5 %sides.1 = (f32[120,384]{1,0:T(8,128)S(1)}, f32[120,384]{1,0:T(8,128)S(1)}, f32[56,384]{1,0:T(8,128)S(1)}, f32[40,384]{1,0:T(8,128)S(1)}, f32[120,128]{1,0:T(8,128)S(1)}, /*index=5*/f32[120,128]{1,0:T(8,128)S(1)}) custom-call(f32[56,128]{1,0:T(8,128)S(1)} %collective-permute-done.sent_w, f32[56,128]{1,0:T(8,128)S(1)} %collective-permute-done.1.sent_e, ...), custom_call_target="tpu_custom_call" | custom-call | tf_op jit(solution)/shard_map/sides/pallas_call | solution.py:417
  14.6 2.5 %collective-permute-start.2 = (f32[56,384]{1,0:T(8,128)S(1)}, f32[56,384]{1,0:T(8,128)S(1)}, u32[]{:S(2)}, u32[]{:S(2)}) collective-permute-start(f32[56,384]{1,0:T(8,128)S(1)} %get-tuple-element.50.own_n), channel_id=1, source_target_pairs={{0,1},{1,2},{2,3},{3,4},{4,5},{5,6},{6,7},{7,0},{8,9},{9,10},{10,1... | collective-permute-start | bytes 258056 | tf_op jit(solution)/shard_map/ppermute | solution.py:747
  17.2 0.0 collective-permute-start.3
  17.2 1.5 %edges.1.partial = f32[12,120,360]{2,1,0:T(8,128)} custom-call(f32[12,120,360]{2,1,0:T(8,128)S(1)} %get-tuple-element.54.partial, f32[120,128]{1,0:T(8,128)S(1)} %get-tuple-element.55.flux_e, f32[120,128]{1,0:T(8,128)S(1)} %get-tuple-element.56.flux_w), custom_call_target="tpu_custom_call" | custom-call | tf_op jit(solution)/shard_map/edges/pallas_call | solution.py:725
  18.7 2.1 %collective-permute-done.3.from_n = f32[40,384]{1,0:T(8,128)S(1)} collective-permute-done((f32[40,384]{1,0:T(8,128)S(1)}, f32[40,384]{1,0:T(8,128)S(1)}, u32[]{:S(2)}, u32[]{:S(2)}) %collective-permute-start.3) | collective-permute-done | bytes 61472 | tf_op jit(solution)/shard_map/ppermute | solution.py:748
  20.8 0.0 collective-permute-done.2.from_s
  20.8 3.0 %basis.1 = (f32[9,18,8,384]{3,2,1,0:T(8,128)S(1)}, f32[18,8,384]{2,1,0:T(8,128)S(1)}, f32[128,128]{1,0:T(8,128)S(1)}, f32[12,120,360]{2,1,0:T(8,128)}) custom-call(f32[56,384]{1,0:T(8,128)S(1)} %collective-permute-done.2.from_s, f32[40,384]{1,0:T(8,128)S(1)} %collective-permute-done.3.from_n, ...), custom_call_target="tpu_custom_call", output_to_operand_aliasing={{3}: (6, {})} | custom-call | tf_op jit(solution)/shard_map/basis/pallas_call | solution.py:582
  23.8 17.6 %all_to_all.11 = f32[128,1,128]{2,1,0:T(1,128)S(1)} all-to-all(f32[128,1,128]{2,1,0:T(1,128)S(1)} %bitcast.5), channel_id=1, replica_groups=mesh['gx'=16,'gy'=8] {'gx','gy'}, dimensions={0} | all-to-all | bytes 131072 | tf_op jit(solution)/shard_map/all_to_all | solution.py:753
  41.4 1.2 %finish.1 = (f32[120,360]{1,0:T(8,128)}, f32[120,360]{1,0:T(8,128)}) custom-call(f32[128,128]{1,0:T(8,128)S(1)} %bitcast.4, f32[9,18,8,384]{3,2,1,0:T(8,128)S(1)} %get-tuple-element.59.basis, f32[18,8,384]{2,1,0:T(8,128)S(1)} %get-tuple-element.60.diag), custom_call_target="tpu_custom_call" | custom-call | tf_op jit(solution)/shard_map/finish/pallas_call | solution.py:691
Async XLA Ops:
  5.3 8.7 %collective-permute-start = (f32[56,128]{1,0:T(8,128)S(1)}, f32[56,128]{1,0:T(8,128)S(1)}, u32[]{:S(2)}, u32[]{:S(2)}) collective-permute-start(f32[56,128]{1,0:T(8,128)S(1)} %get-tuple-element.33), channel_id=1, source_target_pairs={{0,8},{8,16},{16,24},{24,32},{32,40},{40,48},{48,56},{56,64},{64,7... | collective-permute-start | bytes 86024 | tf_op jit(solution)/shard_map/ppermute | solution.py:741
  7.4 6.6 %collective-permute-start.1 = (f32[56,128]{1,0:T(8,128)S(1)}, f32[56,128]{1,0:T(8,128)S(1)}, u32[]{:S(2)}, u32[]{:S(2)}) collective-permute-start(f32[56,128]{1,0:T(8,128)S(1)} %get-tuple-element.34), channel_id=1, source_target_pairs={{8,0},{16,8},{24,16},{32,24},{40,32},{48,40},{56,48},{64,56},{72,6... | collective-permute-start | bytes 86024 | tf_op jit(solution)/shard_map/ppermute | solution.py:742
  14.6 6.2 %collective-permute-start.2 = (f32[56,384]{1,0:T(8,128)S(1)}, f32[56,384]{1,0:T(8,128)S(1)}, u32[]{:S(2)}, u32[]{:S(2)}) collective-permute-start(f32[56,384]{1,0:T(8,128)S(1)} %get-tuple-element.50.own_n), channel_id=1, source_target_pairs={{0,1},{1,2},{2,3},{3,4},{4,5},{5,6},{6,7},{7,0},{8,9},{9,10},{10,1... | collective-permute-start | bytes 258056 | tf_op jit(solution)/shard_map/ppermute | solution.py:747
  17.2 3.6 %collective-permute-start.3 = (f32[40,384]{1,0:T(8,128)S(1)}, f32[40,384]{1,0:T(8,128)S(1)}, u32[]{:S(2)}, u32[]{:S(2)}) collective-permute-start(f32[40,384]{1,0:T(8,128)S(1)} %get-tuple-element.51.own_s), channel_id=1, source_target_pairs={{1,0},{2,1},{3,2},{4,3},{5,4},{6,5},{7,6},{0,7},{9,8},{10,9},{11,1... | collective-permute-start | bytes 184328 | tf_op jit(solution)/shard_map/ppermute | solution.py:748

commit v6 on v5

--- a/solution.py
+++ b/solution.py
@@ -85,61 +85,17 @@
     return 1.0 + (0.5 / KL) * level
 
 
-def tile(ref, j, *at):
-    if ref.shape[-1] == LW or j < 2:
-        return ref[(*at, slice(128 * j, 128 * j + 128))]
-    return widen(ref[(*at, slice(256, W))], 128)
-
-
-def sweep_level(k, j, t_s, u_s, v_s, lev_ref, min_e, min_n, drop, col, put):
-    static = isinstance(k, int)
-    kf = float(k) if static else k.astype(F32)
-    first, last = static and k == 0, static and k == KL - 1
-    above = min(k + 1, KL - 1) if static else jnp.minimum(k + 1, KL - 1)
-    lane = lanes((8, 128))
-    row = rows((8, 128))
-    f_low = jnp.zeros((8, 128), F32)
-    t = tile(t_s, j, k, slice(0, 8))
-    t_turned = roll(t, -1, 0)
-    for r in range(0, H, 8):
-        here = slice(r, r + 8)
-        if r + 8 < H:
-            ahead = tile(t_s, j, k, slice(r + 8, r + 16))
-            ahead_turned = roll(ahead, -1, 0)
-            t_n = jnp.where(row == 7, ahead_turned, t_turned)
-        else:
-            ahead = ahead_turned = None
-            t_n = t_turned
-        t_e = roll(t, -1, 1)
-        f_e = (t_e - t) - (ADV / GRAD * tile(u_s, j, k, here)) * (t + t_e)
-        f_n = (t_n - t) - (ADV / GRAD * tile(v_s, j, k, here)) * (t + t_n)
-        f_e = jnp.where(tile(min_e, j, here) > kf, f_e, 0.0)
-        f_n = jnp.where(tile(min_n, j, here) > kf, f_n, 0.0)
-        f_w = roll(f_e, 1, 1)
-        f_turned = roll(f_n, 1, 0)
-        f_s = jnp.where(row == 0, f_low, f_turned)
-        f_low = f_turned
-        lev = tile(lev_ref, j, here)
-        gain = (f_e - f_w) + (f_n - f_s)
-        if not last:
-            step = VERT / GRAD * (tile(t_s, j, above, here) - t)
-            step = jnp.where(lev > kf + 1.0, step, 0.0)
-            gain = gain + step
-        if not first:
-            gain = gain - tile(drop, j, here)
-        if not last:
-            drop[here, 128 * j : 128 * j + 128] = step
-        updated = t + GRAD * gain
-        put(here, updated)
-        share = jnp.where(lev > kf, thickness(kf) * updated, 0.0)
-        col[here, 128 * j : 128 * j + 128] = share if first else tile(col, j, here) + share
-        t, t_turned = ahead, ahead_turned
+def strip(ref, *at):
+    last = ref[(*at, slice(256, ref.shape[-1]))]
+    if ref.shape[-1] < LW:
+        last = widen(last, 128)
+    return jnp.where(lanes((8, 128)) < 64, ref[(*at, slice(0, 128))], last)
 
 
 def outer_kernel(
     mask_hbm, kmt_hbm, forcing_hbm, t_hbm, u_hbm, v_hbm,
-    t_s, u_s, v_s, forcing, outer, rhs_ref, lev_ref, min_e, min_in, min_n, msg_e, msg_w, out_e, out_w, row_n, row_s,
-    kmt, mask, col, drop, sem_in, sem_2d,
+    t_s, u_s, v_s, forcing, lev_ref, min_e, min_n, msg_e, msg_w, out_e, out_w, row_n, row_s,
+    kmt, mask, t_x, u_x, lev_x, min_ex, min_nx, col, drop, sem_in, sem_2d,
 ):
     def load(i, k):
         src, dst = ((t_hbm, t_s), (u_hbm, u_s), (v_hbm, v_s))[i]
@@ -168,7 +124,6 @@
             keep = jnp.where(inside, upper, keep)
         lev = widen(kmt[r : r + 8, :], LW) * keep
         lev_ref[r : r + 8, :] = lev.astype(F32)
-    inner = (lane != 127) & (lane != 255)
     for r in range(0, H, 8):
         here = slice(r, r + 8)
         lev = lev_ref[here, :]
@@ -176,27 +131,29 @@
             north = lev_ref[r + 1 : r + 9, :]
         else:
             north = jnp.where(row == 7, 0.0, roll(lev, -1, 0))
-        east = jnp.minimum(lev, roll(lev, -1, 1))
-        min_e[here, :] = east
-        min_in[here, :] = jnp.where(inner, east, 0.0)
+        min_e[here, :] = jnp.minimum(lev, roll(lev, -1, 1))
         min_n[here, :] = jnp.minimum(lev, north)
+        lev_x[here, :] = strip(lev_ref, here)
+        min_ex[here, :] = strip(min_e, here)
+        min_nx[here, :] = strip(min_n, here)
     row_n[...] = jnp.zeros((32, LW), F32)
     row_s[...] = jnp.zeros((16, LW), F32)
 
-    lane128 = lanes((8, 128))
+    lane = lanes((8, 128))
+    row = rows((8, 128))
 
     def pack(levels, r, east, west):
         here = slice(r, r + 8)
         for k in levels:
-            t2 = roll(tile(t_s, 2, k, here), TR0 + k - 103, 1)
-            u2 = roll(tile(u_s, 2, k, here), VE0 + k - 103, 1)
-            t0 = roll(tile(t_s, 0, k, here), TR0 + k, 1)
-            east = jnp.where(lane128 == TR0 + k, t2, east)
-            east = jnp.where(lane128 == VE0 + k, u2, east)
-            west = jnp.where(lane128 == TR0 + k, t0, west)
+            t = t_x[k, here, :]
+            east = jnp.where(lane == TR0 + k, roll(t, TR0 + k - 103, 1), east)
+            east = jnp.where(lane == VE0 + k, roll(u_x[k, here, :], VE0 + k - 103, 1), east)
+            west = jnp.where(lane == TR0 + k, roll(t, TR0 + k, 1), west)
         return east, west
 
     load(0, 0).wait()
+    for r in range(0, H, 8):
+        t_x[0, r : r + 8, :] = strip(t_s, 0, slice(r, r + 8))
     for k in range(KL):
         if k + 1 in CHUNKS[:-1]:
             load(0, CHUNKS.index(k + 1)).wait()
@@ -207,28 +164,56 @@
             for r in range(0, H, 8):
                 zero = jnp.zeros((8, 128), F32)
                 msg_e[r : r + 8, :], msg_w[r : r + 8, :] = pack(range(EARLY), r, zero, zero)
-        for j in (0, 2):
-
-            def put(here, updated, k=k, j=j):
-                outer[k, here, 64 * j : 64 * j + 128] = updated
-
-            sweep_level(k, j, t_s, u_s, v_s, lev_ref, min_in, min_n, drop, col, put)
+        kf = float(k)
+        f_low = jnp.zeros((8, 128), F32)
+        t = t_x[k, 0:8, :]
+        t_turned = roll(t, -1, 0)
+        for r in range(0, H, 8):
+            here = slice(r, r + 8)
+            if r + 8 < H:
+                ahead = t_x[k, r + 8 : r + 16, :]
+                ahead_turned = roll(ahead, -1, 0)
+                t_n = jnp.where(row == 7, ahead_turned, t_turned)
+            else:
+                ahead = ahead_turned = None
+                t_n = t_turned
+            t_e = roll(t, -1, 1)
+            u = strip(u_s, k, here)
+            u_x[k, here, :] = u
+            f_e = (t_e - t) - (ADV / GRAD * u) * (t + t_e)
+            f_n = (t_n - t) - (ADV / GRAD * strip(v_s, k, here)) * (t + t_n)
+            f_e = jnp.where(min_ex[here, :] > kf, f_e, 0.0)
+            f_n = jnp.where(min_nx[here, :] > kf, f_n, 0.0)
+            f_w = roll(f_e, 1, 1)
+            f_turned = roll(f_n, 1, 0)
+            f_s = jnp.where(row == 0, f_low, f_turned)
+            f_low = f_turned
+            lev = lev_x[here, :]
+            gain = (f_e - f_w) + (f_n - f_s)
+            if k + 1 < KL:
+                above = strip(t_s, k + 1, here)
+                t_x[k + 1, here, :] = above
+                step = jnp.where(lev > kf + 1.0, VERT / GRAD * (above - t), 0.0)
+                gain = gain + step
+            if k > 0:
+                gain = gain - drop[here, :]
+            if k + 1 < KL:
+                drop[here, :] = step
+            share = jnp.where(lev > kf, thickness(kf) * (t + GRAD * gain), 0.0)
+            col[here, :] = share if k == 0 else col[here, :] + share
+            t, t_turned = ahead, ahead_turned
         row_s[k : k + 1, :] = widen(t_s[k, 0:1, :], LW)
         row_n[k : k + 1, :] = widen(t_s[k, H - 1 : H, :], LW)
         row_n[16 + k : 17 + k, :] = widen(v_s[k, H - 1 : H, :], LW)
 
     load_forcing.wait()
-    lane = lane128
     for r in range(0, H, 8):
         here = slice(r, r + 8)
-        lev0, lev2 = tile(lev_ref, 0, here), tile(lev_ref, 2, here)
-        rhs0 = jnp.where(lev0 > 0.0, ROOT * tile(col, 0, here) + tile(forcing, 0, here), 0.0)
-        rhs2 = jnp.where(lev2 > 0.0, ROOT * tile(col, 2, here) + tile(forcing, 2, here), 0.0)
-        rhs_ref[here, :128] = rhs0
-        rhs_ref[here, 128:] = rhs2
+        lev = lev_x[here, :]
+        rhs = jnp.where(lev > 0.0, ROOT * col[here, :] + strip(forcing, here), 0.0)
         east, west = pack(range(EARLY, KL), r, msg_e[here, :], msg_w[here, :])
-        head_e = jnp.where(lane < LEV0, roll(rhs2, 32, 1), roll(lev2, LEV0 - 95, 1))
-        head_w = jnp.where(lane < LEV0, rhs0, roll(lev0, LEV0, 1))
+        head_e = jnp.where(lane < LEV0, roll(rhs, 32, 1), roll(lev, LEV0 - 95, 1))
+        head_w = jnp.where(lane < LEV0, rhs, roll(lev, LEV0, 1))
         east = jnp.where(lane < TR0, head_e, east)
         west = jnp.where(lane < TR0, head_w, west)
         if r < 16:
@@ -256,90 +241,83 @@
     return pl.pallas_call(
         outer_kernel,
         out_shape=[shape((KL, H, W), F32)] * 3
-        + [
-            shape((H, W), F32),
-            shape((KL, H, 256), F32),
-            shape((H, 256), F32),
-            shape((H, LW), F32),
-            shape((H, LW), F32),
-            shape((H, LW), F32),
-            shape((H, LW), F32),
-            shape((H, 128), F32),
-            shape((H, 128), F32),
-            shape((THIRD + 16, 128), F32),
-            shape((THIRD + 16, 128), F32),
-            shape((32, LW), F32),
-            shape((16, LW), F32),
-        ],
+        + [shape((H, W), F32)]
+        + [shape((H, LW), F32)] * 3
+        + [shape((H, 128), F32)] * 2
+        + [shape((THIRD + 16, 128), F32)] * 2
+        + [shape((32, LW), F32), shape((16, LW), F32)],
         in_specs=[hbm] * 6,
-        out_specs=[vmem] * 16,
+        out_specs=[vmem] * 13,
         scratch_shapes=[pltpu.VMEM((H, W), jnp.int32), pltpu.SMEM(mask.shape, jnp.int32)]
-        + [pltpu.VMEM((H, LW), F32)] * 2
+        + [pltpu.VMEM((KL, H, 128), F32)] * 2
+        + [pltpu.VMEM((H, 128), F32)] * 5
         + [pltpu.SemaphoreType.DMA((3, len(CHUNKS) - 1)), pltpu.SemaphoreType.DMA((3,))],
         compiler_params=pltpu.CompilerParams(vmem_limit_bytes=VMEM_LIMIT),
         name="outer",
     )(*(pltpu.with_memory_space_constraint(x, pltpu.HBM) for x in (mask, kmt, forcing, tracer, east, north)))
 
 
-def middle_kernel(
-    t_s, u_s, v_s, forcing, outer, rhs_outer, lev_ref, min_e, min_in, min_n,
-    partial, rhs_ref, min_w, col, col_w, col_e, drop,
-):
-    lane = lanes((8, 128))
+def tracer_kernel(t_s, u_s, v_s, forcing, lev_ref, min_e, min_n, partial, rhs_ref, col, drop):
+    row = rows((8, W))
     for r in range(0, H, 8):
-        here = slice(r, r + 8)
-        min_w[here, :] = roll(tile(min_e, 0, here), 1, 1)
-        for total in (col_w, col_e):
-            total[here, :] = jnp.zeros((8, 128), F32)
-        for total in (col, drop):
-            total[here, 128:256] = jnp.zeros((8, 128), F32)
+        col[r : r + 8, :] = jnp.zeros((8, W), F32)
+        drop[r : r + 8, :] = jnp.zeros((8, W), F32)
 
     def level(k, carry):
         kf = k.astype(F32)
-
-        def put(here, updated):
-            t = t_s[k, here, 128:256]
-            t_w = roll(t_s[k, here, :128], 1, 1)
-            u_w = roll(u_s[k, here, :128], 1, 1)
-            t_e = roll(tile(t_s, 2, k, here), -1, 1)
-            f_w = (t - t_w) - (ADV / GRAD * u_w) * (t_w + t)
-            f_e = (t_e - t) - (ADV / GRAD * u_s[k, here, 128:256]) * (t + t_e)
-            f_w = jnp.where((lane == 0) & (min_w[here, :] > kf), GRAD * f_w, 0.0)
-            f_e = jnp.where((lane == 127) & (tile(min_e, 1, here) > kf), GRAD * f_e, 0.0)
-            col_w[here, :] = col_w[here, :] + thickness(kf) * f_w
-            col_e[here, :] = col_e[here, :] + thickness(kf) * f_e
-            partial[k, here, :128] = outer[k, here, :128] + roll(f_w, -1, 1)
-            partial[k, here, 128:256] = updated + (f_e - f_w)
-            partial[k, here, 256:W] = (outer[k, here, 128:] - roll(f_e, 1, 1))[:, : W - 256]
-
-        sweep_level(k, 1, t_s, u_s, v_s, lev_ref, min_in, min_n, drop, col, put)
+        thick = thickness(kf)
+        above = jnp.minimum(k + 1, KL - 1)
+        f_low = jnp.zeros((8, W), F32)
+        t = t_s[k, 0:8, :]
+        t_turned = roll(t, -1, 0)
+        for r in range(0, H, 8):
+            here = slice(r, r + 8)
+            if r + 8 < H:
+                ahead = t_s[k, r + 8 : r + 16, :]
+                ahead_turned = roll(ahead, -1, 0)
+                t_n = jnp.where(row == 7, ahead_turned, t_turned)
+            else:
+                ahead = ahead_turned = None
+                t_n = t_turned
+            t_e = roll(widen(t, LW), -1, 1)[:, :W]
+            f_e = (t_e - t) - (ADV / GRAD * u_s[k, here, :]) * (t + t_e)
+            f_n = (t_n - t) - (ADV / GRAD * v_s[k, here, :]) * (t + t_n)
+            f_e = jnp.where(min_e[here, :W] > kf, f_e, 0.0)
+            f_n = jnp.where(min_n[here, :W] > kf, f_n, 0.0)
+            f_w = roll(widen(f_e, LW), 1, 1)[:, :W]
+            f_turned = roll(f_n, 1, 0)
+            f_s = jnp.where(row == 0, f_low, f_turned)
+            f_low = f_turned
+            lev = lev_ref[here, :W]
+            step = VERT / GRAD * (t_s[above, here, :] - t)
+            step = jnp.where(lev > kf + 1.0, step, 0.0)
+            gain = (f_e - f_w) + (f_n - f_s) + (step - drop[here, :])
+            drop[here, :] = step
+            updated = t + GRAD * gain
+            partial[k, here, :] = updated
+            col[here, :] += jnp.where(lev > kf, thick * updated, 0.0)
+            t, t_turned = ahead, ahead_turned
         return carry
 
     lax.fori_loop(0, KL, level, 0)
     for r in range(0, H, 8):
         here = slice(r, r + 8)
-        c_w, c_e = ROOT * col_w[here, :], ROOT * col_e[here, :]
-        rhs = ROOT * tile(col, 1, here) + tile(forcing, 1, here) + (c_e - c_w)
-        rhs_ref[here, :128] = rhs_outer[here, :128] + roll(c_w, -1, 1)
-        rhs_ref[here, 128:256] = jnp.where(tile(lev_ref, 1, here) > 0.0, rhs, 0.0)
-        rhs_ref[here, 256:] = rhs_outer[here, 128:] - roll(c_e, 1, 1)
-
-
-def middle_part(t_s, u_s, v_s, forcing, outer, rhs_outer, lev, min_e, min_in, min_n):
+        rhs = ROOT * col[here, :] + forcing[here, :]
+        rhs_ref[here, :] = widen(jnp.where(lev_ref[here, :W] > 0.0, rhs, 0.0), LW)
+
+
+def tracer_part(t_s, u_s, v_s, forcing, lev, min_e, min_n):
     vmem = pl.BlockSpec(memory_space=pltpu.VMEM)
     shape = jax.ShapeDtypeStruct
     return pl.pallas_call(
-        middle_kernel,
+        tracer_kernel,
         out_shape=[shape((KL, H, W), F32), shape((H, LW), F32)],
-        in_specs=[vmem] * 10,
+        in_specs=[vmem] * 7,
         out_specs=[vmem] * 2,
-        scratch_shapes=[pltpu.VMEM((H, 128), F32)]
-        + [pltpu.VMEM((H, LW), F32)]
-        + [pltpu.VMEM((H, 128), F32)] * 2
-        + [pltpu.VMEM((H, LW), F32)],
+        scratch_shapes=[pltpu.VMEM((H, W), F32)] * 2,
         compiler_params=pltpu.CompilerParams(vmem_limit_bytes=VMEM_LIMIT),
-        name="middle",
-    )(t_s, u_s, v_s, forcing, outer, rhs_outer, lev, min_e, min_in, min_n)
+        name="tracer",
+    )(t_s, u_s, v_s, forcing, lev, min_e, min_n)
 
 
 def sides_kernel(
@@ -735,12 +713,12 @@
 
 def shards(tracer, east_velocity, north_velocity, kmt, block_mask, surface_forcing):
     nx, ny = lax.axis_size("gx"), lax.axis_size("gy")
-    *fields, lev, min_e, min_in, min_n, msg_e, msg_w, out_e, out_w, row_n, row_s = outer_part(
+    *fields, lev, min_e, min_n, msg_e, msg_w, out_e, out_w, row_n, row_s = outer_part(
         block_mask, kmt, surface_forcing, tracer, east_velocity, north_velocity
     )
     from_w = lax.ppermute(out_e, "gx", [(i, (i + 1) % nx) for i in range(nx)])
     from_e = lax.ppermute(out_w, "gx", [((i + 1) % nx, i) for i in range(nx)])
-    partial, rhs = middle_part(*fields, lev, min_e, min_in, min_n)
+    partial, rhs = tracer_part(*fields, lev, min_e, min_n)
     rhs_x, lev_x, msg_n, msg_s, flux_e, flux_w = sides_part(
         from_w, from_e, msg_e, msg_w, rhs, lev, row_n, row_s
     )

time: 42.8 us -> 42.2 us (0.986)
  blocking collectives: 17.6 us -> 16.4 us
  Pallas kernels: 13.8 us -> 14.4 us
    pallas_call x1, Pallas kernels: 2.82 us -> 4.04 us  [tracer_part(): pl.pallas_call(tracer_kernel, out_shape=[shape((KL, H, W), F32), shape((H...]
    all_to_all x1, blocking collectives: 17.6 us -> 16.4 us  [shards(): gathered = lax.all_to_all(sums, ('gx', 'gy'), 0, 0, tiled=True)]
    pallas_call x1, Pallas kernels: 4.68 us -> 4.11 us  [outer_part(): pl.pallas_call(outer_kernel, out_shape=[shape((KL, H, W), F32)] * 3 + [sh...]
  transfers between devices with their start and end apart: 4 -> 4, of which waited for: 1 -> 1; matrix products, arithmetic and copies ran while one was open for 0% -> 0% of each run, Pallas kernels for 10% -> 13%
where the time goes in v6:
time: 42.2 us; the launch traced here: 42 us
  blocking collectives  16.4 us (39%)
  Pallas kernels  14.4 us (34%)
  starting transfers between devices  8.46 us (20%)
  waiting for transfers between devices  2.1 us (5%)
  between operations  0.69 us (2%)
    all_to_all x1, blocking collectives, shards(): gathered = lax.all_to_all(sums, ('gx', 'gy'), 0, 0, tiled=True)  16.4 us
    pallas_call x1, Pallas kernels, outer_part(): pl.pallas_call(outer_kernel, out_shape=[shape((KL, H, W), F32)] * 3 + [sh...  4.11 us
    pallas_call x1, Pallas kernels, tracer_part(): pl.pallas_call(tracer_kernel, out_shape=[shape((KL, H, W), F32), shape((H...  4.04 us
    ppermute x1, starting transfers between devices, shards(): from_e = lax.ppermute(out_w, 'gx', [((i + 1) % nx, i) for i in range(nx)])  3.8 us
    pallas_call x1, Pallas kernels, basis_part(): pl.pallas_call(basis_kernel, out_shape=[shape((ITERS + 1, EB, 8, LW), F32...  2.95 us
    ppermute x1, starting transfers between devices, shards(): from_s = lax.ppermute(msg_n, 'gy', [(i, (i + 1) % ny) for i in range(ny)])  2.55 us
    ppermute x1, starting transfers between devices, shards(): from_w = lax.ppermute(out_e, 'gx', [(i, (i + 1) % nx) for i in range(nx)])  2.11 us
    ppermute x1, waiting for transfers between devices, shards(): from_n = lax.ppermute(msg_s, 'gy', [((i + 1) % ny, i) for i in range(ny)])  2.09 us
  transfers between devices with their start and end apart: 4, of which 1 were waited for; matrix products, arithmetic and copies ran while one was open for 0% of the time, Pallas kernels for 13%

profile of v6, /device:TPU:1, one launch (start us, length us, event | category | flops | bytes accessed | tf_op | source)
XLA Modules:
  0.0 42.0 jit_solution(6625977165981289201)
XLA Ops:
  0.6 4.1 %outer.1 = (f32[12,120,360]{2,1,0:T(8,128)S(1)}, f32[12,120,360]{2,1,0:T(8,128)S(1)}, f32[12,120,360]{2,1,0:T(8,128)S(1)}, f32[120,360]{1,0:T(8,128)S(1)}, f32[1...) custom-call(s32[2,4]{1,0:T(2,128)} %mask_hbm.1, ...), custom_call_target="tpu_custom_call" | custom-call | tf_op jit(solution)/shard_map/outer/pallas_call | solution.py:241
  4.8 2.1 %collective-permute-start = (f32[56,128]{1,0:T(8,128)S(1)}, f32[56,128]{1,0:T(8,128)S(1)}, u32[]{:S(2)}, u32[]{:S(2)}) collective-permute-start(f32[56,128]{1,0:T(8,128)S(1)} %get-tuple-element.30), channel_id=1, source_target_pairs={{0,8},{8,16},{16,24},{24,32},{32,40},{40,48},{48,56},{56,64},{64,7... | collective-permute-start | bytes 86024 | tf_op jit(solution)/shard_map/ppermute | solution.py:719
  6.9 3.8 %collective-permute-start.1 = (f32[56,128]{1,0:T(8,128)S(1)}, f32[56,128]{1,0:T(8,128)S(1)}, u32[]{:S(2)}, u32[]{:S(2)}) collective-permute-start(f32[56,128]{1,0:T(8,128)S(1)} %get-tuple-element.31), channel_id=1, source_target_pairs={{8,0},{16,8},{24,16},{32,24},{40,32},{48,40},{56,48},{64,56},{72,6... | collective-permute-start | bytes 86024 | tf_op jit(solution)/shard_map/ppermute | solution.py:720
  10.7 4.0 %tracer.1 = (f32[12,120,360]{2,1,0:T(8,128)S(1)}, f32[120,384]{1,0:T(8,128)S(1)}) custom-call(f32[12,120,360]{2,1,0:T(8,128)S(1)} %get-tuple-element.34.t_s, f32[12,120,360]{2,1,0:T(8,128)S(1)} %get-tuple-element.35.u_s, f32[12,120,360]{2,1,0:T(8,128)S(1)} %get-tuple-element.36.v_s, f32[120,360]{1,0:T(8,128)S(1)} %get-tuple-element.37.forcing, ...), custom_call_target="tpu_custom_call" | custom-call | tf_op jit(solution)/shard_map/tracer/pallas_call | solution.py:312
  14.7 0.0 collective-permute-done.sent_w
  14.7 0.0 collective-permute-done.1.sent_e
  14.7 0.5 %sides.1 = (f32[120,384]{1,0:T(8,128)S(1)}, f32[120,384]{1,0:T(8,128)S(1)}, f32[56,384]{1,0:T(8,128)S(1)}, f32[40,384]{1,0:T(8,128)S(1)}, f32[120,128]{1,0:T(8,128)S(1)}, /*index=5*/f32[120,128]{1,0:T(8,128)S(1)}) custom-call(f32[56,128]{1,0:T(8,128)S(1)} %collective-permute-done.sent_w, f32[56,128]{1,0:T(8,128)S(1)} %collective-permute-done.1.sent_e, ...), custom_call_target="tpu_custom_call" | custom-call | tf_op jit(solution)/shard_map/sides/pallas_call | solution.py:395
  15.3 2.5 %collective-permute-start.2 = (f32[56,384]{1,0:T(8,128)S(1)}, f32[56,384]{1,0:T(8,128)S(1)}, u32[]{:S(2)}, u32[]{:S(2)}) collective-permute-start(f32[56,384]{1,0:T(8,128)S(1)} %get-tuple-element.44.own_n), channel_id=1, source_target_pairs={{0,1},{1,2},{2,3},{3,4},{4,5},{5,6},{6,7},{7,0},{8,9},{9,10},{10,1... | collective-permute-start | bytes 258056 | tf_op jit(solution)/shard_map/ppermute | solution.py:725
  17.8 0.0 collective-permute-start.3
  17.8 1.5 %edges.1.partial = f32[12,120,360]{2,1,0:T(8,128)} custom-call(f32[12,120,360]{2,1,0:T(8,128)S(1)} %get-tuple-element.48.partial, f32[120,128]{1,0:T(8,128)S(1)} %get-tuple-element.49.flux_e, f32[120,128]{1,0:T(8,128)S(1)} %get-tuple-element.50.flux_w), custom_call_target="tpu_custom_call" | custom-call | tf_op jit(solution)/shard_map/edges/pallas_call | solution.py:703
  19.4 2.1 %collective-permute-done.3.from_n = f32[40,384]{1,0:T(8,128)S(1)} collective-permute-done((f32[40,384]{1,0:T(8,128)S(1)}, f32[40,384]{1,0:T(8,128)S(1)}, u32[]{:S(2)}, u32[]{:S(2)}) %collective-permute-start.3) | collective-permute-done | bytes 61472 | tf_op jit(solution)/shard_map/ppermute | solution.py:726
  21.5 0.0 collective-permute-done.2.from_s
  21.5 3.0 %basis.1 = (f32[9,18,8,384]{3,2,1,0:T(8,128)S(1)}, f32[18,8,384]{2,1,0:T(8,128)S(1)}, f32[128,128]{1,0:T(8,128)S(1)}, f32[12,120,360]{2,1,0:T(8,128)}) custom-call(f32[56,384]{1,0:T(8,128)S(1)} %collective-permute-done.2.from_s, f32[40,384]{1,0:T(8,128)S(1)} %collective-permute-done.3.from_n, ...), custom_call_target="tpu_custom_call", output_to_operand_aliasing={{3}: (6, {})} | custom-call | tf_op jit(solution)/shard_map/basis/pallas_call | solution.py:560
  24.4 16.4 %all_to_all.11 = f32[128,1,128]{2,1,0:T(1,128)S(1)} all-to-all(f32[128,1,128]{2,1,0:T(1,128)S(1)} %bitcast.5), channel_id=1, replica_groups=mesh['gx'=16,'gy'=8] {'gx','gy'}, dimensions={0} | all-to-all | bytes 131072 | tf_op jit(solution)/shard_map/all_to_all | solution.py:731
  40.8 1.2 %finish.1 = (f32[120,360]{1,0:T(8,128)}, f32[120,360]{1,0:T(8,128)}) custom-call(f32[128,128]{1,0:T(8,128)S(1)} %bitcast.4, f32[9,18,8,384]{3,2,1,0:T(8,128)S(1)} %get-tuple-element.53.basis, f32[18,8,384]{2,1,0:T(8,128)S(1)} %get-tuple-element.54.diag), custom_call_target="tpu_custom_call" | custom-call | tf_op jit(solution)/shard_map/finish/pallas_call | solution.py:669
Async XLA Ops:
  4.8 10.0 %collective-permute-start = (f32[56,128]{1,0:T(8,128)S(1)}, f32[56,128]{1,0:T(8,128)S(1)}, u32[]{:S(2)}, u32[]{:S(2)}) collective-permute-start(f32[56,128]{1,0:T(8,128)S(1)} %get-tuple-element.30), channel_id=1, source_target_pairs={{0,8},{8,16},{16,24},{24,32},{32,40},{40,48},{48,56},{56,64},{64,7... | collective-permute-start | bytes 86024 | tf_op jit(solution)/shard_map/ppermute | solution.py:719
  6.9 7.9 %collective-permute-start.1 = (f32[56,128]{1,0:T(8,128)S(1)}, f32[56,128]{1,0:T(8,128)S(1)}, u32[]{:S(2)}, u32[]{:S(2)}) collective-permute-start(f32[56,128]{1,0:T(8,128)S(1)} %get-tuple-element.31), channel_id=1, source_target_pairs={{8,0},{16,8},{24,16},{32,24},{40,32},{48,40},{56,48},{64,56},{72,6... | collective-permute-start | bytes 86024 | tf_op jit(solution)/shard_map/ppermute | solution.py:720
  15.3 6.2 %collective-permute-start.2 = (f32[56,384]{1,0:T(8,128)S(1)}, f32[56,384]{1,0:T(8,128)S(1)}, u32[]{:S(2)}, u32[]{:S(2)}) collective-permute-start(f32[56,384]{1,0:T(8,128)S(1)} %get-tuple-element.44.own_n), channel_id=1, source_target_pairs={{0,1},{1,2},{2,3},{3,4},{4,5},{5,6},{6,7},{7,0},{8,9},{9,10},{10,1... | collective-permute-start | bytes 258056 | tf_op jit(solution)/shard_map/ppermute | solution.py:725
  17.8 3.6 %collective-permute-start.3 = (f32[40,384]{1,0:T(8,128)S(1)}, f32[40,384]{1,0:T(8,128)S(1)}, u32[]{:S(2)}, u32[]{:S(2)}) collective-permute-start(f32[40,384]{1,0:T(8,128)S(1)} %get-tuple-element.45.own_s), channel_id=1, source_target_pairs={{1,0},{2,1},{3,2},{4,3},{5,4},{6,5},{7,6},{0,7},{9,8},{10,9},{11,1... | collective-permute-start | bytes 184328 | tf_op jit(solution)/shard_map/ppermute | solution.py:726

commit v7 on v6

--- a/solution.py
+++ b/solution.py
@@ -43,8 +43,9 @@
 EARLY = 8
 
 R_LEV = 8
-R_TR = 24
-R_VE = 40
+R_TR = 16
+R_NINTH = 28
+R_VE = 32
 
 F32 = jnp.float32
 VMEM_LIMIT = 40 * 1024 * 1024
@@ -373,8 +374,8 @@
         lev_x[here, 256:] = last
     msg_n[0:8, :] = rhs_x[H - 8 : H, :]
     msg_s[0:8, :] = rhs_x[0:8, :]
-    msg_n[R_LEV : R_LEV + 16, :] = lev_x[H - 16 : H, :]
-    msg_s[R_LEV : R_LEV + 16, :] = lev_x[0:16, :]
+    msg_n[R_LEV : R_LEV + 8, :] = lev_x[H - 8 : H, :]
+    msg_s[R_LEV : R_LEV + 8, :] = lev_x[0:8, :]
     for dst, at, src, base, lane0 in (
         (msg_s, R_TR, row_s, 0, C_T0), (msg_n, R_TR, row_n, 0, C_T1), (msg_n, R_VE, row_n, 16, C_V1),
     ):
@@ -387,6 +388,8 @@
             last = jnp.where(lane >= 120, roll(mw, 120 - lane0, 1), last)
             dst[at + r : at + r + 8, :256] = piece[:, :256]
             dst[at + r : at + r + 8, 256:] = last
+    msg_n[R_NINTH : R_NINTH + 1, :] = lev_x[H - 9 : H - 8, :]
+    msg_s[R_NINTH : R_NINTH + 1, :] = lev_x[8:9, :]
 
 
 def sides_part(from_w, from_e, own_e, own_w, rhs, lev, row_n, row_s):
@@ -397,8 +400,8 @@
         out_shape=[
             shape((H, LW), F32),
             shape((H, LW), F32),
-            shape((56, LW), F32),
-            shape((40, LW), F32),
+            shape((48, LW), F32),
+            shape((32, LW), F32),
             shape((H, 128), F32),
             shape((H, 128), F32),
         ],
@@ -437,19 +440,19 @@
     tr = slice(R_TR, R_TR + 16)
     ve = slice(R_VE, R_VE + 16)
     lev_n = jnp.minimum(lev_ref[H - 1 : H, :], from_n[R_LEV : R_LEV + 1, :])
-    lev_s = jnp.minimum(lev_ref[0:1, :], from_s[R_LEV + 15 : R_LEV + 16, :])
+    lev_s = jnp.minimum(lev_ref[0:1, :], from_s[R_LEV + 7 : R_LEV + 8, :])
     f_n = flux(own_n[tr, :], from_n[tr, :], own_n[ve, :], lev_n)
     f_s = flux(from_s[tr, :], own_s[tr, :], from_s[ve, :], lev_s)
     c_n = jnp.sum(factor * f_n, axis=0, keepdims=True)
     c_s = jnp.sum(factor * f_s, axis=0, keepdims=True)
 
     row = rows((8, LW))
-    ninth = jnp.where(row == 7, from_s[R_LEV : R_LEV + 8, :], 0.0)
-    ninth = jnp.where(row == 0, from_n[R_LEV + 8 : R_LEV + 16, :], ninth)
+    ninth = jnp.where(row == 7, from_s[R_NINTH : R_NINTH + 1, :], 0.0)
+    ninth = jnp.where(row == 0, from_n[R_NINTH : R_NINTH + 1, :], ninth)
     tiles(lev_x, slice(0, H), lev_ref[...])
     tiles(lev_x, slice(H, H + 8), from_n[R_LEV : R_LEV + 8, :])
     tiles(lev_x, slice(H + 8, H + 16), ninth)
-    tiles(lev_x, slice(H + 16, EH), from_s[R_LEV + 8 : R_LEV + 16, :])
+    tiles(lev_x, slice(H + 16, EH), from_s[R_LEV : R_LEV + 8, :])
     tiles(rhs_x, slice(0, 8), rhs_ref[0:8, :] - jnp.where(row == 0, c_s, 0.0))
     tiles(rhs_x, slice(8, H - 8), rhs_ref[8 : H - 8, :])
     tiles(rhs_x, slice(H - 8, H), rhs_ref[H - 8 : H, :] + jnp.where(row == 7, c_n, 0.0))
@@ -624,7 +627,7 @@
     for k in range(ITERS):
         size = total([now[k], lone_part(k)])
         cross = total([now[k + 1], lone_part(k + 1)])
-        inv = 1.0 / size
+        inv = jnp.where(size == 0.0, 0.0, 1.0 / size)
         ratio = cross * inv * (1.0 if k == 0 else 0.5)
         if k == 0:
             a, b = ratio, jnp.zeros((8, 128), F32)

time: 42.2 us -> 42.1 us (level)
  no operation moved by 1% of the time
where the time goes in v7:
time: 42.1 us; the launch traced here: 41.9 us
  blocking collectives  16.4 us (39%)
  Pallas kernels  14.4 us (34%)
  starting transfers between devices  8.46 us (20%)
  waiting for transfers between devices  1.96 us (5%)
  between operations  0.69 us (2%)
    all_to_all x1, blocking collectives, shards(): gathered = lax.all_to_all(sums, ('gx', 'gy'), 0, 0, tiled=True)  16.4 us
    pallas_call x1, Pallas kernels, outer_part(): pl.pallas_call(outer_kernel, out_shape=[shape((KL, H, W), F32)] * 3 + [sh...  4.11 us
    pallas_call x1, Pallas kernels, tracer_part(): pl.pallas_call(tracer_kernel, out_shape=[shape((KL, H, W), F32), shape((H...  4.04 us
    ppermute x1, starting transfers between devices, shards(): from_e = lax.ppermute(out_w, 'gx', [((i + 1) % nx, i) for i in range(nx)])  3.8 us
    pallas_call x1, Pallas kernels, basis_part(): pl.pallas_call(basis_kernel, out_shape=[shape((ITERS + 1, EB, 8, LW), F32...  2.95 us
    ppermute x1, starting transfers between devices, shards(): from_s = lax.ppermute(msg_n, 'gy', [(i, (i + 1) % ny) for i in range(ny)])  2.55 us
    ppermute x1, starting transfers between devices, shards(): from_w = lax.ppermute(out_e, 'gx', [(i, (i + 1) % nx) for i in range(nx)])  2.11 us
    ppermute x1, waiting for transfers between devices, shards(): from_n = lax.ppermute(msg_s, 'gy', [((i + 1) % ny, i) for i in range(ny)])  1.96 us
  transfers between devices with their start and end apart: 4, of which 1 were waited for; matrix products, arithmetic and copies ran while one was open for 0% of the time, Pallas kernels for 13%

profile of v7, /device:TPU:1, one launch (start us, length us, event | category | flops | bytes accessed | tf_op | source)
XLA Modules:
  0.0 41.9 jit_solution(9063165838604809559)
XLA Ops:
  0.6 4.1 %outer.1 = (f32[12,120,360]{2,1,0:T(8,128)S(1)}, f32[12,120,360]{2,1,0:T(8,128)S(1)}, f32[12,120,360]{2,1,0:T(8,128)S(1)}, f32[120,360]{1,0:T(8,128)S(1)}, f32[1...) custom-call(s32[2,4]{1,0:T(2,128)} %mask_hbm.1, ...), custom_call_target="tpu_custom_call" | custom-call | tf_op jit(solution)/shard_map/outer/pallas_call | solution.py:242
  4.8 2.1 %collective-permute-start = (f32[56,128]{1,0:T(8,128)S(1)}, f32[56,128]{1,0:T(8,128)S(1)}, u32[]{:S(2)}, u32[]{:S(2)}) collective-permute-start(f32[56,128]{1,0:T(8,128)S(1)} %get-tuple-element.30), channel_id=1, source_target_pairs={{0,8},{8,16},{16,24},{24,32},{32,40},{40,48},{48,56},{56,64},{64,7... | collective-permute-start | bytes 86024 | tf_op jit(solution)/shard_map/ppermute | solution.py:722
  6.9 3.8 %collective-permute-start.1 = (f32[56,128]{1,0:T(8,128)S(1)}, f32[56,128]{1,0:T(8,128)S(1)}, u32[]{:S(2)}, u32[]{:S(2)}) collective-permute-start(f32[56,128]{1,0:T(8,128)S(1)} %get-tuple-element.31), channel_id=1, source_target_pairs={{8,0},{16,8},{24,16},{32,24},{40,32},{48,40},{56,48},{64,56},{72,6... | collective-permute-start | bytes 86024 | tf_op jit(solution)/shard_map/ppermute | solution.py:723
  10.7 4.0 %tracer.1 = (f32[12,120,360]{2,1,0:T(8,128)S(1)}, f32[120,384]{1,0:T(8,128)S(1)}) custom-call(f32[12,120,360]{2,1,0:T(8,128)S(1)} %get-tuple-element.34.t_s, f32[12,120,360]{2,1,0:T(8,128)S(1)} %get-tuple-element.35.u_s, f32[12,120,360]{2,1,0:T(8,128)S(1)} %get-tuple-element.36.v_s, f32[120,360]{1,0:T(8,128)S(1)} %get-tuple-element.37.forcing, ...), custom_call_target="tpu_custom_call" | custom-call | tf_op jit(solution)/shard_map/tracer/pallas_call | solution.py:313
  14.7 0.0 collective-permute-done.sent_w
  14.7 0.0 collective-permute-done.1.sent_e
  14.7 0.5 %sides.1 = (f32[120,384]{1,0:T(8,128)S(1)}, f32[120,384]{1,0:T(8,128)S(1)}, f32[48,384]{1,0:T(8,128)S(1)}, f32[32,384]{1,0:T(8,128)S(1)}, f32[120,128]{1,0:T(8,128)S(1)}, /*index=5*/f32[120,128]{1,0:T(8,128)S(1)}) custom-call(f32[56,128]{1,0:T(8,128)S(1)} %collective-permute-done.sent_w, f32[56,128]{1,0:T(8,128)S(1)} %collective-permute-done.1.sent_e, ...), custom_call_target="tpu_custom_call" | custom-call | tf_op jit(solution)/shard_map/sides/pallas_call | solution.py:398
  15.3 2.5 %collective-permute-start.2 = (f32[48,384]{1,0:T(8,128)S(1)}, f32[48,384]{1,0:T(8,128)S(1)}, u32[]{:S(2)}, u32[]{:S(2)}) collective-permute-start(f32[48,384]{1,0:T(8,128)S(1)} %get-tuple-element.44.own_n), channel_id=1, source_target_pairs={{0,1},{1,2},{2,3},{3,4},{4,5},{5,6},{6,7},{7,0},{8,9},{9,10},{10,1... | collective-permute-start | bytes 221192 | tf_op jit(solution)/shard_map/ppermute | solution.py:728
  17.8 0.0 collective-permute-start.3
  17.8 1.5 %edges.1.partial = f32[12,120,360]{2,1,0:T(8,128)} custom-call(f32[12,120,360]{2,1,0:T(8,128)S(1)} %get-tuple-element.48.partial, f32[120,128]{1,0:T(8,128)S(1)} %get-tuple-element.49.flux_e, f32[120,128]{1,0:T(8,128)S(1)} %get-tuple-element.50.flux_w), custom_call_target="tpu_custom_call" | custom-call | tf_op jit(solution)/shard_map/edges/pallas_call | solution.py:706
  19.4 2.0 %collective-permute-done.3.from_n = f32[32,384]{1,0:T(8,128)S(1)} collective-permute-done((f32[32,384]{1,0:T(8,128)S(1)}, f32[32,384]{1,0:T(8,128)S(1)}, u32[]{:S(2)}, u32[]{:S(2)}) %collective-permute-start.3) | collective-permute-done | bytes 49184 | tf_op jit(solution)/shard_map/ppermute | solution.py:729
  21.3 0.0 collective-permute-done.2.from_s
  21.3 3.0 %basis.1 = (f32[9,18,8,384]{3,2,1,0:T(8,128)S(1)}, f32[18,8,384]{2,1,0:T(8,128)S(1)}, f32[128,128]{1,0:T(8,128)S(1)}, f32[12,120,360]{2,1,0:T(8,128)}) custom-call(f32[48,384]{1,0:T(8,128)S(1)} %collective-permute-done.2.from_s, f32[32,384]{1,0:T(8,128)S(1)} %collective-permute-done.3.from_n, ...), custom_call_target="tpu_custom_call", output_to_operand_aliasing={{3}: (6, {})} | custom-call | tf_op jit(solution)/shard_map/basis/pallas_call | solution.py:563
  24.3 16.4 %all_to_all.11 = f32[128,1,128]{2,1,0:T(1,128)S(1)} all-to-all(f32[128,1,128]{2,1,0:T(1,128)S(1)} %bitcast.5), channel_id=1, replica_groups=mesh['gx'=16,'gy'=8] {'gx','gy'}, dimensions={0} | all-to-all | bytes 131072 | tf_op jit(solution)/shard_map/all_to_all | solution.py:734
  40.7 1.2 %finish.1 = (f32[120,360]{1,0:T(8,128)}, f32[120,360]{1,0:T(8,128)}) custom-call(f32[128,128]{1,0:T(8,128)S(1)} %bitcast.4, f32[9,18,8,384]{3,2,1,0:T(8,128)S(1)} %get-tuple-element.53.basis, f32[18,8,384]{2,1,0:T(8,128)S(1)} %get-tuple-element.54.diag), custom_call_target="tpu_custom_call" | custom-call | tf_op jit(solution)/shard_map/finish/pallas_call | solution.py:672
Async XLA Ops:
  4.8 10.0 %collective-permute-start = (f32[56,128]{1,0:T(8,128)S(1)}, f32[56,128]{1,0:T(8,128)S(1)}, u32[]{:S(2)}, u32[]{:S(2)}) collective-permute-start(f32[56,128]{1,0:T(8,128)S(1)} %get-tuple-element.30), channel_id=1, source_target_pairs={{0,8},{8,16},{16,24},{24,32},{32,40},{40,48},{48,56},{56,64},{64,7... | collective-permute-start | bytes 86024 | tf_op jit(solution)/shard_map/ppermute | solution.py:722
  6.9 7.9 %collective-permute-start.1 = (f32[56,128]{1,0:T(8,128)S(1)}, f32[56,128]{1,0:T(8,128)S(1)}, u32[]{:S(2)}, u32[]{:S(2)}) collective-permute-start(f32[56,128]{1,0:T(8,128)S(1)} %get-tuple-element.31), channel_id=1, source_target_pairs={{8,0},{16,8},{24,16},{32,24},{40,32},{48,40},{56,48},{64,56},{72,6... | collective-permute-start | bytes 86024 | tf_op jit(solution)/shard_map/ppermute | solution.py:723
  15.3 6.1 %collective-permute-start.2 = (f32[48,384]{1,0:T(8,128)S(1)}, f32[48,384]{1,0:T(8,128)S(1)}, u32[]{:S(2)}, u32[]{:S(2)}) collective-permute-start(f32[48,384]{1,0:T(8,128)S(1)} %get-tuple-element.44.own_n), channel_id=1, source_target_pairs={{0,1},{1,2},{2,3},{3,4},{4,5},{5,6},{6,7},{7,0},{8,9},{9,10},{10,1... | collective-permute-start | bytes 221192 | tf_op jit(solution)/shard_map/ppermute | solution.py:728
  17.8 3.5 %collective-permute-start.3 = (f32[32,384]{1,0:T(8,128)S(1)}, f32[32,384]{1,0:T(8,128)S(1)}, u32[]{:S(2)}, u32[]{:S(2)}) collective-permute-start(f32[32,384]{1,0:T(8,128)S(1)} %get-tuple-element.45.own_s), channel_id=1, source_target_pairs={{1,0},{2,1},{3,2},{4,3},{5,4},{6,5},{7,6},{0,7},{9,8},{10,9},{11,1... | collective-permute-start | bytes 147464 | tf_op jit(solution)/shard_map/ppermute | solution.py:729

commit v8 on v7

--- a/solution.py
+++ b/solution.py
@@ -533,6 +533,8 @@
         parts[2 * k - 1 : 2 * k, :] = fold(odd)
 
     step(1, None)
+    for k in range(2, 4):
+        step(k, k - 2)
     row360 = rows((8, W))
     for load in loads:
         load.wait()
@@ -543,7 +545,7 @@
         slab_s[k] = slab_s[k] - at_s
     for store in stores:
         store.start()
-    for k in range(2, ITERS + 1):
+    for k in range(4, ITERS + 1):
         step(k, k - 2)
 
     total = jnp.sum(parts[...], axis=1, keepdims=True)

time: 42.1 us -> 41.7 us (level)
  no operation moved by 1% of the time
where the time goes in v8:
time: 41.7 us; the launch traced here: 41.6 us
  blocking collectives  16.4 us (39%)
  Pallas kernels  14.1 us (34%)
  starting transfers between devices  8.46 us (20%)
  waiting for transfers between devices  1.96 us (5%)
  between operations  0.69 us (2%)
    all_to_all x1, blocking collectives, shards(): gathered = lax.all_to_all(sums, ('gx', 'gy'), 0, 0, tiled=True)  16.4 us
    pallas_call x1, Pallas kernels, outer_part(): pl.pallas_call(outer_kernel, out_shape=[shape((KL, H, W), F32)] * 3 + [sh...  4.11 us
    pallas_call x1, Pallas kernels, tracer_part(): pl.pallas_call(tracer_kernel, out_shape=[shape((KL, H, W), F32), shape((H...  4.04 us
    ppermute x1, starting transfers between devices, shards(): from_e = lax.ppermute(out_w, 'gx', [((i + 1) % nx, i) for i in range(nx)])  3.8 us
    pallas_call x1, Pallas kernels, basis_part(): pl.pallas_call(basis_kernel, out_shape=[shape((ITERS + 1, EB, 8, LW), F32...  2.63 us
    ppermute x1, starting transfers between devices, shards(): from_s = lax.ppermute(msg_n, 'gy', [(i, (i + 1) % ny) for i in range(ny)])  2.55 us
    ppermute x1, starting transfers between devices, shards(): from_w = lax.ppermute(out_e, 'gx', [(i, (i + 1) % nx) for i in range(nx)])  2.11 us
    ppermute x1, waiting for transfers between devices, shards(): from_n = lax.ppermute(msg_s, 'gy', [((i + 1) % ny, i) for i in range(ny)])  1.96 us
  transfers between devices with their start and end apart: 4, of which 1 were waited for; matrix products, arithmetic and copies ran while one was open for 0% of the time, Pallas kernels for 13%

profile of v8, /device:TPU:1, one launch (start us, length us, event | category | flops | bytes accessed | tf_op | source)
XLA Modules:
  0.0 41.6 jit_solution(12103220432980905213)
XLA Ops:
  0.6 4.1 %outer.1 = (f32[12,120,360]{2,1,0:T(8,128)S(1)}, f32[12,120,360]{2,1,0:T(8,128)S(1)}, f32[12,120,360]{2,1,0:T(8,128)S(1)}, f32[120,360]{1,0:T(8,128)S(1)}, f32[1...) custom-call(s32[2,4]{1,0:T(2,128)} %mask_hbm.1, ...), custom_call_target="tpu_custom_call" | custom-call | tf_op jit(solution)/shard_map/outer/pallas_call | solution.py:242
  4.8 2.1 %collective-permute-start = (f32[56,128]{1,0:T(8,128)S(1)}, f32[56,128]{1,0:T(8,128)S(1)}, u32[]{:S(2)}, u32[]{:S(2)}) collective-permute-start(f32[56,128]{1,0:T(8,128)S(1)} %get-tuple-element.30), channel_id=1, source_target_pairs={{0,8},{8,16},{16,24},{24,32},{32,40},{40,48},{48,56},{56,64},{64,7... | collective-permute-start | bytes 86024 | tf_op jit(solution)/shard_map/ppermute | solution.py:724
  6.9 3.8 %collective-permute-start.1 = (f32[56,128]{1,0:T(8,128)S(1)}, f32[56,128]{1,0:T(8,128)S(1)}, u32[]{:S(2)}, u32[]{:S(2)}) collective-permute-start(f32[56,128]{1,0:T(8,128)S(1)} %get-tuple-element.31), channel_id=1, source_target_pairs={{8,0},{16,8},{24,16},{32,24},{40,32},{48,40},{56,48},{64,56},{72,6... | collective-permute-start | bytes 86024 | tf_op jit(solution)/shard_map/ppermute | solution.py:725
  10.7 4.0 %tracer.1 = (f32[12,120,360]{2,1,0:T(8,128)S(1)}, f32[120,384]{1,0:T(8,128)S(1)}) custom-call(f32[12,120,360]{2,1,0:T(8,128)S(1)} %get-tuple-element.34.t_s, f32[12,120,360]{2,1,0:T(8,128)S(1)} %get-tuple-element.35.u_s, f32[12,120,360]{2,1,0:T(8,128)S(1)} %get-tuple-element.36.v_s, f32[120,360]{1,0:T(8,128)S(1)} %get-tuple-element.37.forcing, ...), custom_call_target="tpu_custom_call" | custom-call | tf_op jit(solution)/shard_map/tracer/pallas_call | solution.py:313
  14.7 0.0 collective-permute-done.sent_w
  14.7 0.0 collective-permute-done.1.sent_e
  14.7 0.5 %sides.1 = (f32[120,384]{1,0:T(8,128)S(1)}, f32[120,384]{1,0:T(8,128)S(1)}, f32[48,384]{1,0:T(8,128)S(1)}, f32[32,384]{1,0:T(8,128)S(1)}, f32[120,128]{1,0:T(8,128)S(1)}, /*index=5*/f32[120,128]{1,0:T(8,128)S(1)}) custom-call(f32[56,128]{1,0:T(8,128)S(1)} %collective-permute-done.sent_w, f32[56,128]{1,0:T(8,128)S(1)} %collective-permute-done.1.sent_e, ...), custom_call_target="tpu_custom_call" | custom-call | tf_op jit(solution)/shard_map/sides/pallas_call | solution.py:398
  15.3 2.5 %collective-permute-start.2 = (f32[48,384]{1,0:T(8,128)S(1)}, f32[48,384]{1,0:T(8,128)S(1)}, u32[]{:S(2)}, u32[]{:S(2)}) collective-permute-start(f32[48,384]{1,0:T(8,128)S(1)} %get-tuple-element.44.own_n), channel_id=1, source_target_pairs={{0,1},{1,2},{2,3},{3,4},{4,5},{5,6},{6,7},{7,0},{8,9},{9,10},{10,1... | collective-permute-start | bytes 221192 | tf_op jit(solution)/shard_map/ppermute | solution.py:730
  17.8 0.0 collective-permute-start.3
  17.8 1.5 %edges.1.partial = f32[12,120,360]{2,1,0:T(8,128)} custom-call(f32[12,120,360]{2,1,0:T(8,128)S(1)} %get-tuple-element.48.partial, f32[120,128]{1,0:T(8,128)S(1)} %get-tuple-element.49.flux_e, f32[120,128]{1,0:T(8,128)S(1)} %get-tuple-element.50.flux_w), custom_call_target="tpu_custom_call" | custom-call | tf_op jit(solution)/shard_map/edges/pallas_call | solution.py:708
  19.4 2.0 %collective-permute-done.3.from_n = f32[32,384]{1,0:T(8,128)S(1)} collective-permute-done((f32[32,384]{1,0:T(8,128)S(1)}, f32[32,384]{1,0:T(8,128)S(1)}, u32[]{:S(2)}, u32[]{:S(2)}) %collective-permute-start.3) | collective-permute-done | bytes 49184 | tf_op jit(solution)/shard_map/ppermute | solution.py:731
  21.3 0.0 collective-permute-done.2.from_s
  21.3 2.6 %basis.1 = (f32[9,18,8,384]{3,2,1,0:T(8,128)S(1)}, f32[18,8,384]{2,1,0:T(8,128)S(1)}, f32[128,128]{1,0:T(8,128)S(1)}, f32[12,120,360]{2,1,0:T(8,128)}) custom-call(f32[48,384]{1,0:T(8,128)S(1)} %collective-permute-done.2.from_s, f32[32,384]{1,0:T(8,128)S(1)} %collective-permute-done.3.from_n, ...), custom_call_target="tpu_custom_call", output_to_operand_aliasing={{3}: (6, {})} | custom-call | tf_op jit(solution)/shard_map/basis/pallas_call | solution.py:565
  24.0 16.4 %all_to_all.11 = f32[128,1,128]{2,1,0:T(1,128)S(1)} all-to-all(f32[128,1,128]{2,1,0:T(1,128)S(1)} %bitcast.5), channel_id=1, replica_groups=mesh['gx'=16,'gy'=8] {'gx','gy'}, dimensions={0} | all-to-all | bytes 131072 | tf_op jit(solution)/shard_map/all_to_all | solution.py:736
  40.3 1.2 %finish.1 = (f32[120,360]{1,0:T(8,128)}, f32[120,360]{1,0:T(8,128)}) custom-call(f32[128,128]{1,0:T(8,128)S(1)} %bitcast.4, f32[9,18,8,384]{3,2,1,0:T(8,128)S(1)} %get-tuple-element.53.basis, f32[18,8,384]{2,1,0:T(8,128)S(1)} %get-tuple-element.54.diag), custom_call_target="tpu_custom_call" | custom-call | tf_op jit(solution)/shard_map/finish/pallas_call | solution.py:674
Async XLA Ops:
  4.8 10.0 %collective-permute-start = (f32[56,128]{1,0:T(8,128)S(1)}, f32[56,128]{1,0:T(8,128)S(1)}, u32[]{:S(2)}, u32[]{:S(2)}) collective-permute-start(f32[56,128]{1,0:T(8,128)S(1)} %get-tuple-element.30), channel_id=1, source_target_pairs={{0,8},{8,16},{16,24},{24,32},{32,40},{40,48},{48,56},{56,64},{64,7... | collective-permute-start | bytes 86024 | tf_op jit(solution)/shard_map/ppermute | solution.py:724
  6.9 7.9 %collective-permute-start.1 = (f32[56,128]{1,0:T(8,128)S(1)}, f32[56,128]{1,0:T(8,128)S(1)}, u32[]{:S(2)}, u32[]{:S(2)}) collective-permute-start(f32[56,128]{1,0:T(8,128)S(1)} %get-tuple-element.31), channel_id=1, source_target_pairs={{8,0},{16,8},{24,16},{32,24},{40,32},{48,40},{56,48},{64,56},{72,6... | collective-permute-start | bytes 86024 | tf_op jit(solution)/shard_map/ppermute | solution.py:725
  15.3 6.1 %collective-permute-start.2 = (f32[48,384]{1,0:T(8,128)S(1)}, f32[48,384]{1,0:T(8,128)S(1)}, u32[]{:S(2)}, u32[]{:S(2)}) collective-permute-start(f32[48,384]{1,0:T(8,128)S(1)} %get-tuple-element.44.own_n), channel_id=1, source_target_pairs={{0,1},{1,2},{2,3},{3,4},{4,5},{5,6},{6,7},{7,0},{8,9},{9,10},{10,1... | collective-permute-start | bytes 221192 | tf_op jit(solution)/shard_map/ppermute | solution.py:730
  17.8 3.5 %collective-permute-start.3 = (f32[32,384]{1,0:T(8,128)S(1)}, f32[32,384]{1,0:T(8,128)S(1)}, u32[]{:S(2)}, u32[]{:S(2)}) collective-permute-start(f32[32,384]{1,0:T(8,128)S(1)} %get-tuple-element.45.own_s), channel_id=1, source_target_pairs={{1,0},{2,1},{3,2},{4,3},{5,4},{6,5},{7,6},{0,7},{9,8},{10,9},{11,1... | collective-permute-start | bytes 147464 | tf_op jit(solution)/shard_map/ppermute | solution.py:731
